TPU v7x, 32 devices: a whole 2x2x4 slice. The times are simulated.
32 devices in a mesh: dp: 4 (over y, core), ctx: 2 (over x), tensor: 4 (over z).
Axes of the slice: x: 2, y: 2, z: 4, core: 2. Of those that a mesh axis runs over, the one named last changes fastest.
Arguments:
- layer_input: bfloat16 [4, 1024, 2304], P('dp', 'ctx'), may hold values from -6 to 6
- query_weight: bfloat16 [2304, 2048], P(('dp', 'ctx'), 'tensor'), may hold values from -0.125 to 0.125
- key_weight: bfloat16 [2304, 1024], P(('dp', 'ctx'), 'tensor'), may hold values from -0.125 to 0.125
- value_weight: bfloat16 [2304, 1024], P(('dp', 'ctx'), 'tensor'), may hold values from -0.125 to 0.125
- output_weight: bfloat16 [2304, 2048], P(('dp', 'ctx'), 'tensor'), may hold values from -0.125 to 0.125
- gate_weight: bfloat16 [2304, 9216], P(('dp', 'ctx'), 'tensor'), may hold values from -0.125 to 0.125
- up_weight: bfloat16 [2304, 9216], P(('dp', 'ctx'), 'tensor'), may hold values from -0.125 to 0.125
- down_weight: bfloat16 [2304, 9216], P(('dp', 'ctx'), 'tensor'), may hold values from -0.0625 to 0.0625
- attn_in_gain: bfloat16 [2304], P(('dp', 'ctx')), may hold values from -0.5 to 0.5
- attn_out_gain: bfloat16 [2304], P(('dp', 'ctx')), may hold values from -0.5 to 0.5
- ffn_in_gain: bfloat16 [2304], P(('dp', 'ctx')), may hold values from -0.5 to 0.5
- ffn_out_gain: bfloat16 [2304], P(('dp', 'ctx')), may hold values from -0.5 to 0.5
- out_cotangent: bfloat16 [4, 1024, 2304], P('dp', 'ctx'), may hold values from -6 to 6
- segment_ids: int32 [4, 1024], P('dp', 'ctx'), may hold values from 0 to 3, as said below
- live_mask: int32 [4, 1024], P('dp', 'ctx'), may hold values from 0 to 1, as said below
Outputs:
- layer_output: bfloat16 [4, 1024, 2304], P('dp', 'ctx')
- input_grad: float32 [4, 1024, 2304], P('dp', 'ctx')
- query_grad: float32 [2304, 2048], P(('dp', 'ctx'), 'tensor')
- key_grad: float32 [2304, 1024], P(('dp', 'ctx'), 'tensor')
- value_grad: float32 [2304, 1024], P(('dp', 'ctx'), 'tensor')
- output_grad: float32 [2304, 2048], P(('dp', 'ctx'), 'tensor')
- gate_grad: float32 [2304, 9216], P(('dp', 'ctx'), 'tensor')
- up_grad: float32 [2304, 9216], P(('dp', 'ctx'), 'tensor')
- down_grad: float32 [2304, 9216], P(('dp', 'ctx'), 'tensor')
- attn_in_gain_grad: float32 [2304], P(('dp', 'ctx'))
- attn_out_gain_grad: float32 [2304], P(('dp', 'ctx'))
- ffn_in_gain_grad: float32 [2304], P(('dp', 'ctx'))
- ffn_out_gain_grad: float32 [2304], P(('dp', 'ctx'))
Inputs may be any that keep to these rules, and one draw needn't show every extreme that they name: `segment_ids`: each row holds four documents numbered 0 to 3 in order; document 1 starts within the first 256 positions of its row and its last position lies within the last 512 positions of its row. `live_mask`: the zeros form a nonempty run of at most 256 positions that ends each row, inside document 3, which keeps at least one real token.
All inputs are finite; a program needn't handle non-finite values.
Results may differ from a plain program's by a relative error of at most 0.017.
Values may be sent and summed in bfloat16 or wider, within the bound.
No kernel may reach another device: no remote copies, remote signals or barrier semaphores. Data moves between devices by JAX's collectives and lax.ppermute only.
A program may use at most 192 MiB of HBM per device.

v0:
```python
import math

import jax
import jax.numpy as jnp
from jax import lax
from jax.sharding import PartitionSpec as P

QH = 8
KVH = 4
HD = 256


NORM_EPSILON = 1e-06
SOFT_CAP = 50.0
MASKED_SCORE = -1e30


def rms_norm(values, gain):
    factor = lax.rsqrt(jnp.mean(values * values, axis=-1, keepdims=True) + NORM_EPSILON)
    return values * factor * (1.0 + gain)


def gelu_tanh(values):
    tanh_input = math.sqrt(2.0 / math.pi) * (values + 0.044715 * values * values * values)
    return 0.5 * values * (1.0 + jnp.tanh(tanh_input))


def geglu(gate_part, up_part):
    return gelu_tanh(gate_part) * up_part


def doc_positions(segments):
    length = segments.shape[1]
    indices = jnp.arange(length, dtype=jnp.int32)[None, :]
    boundary = jnp.concatenate(
        [jnp.ones((segments.shape[0], 1), dtype=bool), segments[:, 1:] != segments[:, :-1]], axis=1
    )
    starts = lax.cummax(jnp.where(boundary, indices, jnp.zeros_like(indices)), axis=1)
    return indices - starts


def rotary_tables(positions, head_size):
    half_size = head_size // 2
    frequency = jnp.exp(
        jnp.arange(half_size, dtype=jnp.float32) * (-2.0 * math.log(10000.0) / head_size)
    )
    angles = positions.astype(jnp.float32)[..., None] * frequency
    return (jnp.cos(angles), jnp.sin(angles))


def rotate(values, cos_table, sin_table):
    half_size = values.shape[-1] // 2
    front_half = values[..., :half_size]
    back_half = values[..., half_size:]
    return jnp.concatenate(
        [
            front_half * cos_table - back_half * sin_table,
            back_half * cos_table + front_half * sin_table,
        ],
        axis=-1,
    )


def rotate_back(grads_in, cos_table, sin_table):
    half_size = grads_in.shape[-1] // 2
    front_half = grads_in[..., :half_size]
    back_half = grads_in[..., half_size:]
    return jnp.concatenate(
        [
            front_half * cos_table + back_half * sin_table,
            back_half * cos_table - front_half * sin_table,
        ],
        axis=-1,
    )


def rows_times(left, right):
    return jnp.einsum("ti,di->td", left, right, preferred_element_type=jnp.float32)


def outer_sum(left, right):
    return jnp.einsum("td,ti->di", left, right, preferred_element_type=jnp.float32)


def local(
    layer_input,
    query_weight,
    key_weight,
    value_weight,
    output_weight,
    gate_weight,
    up_weight,
    down_weight,
    attn_in_gain,
    attn_out_gain,
    ffn_in_gain,
    ffn_out_gain,
    out_cotangent,
    segment_ids,
    live_mask,
):
    row_count, token_count, model_width = layer_input.shape
    token_total = row_count * token_count
    length = token_count * lax.axis_size("ctx")
    group_size = QH // KVH
    query_scale = 1.0 / math.sqrt(HD)
    segments_full, live_full = (
        lax.all_gather(segment_ids, "ctx", axis=1, tiled=True),
        lax.all_gather(live_mask, "ctx", axis=1, tiled=True),
    )
    offset = lax.axis_index("ctx") * token_count
    positions = lax.dynamic_slice_in_dim(doc_positions(segments_full), offset, token_count, 1)
    query_index = offset + jnp.arange(token_count, dtype=jnp.int32)
    key_index = jnp.arange(length, dtype=jnp.int32)
    allowed = (key_index[None, None, :] <= query_index[None, :, None]) & (
        segments_full[:, None, :] == segment_ids[:, :, None]
    )
    allowed = allowed & (
        (live_full[:, None, :] == 1) | (key_index[None, None, :] == query_index[None, :, None])
    )
    cos_table, sin_table = rotary_tables(positions, HD)
    cos_query, sin_query = (cos_table[:, :, None, None, :], sin_table[:, :, None, None, :])
    cos_key, sin_key = (cos_table[:, :, None, :], sin_table[:, :, None, :])
    gathered = (
        lax.all_gather(query_weight, ("dp", "ctx"), axis=0, tiled=True),
        lax.all_gather(key_weight, ("dp", "ctx"), axis=0, tiled=True),
        lax.all_gather(value_weight, ("dp", "ctx"), axis=0, tiled=True),
        lax.all_gather(output_weight, ("dp", "ctx"), axis=0, tiled=True),
        lax.all_gather(gate_weight, ("dp", "ctx"), axis=0, tiled=True),
        lax.all_gather(up_weight, ("dp", "ctx"), axis=0, tiled=True),
        lax.all_gather(down_weight, ("dp", "ctx"), axis=0, tiled=True),
        lax.all_gather(attn_in_gain, ("dp", "ctx"), axis=0, tiled=True),
        lax.all_gather(attn_out_gain, ("dp", "ctx"), axis=0, tiled=True),
        lax.all_gather(ffn_in_gain, ("dp", "ctx"), axis=0, tiled=True),
        lax.all_gather(ffn_out_gain, ("dp", "ctx"), axis=0, tiled=True),
    )
    (
        w_query,
        w_key,
        w_value,
        w_output,
        w_gate,
        w_up,
        w_down,
        gain_one,
        gain_two,
        gain_three,
        gain_four,
    ) = gathered
    gain_one = gain_one.astype(jnp.float32)
    gain_two = gain_two.astype(jnp.float32)
    gain_three = gain_three.astype(jnp.float32)
    gain_four = gain_four.astype(jnp.float32)
    kv_heads = w_key.shape[1] // HD
    flat_input = layer_input.reshape(token_total, model_width).astype(jnp.float32)
    attn_input = rms_norm(flat_input, gain_one).astype(jnp.bfloat16)
    query_raw = jnp.dot(attn_input, w_query, preferred_element_type=jnp.float32).reshape(
        row_count, token_count, kv_heads, group_size, HD
    )
    key_raw = jnp.dot(attn_input, w_key, preferred_element_type=jnp.float32).reshape(
        row_count, token_count, kv_heads, HD
    )
    queries = (rotate(query_raw, cos_query, sin_query) * query_scale).astype(jnp.bfloat16)
    keys_local = rotate(key_raw, cos_key, sin_key).astype(jnp.bfloat16)
    values_local = (
        jnp.dot(attn_input, w_value, preferred_element_type=jnp.float32)
        .astype(jnp.bfloat16)
        .reshape(row_count, token_count, kv_heads, HD)
    )
    keys_full, values_full = (
        lax.all_gather(keys_local, "ctx", axis=1, tiled=True),
        lax.all_gather(values_local, "ctx", axis=1, tiled=True),
    )

    def capped_scores():
        raw_scores = jnp.einsum(
            "rtkgd,rlkd->rkgtl", queries, keys_full, preferred_element_type=jnp.float32
        )
        bounded = jnp.tanh(raw_scores / SOFT_CAP)
        capped = jnp.where(allowed[:, None, None], SOFT_CAP * bounded, MASKED_SCORE)
        return (capped, bounded)

    capped, bounded = capped_scores()
    row_peak = jnp.max(capped, axis=-1, keepdims=True)
    exp_scores = jnp.exp(capped - row_peak)
    total_weight = jnp.sum(exp_scores, axis=-1, keepdims=True)
    log_total = row_peak + jnp.log(total_weight)
    probs_low = (exp_scores / total_weight).astype(jnp.bfloat16)
    attended = jnp.einsum(
        "rkgtl,rlkd->rtkgd", probs_low, values_full, preferred_element_type=jnp.float32
    )
    heads_out = attended.reshape(token_total, -1).astype(jnp.bfloat16)
    attn_sum = lax.psum(rows_times(heads_out, w_output), "tensor")
    mid_rows = flat_input + rms_norm(attn_sum, gain_two)
    ffn_input = rms_norm(mid_rows, gain_three).astype(jnp.bfloat16)
    gate_act = jnp.dot(ffn_input, w_gate, preferred_element_type=jnp.float32)
    up_act = jnp.dot(ffn_input, w_up, preferred_element_type=jnp.float32)
    hidden = geglu(gate_act, up_act).astype(jnp.bfloat16)
    ffn_sum = lax.psum(rows_times(hidden, w_down), "tensor")
    out_rows = mid_rows + rms_norm(ffn_sum, gain_four)
    layer_output = out_rows.astype(jnp.bfloat16).reshape(row_count, token_count, model_width)
    grad_out = out_cotangent.reshape(token_total, model_width).astype(jnp.float32)
    norm_value, pull_four = jax.vjp(rms_norm, ffn_sum, gain_four)
    grad_ffn, grad_four = pull_four(grad_out)
    grad_ffn_low = grad_ffn.astype(jnp.bfloat16)
    grad_hidden = jnp.dot(grad_ffn_low, w_down, preferred_element_type=jnp.float32)
    grad_down = outer_sum(grad_ffn_low, hidden)
    glu_value, pull_glu = jax.vjp(geglu, gate_act, up_act)
    grad_gate_act, grad_up_act = pull_glu(grad_hidden)
    grad_gate_low = grad_gate_act.astype(jnp.bfloat16)
    grad_up_low = grad_up_act.astype(jnp.bfloat16)
    grad_gate = outer_sum(ffn_input, grad_gate_low)
    grad_up = outer_sum(ffn_input, grad_up_low)
    ffn_in_part = rows_times(grad_gate_low, w_gate) + rows_times(grad_up_low, w_up)
    grad_ffn_in = lax.psum(ffn_in_part, "tensor")
    norm_value, pull_three = jax.vjp(rms_norm, mid_rows, gain_three)
    grad_mid_norm, grad_three = pull_three(grad_ffn_in)
    grad_mid = grad_out + grad_mid_norm
    norm_value, pull_two = jax.vjp(rms_norm, attn_sum, gain_two)
    grad_attn, grad_two = pull_two(grad_mid)
    grad_attn_low = grad_attn.astype(jnp.bfloat16)
    grad_output = outer_sum(grad_attn_low, heads_out)
    grad_heads = jnp.dot(grad_attn_low, w_output, preferred_element_type=jnp.float32).astype(
        jnp.bfloat16
    )
    grad_heads = grad_heads.reshape(row_count, token_count, kv_heads, group_size, HD)
    capped, bounded = capped_scores()
    attn_probs = jnp.exp(capped - log_total)
    grad_probs = jnp.einsum(
        "rtkgd,rlkd->rkgtl", grad_heads, values_full, preferred_element_type=jnp.float32
    )
    grad_capped = attn_probs * (
        grad_probs - jnp.sum(attn_probs * grad_probs, axis=-1, keepdims=True)
    )
    grad_scores = (grad_capped * (1.0 - bounded * bounded)).astype(jnp.bfloat16)
    grad_query = jnp.einsum(
        "rkgtl,rlkd->rtkgd", grad_scores, keys_full, preferred_element_type=jnp.float32
    )
    grad_keys_all = jnp.einsum(
        "rkgtl,rtkgd->rlkd", grad_scores, queries, preferred_element_type=jnp.float32
    )
    grad_values_all = jnp.einsum(
        "rkgtl,rtkgd->rlkd",
        attn_probs.astype(jnp.bfloat16),
        grad_heads,
        preferred_element_type=jnp.float32,
    )
    grad_keys, grad_values = (
        lax.psum_scatter(grad_keys_all, "ctx", scatter_dimension=1, tiled=True),
        lax.psum_scatter(grad_values_all, "ctx", scatter_dimension=1, tiled=True),
    )
    grad_query_raw = (
        (rotate_back(grad_query, cos_query, sin_query) * query_scale)
        .astype(jnp.bfloat16)
        .reshape(token_total, -1)
    )
    grad_key_raw = (
        rotate_back(grad_keys, cos_key, sin_key).astype(jnp.bfloat16).reshape(token_total, -1)
    )
    grad_value_low = grad_values.astype(jnp.bfloat16).reshape(token_total, -1)
    grad_query_weight = outer_sum(attn_input, grad_query_raw)
    grad_key_weight = outer_sum(attn_input, grad_key_raw)
    grad_value_weight = outer_sum(attn_input, grad_value_low)
    attn_in_part = (
        rows_times(grad_query_raw, w_query)
        + rows_times(grad_key_raw, w_key)
        + rows_times(grad_value_low, w_value)
    )
    grad_attn_in = lax.psum(attn_in_part, "tensor")
    norm_value, pull_one = jax.vjp(rms_norm, flat_input, gain_one)
    grad_input_norm, grad_one = pull_one(grad_attn_in)
    input_grad = (grad_mid + grad_input_norm).reshape(row_count, token_count, model_width)
    summed = (
        lax.psum_scatter(grad_query_weight, ("dp", "ctx"), scatter_dimension=0, tiled=True),
        lax.psum_scatter(grad_key_weight, ("dp", "ctx"), scatter_dimension=0, tiled=True),
        lax.psum_scatter(grad_value_weight, ("dp", "ctx"), scatter_dimension=0, tiled=True),
        lax.psum_scatter(grad_output, ("dp", "ctx"), scatter_dimension=0, tiled=True),
        lax.psum_scatter(grad_gate, ("dp", "ctx"), scatter_dimension=0, tiled=True),
        lax.psum_scatter(grad_up, ("dp", "ctx"), scatter_dimension=0, tiled=True),
        lax.psum_scatter(grad_down, ("dp", "ctx"), scatter_dimension=0, tiled=True),
        lax.psum_scatter(grad_one, ("dp", "ctx"), scatter_dimension=0, tiled=True),
        lax.psum_scatter(grad_two, ("dp", "ctx"), scatter_dimension=0, tiled=True),
        lax.psum_scatter(grad_three, ("dp", "ctx"), scatter_dimension=0, tiled=True),
        lax.psum_scatter(grad_four, ("dp", "ctx"), scatter_dimension=0, tiled=True),
    )
    (
        grad_query_weight,
        grad_key_weight,
        grad_value_weight,
        grad_output,
        grad_gate,
        grad_up,
        grad_down,
        grad_one,
        grad_two,
        grad_three,
        grad_four,
    ) = summed
    return (
        layer_output,
        input_grad,
        grad_query_weight,
        grad_key_weight,
        grad_value_weight,
        grad_output,
        grad_gate,
        grad_up,
        grad_down,
        grad_one,
        grad_two,
        grad_three,
        grad_four,
    )


def solution(mesh):
    return jax.shard_map(
        local,
        mesh=mesh,
        in_specs=(
            P("dp", "ctx", None),
            P(("dp", "ctx"), "tensor"),
            P(("dp", "ctx"), "tensor"),
            P(("dp", "ctx"), "tensor"),
            P(("dp", "ctx"), "tensor"),
            P(("dp", "ctx"), "tensor"),
            P(("dp", "ctx"), "tensor"),
            P(("dp", "ctx"), "tensor"),
            P(("dp", "ctx")),
            P(("dp", "ctx")),
            P(("dp", "ctx")),
            P(("dp", "ctx")),
            P("dp", "ctx", None),
            P("dp", "ctx"),
            P("dp", "ctx"),
        ),
        out_specs=(
            P("dp", "ctx", None),
            P("dp", "ctx", None),
            P(("dp", "ctx"), "tensor"),
            P(("dp", "ctx"), "tensor"),
            P(("dp", "ctx"), "tensor"),
            P(("dp", "ctx"), "tensor"),
            P(("dp", "ctx"), "tensor"),
            P(("dp", "ctx"), "tensor"),
            P(("dp", "ctx"), "tensor"),
            P(("dp", "ctx")),
            P(("dp", "ctx")),
            P(("dp", "ctx")),
            P(("dp", "ctx")),
        ),
        check_vma=False,
    )
```

profile of v0, /device:TPU:0, one launch (start us, length us, event | category | flops | bytes accessed | tf_op | source)
XLA Modules:
  0.0 1782.4 jit_solution(9195130574729473290)
XLA Ops:
  28.7 24.5 %all-reduce.9 = (bf16[2304]{0:T(1024)(128)(2,1)S(1)}, bf16[2304]{0:T(1024)(128)(2,1)S(1)}, bf16[2304]{0:T(1024)(128)(2,1)S(1)}, bf16[2304]{0:T(1024)(128)(2,1)S(1)}) all-reduce(bf16[2304]{0:T(1024)(128)(2,1)S(1)} %dynamic-update-slice, bf16[2304]{0:T(1024)(128)(2,1)S(1)} %dynamic-update-slice.1, ...), channel_id=1, replica_groups=mesh['dp'=4,'ctx'=2,'tensor'=4] {'dp','ctx'}, use_global_device_ids=true, to_apply=%add | all-reduce | flops 9216 | bytes 36864
  107.1 18.0 %all-gather.15.cloned.1.call-done = bf16[2304,512]{1,0:T(8,128)(2,1)} async-done(((bf16[288,512]{1,0:T(8,128)(2,1)}), bf16[2304,512]{1,0:T(8,128)(2,1)}) %all-gather.15.cloned.1.call-update) | async-done | bytes 2359312 | tf_op jit(solution)/shard_map/all_gather | solution.py:128
  132.8 169.7 %all-reduce.15.cloned.1.call-done = f32[512,2304]{1,0:T(8,128)} async-done(((f32[512,2304]{1,0:T(8,128)}), f32[512,2304]{1,0:T(8,128)}) %all-reduce.15.cloned.1.call-update) | async-done | bytes 4718608 | tf_op jit(solution)/shard_map/psum | solution.py:193
  310.0 57.1 %all-gather.17.cloned.1.call-done = bf16[2304,2304]{1,0:T(8,128)(2,1)} async-done(((bf16[288,2304]{1,0:T(8,128)(2,1)}), bf16[2304,2304]{1,0:T(8,128)(2,1)}) %all-gather.17.cloned.1.call-update) | async-done | bytes 10616848 | tf_op jit(solution)/shard_map/all_gather | solution.py:129
  378.3 54.5 %all-gather.19.cloned.1.call-done = bf16[2304,2304]{1,0:T(8,128)(2,1)} async-done(((bf16[288,2304]{1,0:T(8,128)(2,1)}), bf16[2304,2304]{1,0:T(8,128)(2,1)}) %all-gather.19.cloned.1.call-update) | async-done | bytes 10616848 | tf_op jit(solution)/shard_map/all_gather | solution.py:130
  432.8 12.5 multiply_convert_fusion.1
  445.3 53.2 %all-gather.21.cloned.1.call-done = bf16[2304,2304]{1,0:T(8,128)(2,1)} async-done(((bf16[288,2304]{1,0:T(8,128)(2,1)}), bf16[2304,2304]{1,0:T(8,128)(2,1)}) %all-gather.21.cloned.1.call-update) | async-done | bytes 10616848 | tf_op jit(solution)/shard_map/all_gather | solution.py:131
  510.8 171.6 %all-reduce.17.cloned.1.call-done = f32[512,2304]{1,0:T(8,128)} async-done(((f32[512,2304]{1,0:T(8,128)}), f32[512,2304]{1,0:T(8,128)}) %all-reduce.17.cloned.1.call-update) | async-done | bytes 4718608 | tf_op jit(solution)/shard_map/psum | solution.py:199
  693.2 15.0 multiply_convert_fusion
  715.6 12.4 convolution_add_fusion.2
  728.3 170.9 %all-reduce.19.cloned.1.call-done = f32[512,2304]{1,0:T(8,128)} async-done(((f32[512,2304]{1,0:T(8,128)}), f32[512,2304]{1,0:T(8,128)}) %all-reduce.19.cloned.1.call-update) | async-done | bytes 4718608 | tf_op jit(solution)/shard_map/psum | solution.py:215
  929.7 12.9 reduce-scatter.10.cloned.1.call-done
  950.6 14.5 reduce-scatter.12.cloned.1.call-done
  988.3 12.1 fusion.134
  1000.5 12.1 fusion.133
  1012.7 12.3 fusion.135
  1025.7 117.5 %all-reduce.21.cloned.1.call-done = f32[512,2304]{1,0:T(8,128)} async-done(((f32[512,2304]{1,0:T(8,128)}), f32[512,2304]{1,0:T(8,128)}) %all-reduce.21.cloned.1.call-update) | async-done | bytes 4718608 | tf_op jit(solution)/shard_map/psum | solution.py:269
  1147.1 25.0 %all-reduce.8 = (f32[2304]{0:T(1024)S(1)}, f32[2304]{0:T(1024)S(1)}, f32[2304]{0:T(1024)S(1)}, f32[2304]{0:T(1024)S(1)}) all-reduce(f32[2304]{0:T(1024)S(1)} %get-tuple-element.19, f32[2304]{0:T(1024)S(1)} %copy-done.35, f32[2304]{0:T(1024)S(1)} %copy-done.34, ...), channel_id=12, replica_groups=mesh['dp'=4,'ctx'=2,'tensor'=4] {'dp','ctx'}, use_global_device_ids=true, to_apply=%region_27.28.clone | all-reduce | flops 9216 | bytes 73728
  1188.6 46.7 %reduce-scatter.16.cloned.1.call-done = f32[288,256]{1,0:T(8,128)} async-done(((f32[2304,256]{1,0:T(8,128)}), f32[288,256]{1,0:T(8,128)}) %reduce-scatter.16.cloned.1.call-update) | async-done | bytes 294928 | tf_op jit(solution)/shard_map/reduce_scatter | solution.py:275
  1235.3 57.8 %reduce-scatter.20.cloned.1.call-done = f32[288,512]{1,0:T(8,128)} async-done(((f32[2304,512]{1,0:T(8,128)}), f32[288,512]{1,0:T(8,128)}) %reduce-scatter.20.cloned.1.call-update) | async-done | bytes 589840 | tf_op jit(solution)/shard_map/reduce_scatter | solution.py:277
  1293.1 58.2 %reduce-scatter.14.cloned.1.call-done = f32[288,512]{1,0:T(8,128)} async-done(((f32[2304,512]{1,0:T(8,128)}), f32[288,512]{1,0:T(8,128)}) %reduce-scatter.14.cloned.1.call-update) | async-done | bytes 589840 | tf_op jit(solution)/shard_map/reduce_scatter | solution.py:274
  1351.2 141.2 %reduce-scatter.24.cloned.1.call-done = f32[288,2304]{1,0:T(8,128)} async-done(((f32[2304,2304]{1,0:T(8,128)}), f32[288,2304]{1,0:T(8,128)}) %reduce-scatter.24.cloned.1.call-update) | async-done | bytes 2654224 | tf_op jit(solution)/shard_map/reduce_scatter | solution.py:279
  1492.5 141.4 %reduce-scatter.22.cloned.1.call-done = f32[288,2304]{1,0:T(8,128)} async-done(((f32[2304,2304]{1,0:T(8,128)}), f32[288,2304]{1,0:T(8,128)}) %reduce-scatter.22.cloned.1.call-update) | async-done | bytes 2654224 | tf_op jit(solution)/shard_map/reduce_scatter | solution.py:278
  1633.9 141.2 %reduce-scatter.26.cloned.1.call-done = f32[288,2304]{1,0:T(8,128)} async-done(((f32[2304,2304]{1,0:T(8,128)}), f32[288,2304]{1,0:T(8,128)}) %reduce-scatter.26.cloned.1.call-update) | async-done | bytes 2654224 | tf_op jit(solution)/shard_map/reduce_scatter | solution.py:280
  (241 shorter events, 213.2 us)
Async XLA Ops:
  7.2 49.0 %all-gather.11.cloned.1.call-start = ((), (), s32[]{:S(2)}) async-start(), calls=%async_computation.10 | async-start | bytes 1327104 | tf_op jit(solution)/shard_map/all_gather | solution.py:126
  7.9 55.0 %all-gather.9.cloned.1.call-start = ((), (), s32[]{:S(2)}) async-start(), calls=%async_computation.9 | async-start | bytes 1327104 | tf_op jit(solution)/shard_map/all_gather | solution.py:127
  8.7 85.6 %all-gather.13.cloned.1.call-start = ((), (), s32[]{:S(2)}) async-start(), calls=%async_computation.11 | async-start | bytes 2654208 | tf_op jit(solution)/shard_map/all_gather | solution.py:125
  9.4 115.7 %all-gather.15.cloned.1.call-start = ((), (), s32[]{:S(2)}) async-start(), calls=%async_computation.12 | async-start | bytes 2654208 | tf_op jit(solution)/shard_map/all_gather | solution.py:128
  10.0 292.5 %all-reduce.15.cloned.1.call-start = ((), (), s32[]{:S(2)}) async-start(), calls=%async_computation.13 | async-start | bytes 9437184 | tf_op jit(solution)/shard_map/psum | solution.py:193
  130.4 236.7 %all-gather.17.cloned.1.call-start = ((), (), s32[]{:S(2)}) async-start(), calls=%async_computation.14 | async-start | bytes 11943936 | tf_op jit(solution)/shard_map/all_gather | solution.py:129
  131.0 301.8 %all-gather.19.cloned.1.call-start = ((), (), s32[]{:S(2)}) async-start(), calls=%async_computation.15 | async-start | bytes 11943936 | tf_op jit(solution)/shard_map/all_gather | solution.py:130
  131.7 366.8 %all-gather.21.cloned.1.call-start = ((), (), s32[]{:S(2)}) async-start(), calls=%async_computation.16 | async-start | bytes 11943936 | tf_op jit(solution)/shard_map/all_gather | solution.py:131
  132.5 549.9 %all-reduce.17.cloned.1.call-start = ((), (), s32[]{:S(2)}) async-start(), calls=%async_computation.17 | async-start | bytes 9437184 | tf_op jit(solution)/shard_map/psum | solution.py:199
  310.0 122.8 %copy-start.18 = (bf16[512,2304]{1,0:T(8,128)(2,1)}, bf16[512,2304]{1,0:T(8,128)(2,1)S(1)}, u32[]{:S(2)}) copy-start(bf16[512,2304]{1,0:T(8,128)(2,1)S(1)} %multiply_convert_fusion.2) | copy-start | bytes 7077892
  510.2 175.0 %copy-start.6 = (bf16[1,512,2304]{2,1,0:T(8,128)(2,1)S(1)}, bf16[1,512,2304]{2,1,0:T(8,128)(2,1)}, u32[]{:S(2)}) copy-start(bf16[1,512,2304]{2,1,0:T(8,128)(2,1)} %param.27) | copy-start | bytes 7077892
  510.2 388.9 %all-reduce.19.cloned.1.call-start = ((), (), s32[]{:S(2)}) async-start(), calls=%async_computation.18 | async-start | bytes 9437184 | tf_op jit(solution)/shard_map/psum | solution.py:215
  728.0 214.5 %reduce-scatter.10.cloned.1.call-start = ((), (), s32[]{:S(2)}) async-start(), calls=%async_computation.19 | async-start | bytes 1572864 | tf_op jit(solution)/shard_map/reduce_scatter | solution.py:249
  923.1 42.0 %reduce-scatter.12.cloned.1.call-start = ((), (), s32[]{:S(2)}) async-start(), calls=%async_computation.20 | async-start | bytes 1572864 | tf_op jit(solution)/shard_map/reduce_scatter | solution.py:250
  928.3 214.9 %all-reduce.21.cloned.1.call-start = ((), (), s32[]{:S(2)}) async-start(), calls=%async_computation.21 | async-start | bytes 9437184 | tf_op jit(solution)/shard_map/psum | solution.py:269
  971.1 217.5 %reduce-scatter.18.cloned.1.call-start = ((), (), s32[]{:S(2)}) async-start(), calls=%async_computation.24 | async-start | bytes 2654208 | tf_op jit(solution)/shard_map/reduce_scatter | solution.py:276
  975.3 259.9 %reduce-scatter.16.cloned.1.call-start = ((), (), s32[]{:S(2)}) async-start(), calls=%async_computation.23 | async-start | bytes 2654208 | tf_op jit(solution)/shard_map/reduce_scatter | solution.py:275
  978.7 314.3 %reduce-scatter.20.cloned.1.call-start = ((), (), s32[]{:S(2)}) async-start(), calls=%async_computation.25 | async-start | bytes 5308416 | tf_op jit(solution)/shard_map/reduce_scatter | solution.py:277
  984.1 367.2 %reduce-scatter.14.cloned.1.call-start = ((), (), s32[]{:S(2)}) async-start(), calls=%async_computation.22 | async-start | bytes 5308416 | tf_op jit(solution)/shard_map/reduce_scatter | solution.py:274
  988.0 504.5 %reduce-scatter.24.cloned.1.call-start = ((), (), s32[]{:S(2)}) async-start(), calls=%async_computation.27 | async-start | bytes 23887872 | tf_op jit(solution)/shard_map/reduce_scatter | solution.py:279
  1000.5 633.4 %reduce-scatter.22.cloned.1.call-start = ((), (), s32[]{:S(2)}) async-start(), calls=%async_computation.26 | async-start | bytes 23887872 | tf_op jit(solution)/shard_map/reduce_scatter | solution.py:278
  1012.7 762.4 %reduce-scatter.26.cloned.1.call-start = ((), (), s32[]{:S(2)}) async-start(), calls=%async_computation.28 | async-start | bytes 23887872 | tf_op jit(solution)/shard_map/reduce_scatter | solution.py:280
  1025.0 122.0 %copy-start.34 = (f32[2304]{0:T(1024)S(1)}, f32[2304]{0:T(1024)}, u32[]{:S(2)}) copy-start(f32[2304]{0:T(1024)} %get-tuple-element.13) | copy-start | bytes 27652
  1025.1 149.7 %copy-start.40 = (f32[512]{0:T(512)S(1)}, f32[512]{0:T(512)}, u32[]{:S(2)}) copy-start(f32[512]{0:T(512)} %copy-done.39) | copy-start | bytes 6148
  (50 other events, 841.2 us)
Sparse Core Ops, SparseCore 0:
  9.9 26.9 all-gather.10
  38.8 24.0 all-gather.8
  64.8 29.4 all-gather.12
  96.0 28.9 all-gather.14
  130.5 171.9 all-reduce.14
  304.2 62.7 all-gather.16
  368.9 63.7 all-gather.18
  434.7 63.7 all-gather.20
  510.4 171.9 all-reduce.16
  728.2 170.9 all-reduce.18
  923.2 19.3 reduce-scatter.9
  944.8 20.3 reduce-scatter.11
  971.2 171.9 all-reduce.20
  1147.0 41.5 reduce-scatter.17
  1192.7 42.4 reduce-scatter.15
  1239.1 53.8 reduce-scatter.19
  1297.3 53.8 reduce-scatter.13
  1355.3 137.1 reduce-scatter.23
  1496.7 137.1 reduce-scatter.21
  1637.9 137.1 reduce-scatter.25
where the time goes:
time: 1790 us; the launch traced here: 1780 us
  waiting for transfers between devices  1450 us (81%)
  matrix products  161 us (9%)
  blocking collectives  78.3 us (4%)
  other arithmetic  51.5 us (3%)
  local copies, waits for them, and re-layouts  22.6 us (1%)
    psum x1, waiting for transfers between devices, local(): ffn_sum = lax.psum(rows_times(hidden, w_down), 'tensor')  172 us
    psum x1, waiting for transfers between devices, local(): grad_ffn_in = lax.psum(ffn_in_part, 'tensor')  171 us
    psum x1, waiting for transfers between devices, local(): attn_sum = lax.psum(rows_times(heads_out, w_output), 'tensor')  170 us
    reduce_scatter x1, waiting for transfers between devices, local(): lax.psum_scatter(grad_gate, ('dp', 'ctx'), scatter_dimension=0, tiled=True)  141 us
    reduce_scatter x1, waiting for transfers between devices, local(): lax.psum_scatter(grad_up, ('dp', 'ctx'), scatter_dimension=0, tiled=True)  141 us
    reduce_scatter x1, waiting for transfers between devices, local(): lax.psum_scatter(grad_down, ('dp', 'ctx'), scatter_dimension=0, tiled=True)  141 us
    psum x1, waiting for transfers between devices, local(): grad_attn_in = lax.psum(attn_in_part, 'tensor')  118 us
    reduce_scatter x1, waiting for transfers between devices, local(): lax.psum_scatter(grad_query_weight, ('dp', 'ctx'), scatter_dimension=0, t...  58.2 us
  transfers between devices with their start and end apart: 20, of which 19 were waited for; matrix products, arithmetic and copies ran while one was open for 8% of the time, Pallas kernels for 0%

commit v1 on v0

v1 whole, which is shorter than its diff:
```python
import math

import jax
import jax.numpy as jnp
from jax import lax
from jax.sharding import Mesh
from jax.sharding import PartitionSpec as P

QH = 8
KVH = 4
HD = 256

NORM_EPSILON = 1e-06
SOFT_CAP = 50.0
MASKED_SCORE = -1e30
SWAP = [(0, 1), (1, 0)]
LOW = jnp.bfloat16
F32 = jnp.float32


def wide(a):
    return a.astype(F32)


def norm_factor(v):
    return lax.rsqrt(jnp.mean(v * v, axis=-1, keepdims=True) + NORM_EPSILON)


def norm_back(v, gain, grad):
    r = norm_factor(v)
    w = (1.0 + gain) * grad
    dv = r * w - v * (r * r * r) * jnp.mean(v * w, axis=-1, keepdims=True)
    dg = jnp.sum(grad * v * r, axis=0, keepdims=True)
    return dv, dg


def gelu_parts(u):
    k = math.sqrt(2.0 / math.pi)
    th = jnp.tanh(k * (u + 0.044715 * u * u * u))
    g = 0.5 * u * (1.0 + th)
    dg = 0.5 * (1.0 + th) + 0.5 * u * (1.0 - th * th) * k * (1.0 + 3 * 0.044715 * u * u)
    return g, dg


def dot(a, b):
    return jnp.dot(a, b, preferred_element_type=F32)


def dot_t(a, b):
    return jnp.einsum("ti,di->td", a, b, preferred_element_type=F32)


def outer(a, b):
    return jnp.einsum("td,ti->di", a, b, preferred_element_type=F32)


def to_ctx(a):
    return lax.ppermute(a, "ctx", SWAP)


def to_y(a):
    return lax.ppermute(a, "y", SWAP)


def to_core(a):
    return lax.ppermute(a, "core", SWAP)


def rotate(v, c, s):
    h = HD // 2
    a, b = v[..., :h], v[..., h:]
    return jnp.concatenate([a * c - b * s, b * c + a * s], axis=-1)


def rotate_back(v, c, s):
    h = HD // 2
    a, b = v[..., :h], v[..., h:]
    return jnp.concatenate([a * c + b * s, b * c - a * s], axis=-1)


def make_local(ny, nx):
    square = ny == 2 and nx == 2

    def order(v, back=False):
        blk = v.shape[1] // (2 * ny * nx)
        me_c = lax.axis_index("core")
        cut = lambda j: lax.slice_in_dim(v, j * blk, (j + 1) * blk, axis=1)
        if back:
            parts = {
                (c, y, x): cut((c * ny + y) * nx + x)
                for c in range(2)
                for y in range(ny)
                for x in range(nx)
            }
        else:
            parts = {
                (c, y, x): cut((y * 2 + c) * nx + x)
                for c in range(2)
                for y in range(ny)
                for x in range(nx)
            }
        bits = [(0, me_c)]
        if square:
            bits += [(1, lax.axis_index("y")), (2, lax.axis_index("ctx"))]
        for pos, bit in bits:
            flip = lambda k: tuple(1 - e if i == pos else e for i, e in enumerate(k))
            parts = {k: jnp.where(bit == 0, parts[k], parts[flip(k)]) for k in parts}
        if back:
            out = [
                parts[(c, y, x)]
                for y in range(ny)
                for c in range(2)
                for x in range(nx)
            ]
        else:
            out = [
                parts[(c, y, x)]
                for c in range(2)
                for y in range(ny)
                for x in range(nx)
            ]
        return jnp.concatenate(out, axis=1)

    def gather(w):
        if square:
            h = w.shape[0] // 2
            wx, wy = to_ctx(w), to_y(w)
            d1, d2 = to_y(wx[:h]), to_ctx(wy[h:])
            mine = jnp.concatenate([w, wx, wy, d1, d2], axis=0)
        else:
            mine = lax.all_gather(w, ("y", "ctx"), axis=0, tiled=True)
        return mine, to_core(mine)

    def scatter(mine, other):
        s = wide(mine) + wide(to_core(other))
        if not square:
            return lax.psum_scatter(
                s.astype(LOW), ("y", "ctx"), scatter_dimension=0, tiled=True
            ).astype(F32)
        b = s.shape[0] // 4
        h = b // 2
        s0, s1, s2, s3 = [s[i * b : (i + 1) * b] for i in range(4)]
        s3 = s3.astype(LOW)
        gx, gy = to_ctx(s3[:h]), to_y(s3[h:])
        t1 = jnp.concatenate([s1[:h], s1[h:] + wide(gy)], axis=0).astype(LOW)
        t2 = jnp.concatenate([s2[:h] + wide(gx), s2[h:]], axis=0).astype(LOW)
        return s0 + wide(to_ctx(t1)) + wide(to_y(t2))

    def local(
        layer_input,
        query_weight,
        key_weight,
        value_weight,
        output_weight,
        gate_weight,
        up_weight,
        down_weight,
        attn_in_gain,
        attn_out_gain,
        ffn_in_gain,
        ffn_out_gain,
        out_cotangent,
        segment_ids,
        live_mask,
    ):
        rows, toks, width = layer_input.shape
        blk = query_weight.shape[0]
        qw, kw = query_weight.shape[1], key_weight.shape[1]
        qkv_w = qw + 2 * kw
        half = toks // 2
        halves = [slice(0, half), slice(half, toks)]
        scale = 1.0 / math.sqrt(HD)

        gains = jnp.stack([attn_in_gain, attn_out_gain, ffn_in_gain, ffn_out_gain])
        gains = jnp.pad(gains, ((0, 12), (0, qkv_w - blk)))
        qkv_own = jnp.concatenate([query_weight, key_weight, value_weight], axis=1)
        packet = jnp.concatenate([qkv_own, gains], axis=0)

        def gather_packet():
            if square:
                px, py = to_ctx(packet), to_y(packet)
                h = packet.shape[0] // 2
                d1, d2 = to_y(px[:h]), to_ctx(py[h:])
                four = [packet, px, py, jnp.concatenate([d1, d2], axis=0)]
            else:
                full = lax.all_gather(packet, ("y", "ctx"), axis=0, tiled=True)
                four = [
                    full[i * packet.shape[0] : (i + 1) * packet.shape[0]]
                    for i in range(ny * nx)
                ]
            both = jnp.concatenate(four, axis=0)
            sib = to_core(both)
            n = packet.shape[0]
            pick = lambda a: (
                jnp.concatenate([a[i * n : i * n + blk] for i in range(ny * nx)], 0),
                jnp.concatenate(
                    [a[i * n + blk : i * n + blk + 4, :blk] for i in range(ny * nx)], 1
                ),
            )
            (m, gm), (s, gs) = pick(both), pick(sib)
            return m, s, wide(jnp.concatenate([gm, gs], axis=1))

        qkv_m, qkv_s, gain = gather_packet()
        g1, g2, g3, g4 = [gain[i : i + 1] for i in range(4)]
        out_m, out_s = gather(output_weight)
        gate_m, gate_s = gather(gate_weight)
        up_m, up_s = gather(up_weight)
        down_m, down_s = gather(down_weight)
        mid = width // 2

        def times(h, wm, ws):
            return dot(h[:, :mid], wm) + dot(h[:, mid:], ws)

        def times_t(u, wm, ws):
            return jnp.concatenate([dot_t(u, wm), dot_t(u, ws)], axis=1)

        index = lax.axis_index("ctx") * toks + jnp.arange(toks, dtype=jnp.int32)
        own_info = jnp.concatenate([segment_ids, live_mask, index[None]], axis=0)
        if square:
            info = jnp.concatenate([own_info, to_ctx(own_info)], axis=1)
        else:
            info = lax.all_gather(own_info, "ctx", axis=1, tiled=True)
        seg_all, live_all, index_all = info[0:1], info[1:2], info[2:3]
        seg_col, index_col = segment_ids.reshape(toks, 1), index.reshape(toks, 1)
        start = jnp.sum((seg_all < seg_col).astype(jnp.int32), axis=1)
        pos = index - start
        allowed = (
            (index_all <= index_col)
            & (seg_all == seg_col)
            & ((live_all == 1) | (index_all == index_col))
        )
        freq = jnp.exp(
            jnp.arange(HD // 2, dtype=F32) * (-2.0 * math.log(10000.0) / HD)
        )
        angle = wide(pos)[:, None] * freq
        cos, sin = jnp.cos(angle), jnp.sin(angle)
        cos, sin = cos[:, None, :], sin[:, None, :]

        x = wide(order(layer_input.reshape(toks, width)))
        dy = wide(order(out_cotangent.reshape(toks, width)))
        h1 = (x * norm_factor(x) * (1.0 + g1)).astype(LOW)

        qkv = times(h1, qkv_m, qkv_s)
        heads, groups = qw // HD, kw // HD
        per = heads // groups
        q = (rotate(qkv[:, :qw].reshape(toks, heads, HD), cos, sin) * scale).astype(LOW)
        k = rotate(qkv[:, qw : qw + kw].reshape(toks, groups, HD), cos, sin).astype(LOW)
        kv = jnp.concatenate([k.reshape(toks, kw), qkv[:, qw + kw :].astype(LOW)], 1)
        if square:
            kv_all = jnp.concatenate([kv, to_ctx(kv)], axis=0)
        else:
            kv_all = lax.all_gather(kv, "ctx", axis=0, tiled=True)
        length = kv_all.shape[0]
        k_all = kv_all[:, :kw].reshape(length, groups, HD)
        v_all = kv_all[:, kw:].reshape(length, groups, HD)
        q = q.reshape(toks, groups, per, HD)

        def scores(sl):
            raw = jnp.einsum(
                "tkgd,lkd->kgtl", q[sl], k_all, preferred_element_type=F32
            )
            bounded = jnp.tanh(raw / SOFT_CAP)
            return jnp.where(allowed[sl], SOFT_CAP * bounded, MASKED_SCORE), bounded

        xs = [x[sl] for sl in halves]
        dys = [dy[sl] for sl in halves]
        outs_low, logs, attn = [], [], []
        for sl in halves:
            capped, _ = scores(sl)
            peak = jnp.max(capped, axis=-1, keepdims=True)
            e = jnp.exp(capped - peak)
            total = jnp.sum(e, axis=-1, keepdims=True)
            logs.append(peak + jnp.log(total))
            p = (e / total).astype(LOW)
            o = jnp.einsum("kgtl,lkd->tkgd", p, v_all, preferred_element_type=F32)
            o = o.reshape(half, qw).astype(LOW)
            outs_low.append(o)
            attn.append(lax.psum(times_t(o, out_m, out_s).astype(LOW), "tensor"))
        mids, h3s, gates, ups, hids, fs = [], [], [], [], [], []
        for i, sl in enumerate(halves):
            a = wide(attn[i])
            x2 = xs[i] + a * norm_factor(a) * (1.0 + g2)
            h3 = (x2 * norm_factor(x2) * (1.0 + g3)).astype(LOW)
            mids.append(x2)
            h3s.append(h3)
            gates.append(times(h3, gate_m, gate_s))
            ups.append(times(h3, up_m, up_s))
            hids.append((gelu_parts(gates[i])[0] * ups[i]).astype(LOW))
            f = times_t(hids[i], down_m, down_s)
            fs.append(lax.psum(f.astype(LOW), "tensor"))
        ys, dfs, dgs, dus, dh3s = [], [], [], [], []
        dg4 = 0.0
        for i in range(2):
            f = wide(fs[i])
            ys.append((mids[i] + f * norm_factor(f) * (1.0 + g4)).astype(LOW))
            df, dg = norm_back(f, g4, dys[i])
            dg4 = dg4 + dg
            df = df.astype(LOW)
            dfs.append(df)
            dhid = times(df, down_m, down_s)
            gl, dgl = gelu_parts(gates[i])
            dgs.append((dhid * ups[i] * dgl).astype(LOW))
            dus.append((dhid * gl).astype(LOW))
            part = times_t(dgs[i], gate_m, gate_s) + times_t(dus[i], up_m, up_s)
            dh3s.append(lax.psum(part.astype(LOW), "tensor"))
        cat = lambda a: jnp.concatenate(a, axis=0)
        h3, dgl, dul, dfl, hid = map(cat, (h3s, dgs, dus, dfs, hids))

        def weight_grad(a, b):
            other = outer(a[:, mid:], b).astype(LOW)
            return scatter(outer(a[:, :mid], b), other)

        down_grad = weight_grad(dfl, hid)
        gate_grad = weight_grad(h3, dgl)
        up_grad = weight_grad(h3, dul)

        dx2s, dabs, dqs = [], [], []
        dg3 = dg2 = 0.0
        dk_all = dv_all = 0.0
        for i, sl in enumerate(halves):
            dv3, dg = norm_back(mids[i], g3, wide(dh3s[i]))
            dg3 = dg3 + dg
            dx2 = dys[i] + dv3
            dx2s.append(dx2)
            da, dg = norm_back(wide(attn[i]), g2, dx2)
            dg2 = dg2 + dg
            dab = da.astype(LOW)
            dabs.append(dab)
            do = times(dab, out_m, out_s).astype(LOW).reshape(half, groups, per, HD)
            capped, bounded = scores(sl)
            p = jnp.exp(capped - logs[i])
            dp = jnp.einsum("tkgd,lkd->kgtl", do, v_all, preferred_element_type=F32)
            dc = p * (dp - jnp.sum(p * dp, axis=-1, keepdims=True))
            ds = (dc * (1.0 - bounded * bounded)).astype(LOW)
            dq = jnp.einsum("kgtl,lkd->tkgd", ds, k_all, preferred_element_type=F32)
            dqs.append(dq.reshape(half, heads, HD))
            dk_all = dk_all + jnp.einsum(
                "kgtl,tkgd->lkd", ds, q[sl], preferred_element_type=F32
            )
            dv_all = dv_all + jnp.einsum(
                "kgtl,tkgd->lkd", p.astype(LOW), do, preferred_element_type=F32
            )
        dkv = jnp.concatenate(
            [dk_all.reshape(length, kw), dv_all.reshape(length, kw)], axis=1
        )
        if square:
            dkv = dkv[:toks] + wide(to_ctx(dkv[toks:].astype(LOW)))
        else:
            dkv = wide(
                lax.psum_scatter(
                    dkv.astype(LOW), "ctx", scatter_dimension=0, tiled=True
                )
            )
        dqr = (rotate_back(cat(dqs), cos, sin) * scale).astype(LOW).reshape(toks, qw)
        dkr = rotate_back(dkv[:, :kw].reshape(toks, groups, HD), cos, sin).astype(LOW)
        dqkv = jnp.concatenate(
            [dqr, dkr.reshape(toks, kw), dkv[:, kw:].astype(LOW)], axis=1
        )
        dh1 = wide(
            lax.psum(times_t(dqkv, qkv_m, qkv_s).astype(LOW), "tensor")
        )
        dab, o = cat(dabs), cat(outs_low)
        low = jnp.concatenate(
            [outer(h1[:, mid:], dqkv), outer(dab[:, mid:], o)], axis=1
        ).astype(LOW)
        high = jnp.concatenate(
            [outer(h1[:, :mid], dqkv), outer(dab[:, :mid], o)], axis=1
        )
        attn_grad = scatter(high, low)
        dv1, dg1 = norm_back(x, g1, dh1)
        input_grad = order(cat(dx2s) + dv1, back=True)
        layer_output = order(cat(ys), back=True)

        dgain = jnp.concatenate([dg1, dg2, dg3, dg4], axis=0)
        if square:
            dgain = dgain[:, :mid] + to_core(dgain[:, mid:])
            s = dgain[:, : mid // 2] + to_y(dgain[:, mid // 2 :])
            dgain = s[:, :blk] + to_ctx(s[:, blk:])
        else:
            dgain = dgain[:, :mid] + to_core(dgain[:, mid:])
            dgain = lax.psum_scatter(
                dgain, ("y", "ctx"), scatter_dimension=1, tiled=True
            )
        return (
            layer_output.reshape(rows, toks, width),
            input_grad.reshape(rows, toks, width),
            attn_grad[:, :qw],
            attn_grad[:, qw : qw + kw],
            attn_grad[:, qw + kw : qkv_w],
            attn_grad[:, qkv_w:],
            gate_grad,
            up_grad,
            down_grad,
            dgain[0],
            dgain[1],
            dgain[2],
            dgain[3],
        )

    return local


def solution(mesh):
    dp, nx = mesh.shape["dp"], mesh.shape["ctx"]
    nz = mesh.shape["tensor"]
    fine = Mesh(
        mesh.devices.reshape(dp // 2, 2, nx, nz), ("y", "core", "ctx", "tensor")
    )
    d = ("y", "core")
    w = P(("y", "core", "ctx"), "tensor")
    g = P(("y", "core", "ctx"))
    t = P(d, "ctx", None)
    return jax.shard_map(
        make_local(dp // 2, nx),
        mesh=fine,
        in_specs=(t, w, w, w, w, w, w, w, g, g, g, g, t, P(d, "ctx"), P(d, "ctx")),
        out_specs=(t, t, w, w, w, w, w, w, w, g, g, g, g),
        check_vma=False,
    )
```

time: 1790 us -> 1050 us (0.59)
  waiting for transfers between devices: 1450 us -> 511 us
  local copies, waits for them, and re-layouts: 22.6 us -> 125 us
  other arithmetic: 51.5 us -> 147 us
  blocking collectives: 78.3 us -> 0 us
  starting transfers between devices: 2.16 us -> 47.5 us
  matrix products: 161 us -> 192 us
    reduce_scatter x9 -> x0, waiting for transfers between devices: 620 us -> none  [the longest x1 141 us: local(): lax.psum_scatter(grad_gate, ('dp', 'ctx'), scatter_dimension=0, tiled=True)]
    psum x4, waiting for transfers between devices: 630 us -> 292 us  [the longest x1 78.7 us: local(): fs.append(lax.psum(f.astype(LOW), 'tensor'))]
    ppermute x0 -> x51, waiting for transfers between devices: none -> 219 us  [the longest x22 117 us: to_ctx(): return lax.ppermute(a, 'ctx', SWAP)]
    all_gather x7 -> x0, waiting for transfers between devices: 195 us -> none  [the longest x1 57.1 us: local(): lax.all_gather(gate_weight, ('dp', 'ctx'), axis=0, tiled=True)]
    unnamed x2 -> x0, blocking collectives: 49.5 us -> none
    ppermute x0 -> x51, starting transfers between devices: none -> 47 us  [the longest x22 24.6 us: to_ctx(): return lax.ppermute(a, 'ctx', SWAP)]
    concatenate x0 -> x14, local copies, waits for them, and re-layouts: none -> 33.6 us  [the longest x4 23.4 us: order(): return jnp.concatenate(out, axis=1)]
    slice x1 -> x35, local copies, waits for them, and re-layouts: 0.19 us -> 33.3 us  [the longest x4 11.8 us: scatter(): t1 = jnp.concatenate([s1[:h], s1[h:] + wide(gy)], axis=0).astype(LOW)]
  transfers between devices with their start and end apart: 20 -> 55, of which waited for: 19 -> 21; matrix products, arithmetic and copies ran while one was open for 8% -> 36% of each run, Pallas kernels for 0% -> 0%
where the time goes in v1:
time: 1050 us; the launch traced here: 1040 us
  waiting for transfers between devices  511 us (49%)
  matrix products  192 us (18%)
  other arithmetic  147 us (14%)
  local copies, waits for them, and re-layouts  125 us (12%)
  starting transfers between devices  47.5 us (5%)
  between operations  16.7 us (2%)
    ppermute x22, waiting for transfers between devices, to_ctx(): return lax.ppermute(a, 'ctx', SWAP)  117 us
    ppermute x19, waiting for transfers between devices, to_y(): return lax.ppermute(a, 'y', SWAP)  103 us
    psum x1, waiting for transfers between devices, local(): fs.append(lax.psum(f.astype(LOW), 'tensor'))  78.7 us
    psum x1, waiting for transfers between devices, local(): dh3s.append(lax.psum(part.astype(LOW), 'tensor'))  72.9 us
    psum x1, waiting for transfers between devices, local(): dh1 = wide(lax.psum(times_t(dqkv, qkv_m, qkv_s).astype(LOW), 'tensor'))  72 us
    psum x1, waiting for transfers between devices, local(): attn.append(lax.psum(times_t(o, out_m, out_s).astype(LOW), 'tensor'))  68.4 us
    dot_general x18, matrix products, dot(): return jnp.dot(a, b, preferred_element_type=F32)  63.9 us
    dot_general x18, matrix products, dot_t(): return jnp.einsum('ti,di->td', a, b, preferred_element_type=F32)  58.6 us
  transfers between devices with their start and end apart: 55, of which 21 were waited for; matrix products, arithmetic and copies ran while one was open for 36% of the time, Pallas kernels for 0%

profile of v1, /device:TPU:0, one launch (start us, length us, event | category | flops | bytes accessed | tf_op | source)
XLA Modules:
  0.0 1039.3 jit_solution(12753532132637376627)
XLA Ops:
  52.7 7.5 collective-permute-done
  65.1 29.4 %collective-permute-done.2 = bf16[152,1024]{1,0:T(8,128)(2,1)S(1)} collective-permute-done((bf16[152,1024]{1,0:T(8,128)(2,1)S(1)}, bf16[152,1024]{1,0:T(8,128)(2,1)S(1)}, u32[]{:S(2)}, u32[]{:S(2)}) %collective-permute-start.2) | collective-permute-done | bytes 311328 | tf_op jit(solution)/shard_map/ppermute | solution.py:58
  101.0 10.7 %collective-permute-done.3 = bf16[152,1024]{1,0:T(8,128)(2,1)S(1)} collective-permute-done((bf16[152,1024]{1,0:T(8,128)(2,1)S(1)}, bf16[152,1024]{1,0:T(8,128)(2,1)S(1)}, u32[]{:S(2)}, u32[]{:S(2)}) %collective-permute-start.3) | collective-permute-done | bytes 311328 | tf_op jit(solution)/shard_map/ppermute | solution.py:62
  136.3 36.2 %collective-permute-done.19 = bf16[144,2304]{1,0:T(8,128)(2,1)S(1)} collective-permute-done((bf16[144,2304]{1,0:T(8,128)(2,1)S(1)}, bf16[144,2304]{1,0:T(8,128)(2,1)S(1)}, u32[]{:S(2)}, u32[]{:S(2)}) %collective-permute-start.19) | collective-permute-done | bytes 663584 | tf_op jit(solution)/shard_map/ppermute | solution.py:62
  194.0 12.9 %collective-permute-done.6 = bf16[512,512]{1,0:T(8,128)(2,1)S(1)} collective-permute-done((bf16[512,512]{1,0:T(8,128)(2,1)S(1)}, bf16[512,512]{1,0:T(8,128)(2,1)S(1)}, u32[]{:S(2)}, u32[]{:S(2)}) %collective-permute-start.6) | collective-permute-done | bytes 524320 | tf_op jit(solution)/shard_map/ppermute | solution.py:58
  235.0 10.2 collective-permute-done.24
  247.4 68.4 %all-reduce.15.cloned.1.call-done = (bf16[256,2304]{1,0:T(8,128)(2,1)}, bf16[256,2304]{1,0:T(8,128)(2,1)}) async-done(((bf16[256,2304]{1,0:T(8,128)(2,1)}, bf16[256,2304]{1,0:T(8,128)(2,1)}), (bf16[256,2304]{1,0:T(8,128)(2,1)}, bf16[256,2304]{1,0:T(8,128)(2,1)})) %all-reduce.15.cloned.1.call-update) | async-done | bytes 2359312 | tf_op jit(solution)/shard_map/psum | solution.py:278
  345.1 6.7 multiply_convert_fusion.2
  358.3 6.6 multiply_convert_fusion.4
  396.8 78.7 %all-reduce.13.cloned.1.call-done = (bf16[256,2304]{1,0:T(8,128)(2,1)}, bf16[256,2304]{1,0:T(8,128)(2,1)}) async-done(((bf16[256,2304]{1,0:T(8,128)(2,1)}, bf16[256,2304]{1,0:T(8,128)(2,1)}), (bf16[256,2304]{1,0:T(8,128)(2,1)}, bf16[256,2304]{1,0:T(8,128)(2,1)})) %all-reduce.13.cloned.1.call-update) | async-done | bytes 2359312 | tf_op jit(solution)/shard_map/psum | solution.py:290
  542.9 7.6 convolution_convert_fusion
  561.3 72.9 %all-reduce.11.cloned.1.call-done = (bf16[256,2304]{1,0:T(8,128)(2,1)}, bf16[256,2304]{1,0:T(8,128)(2,1)}) async-done(((bf16[256,2304]{1,0:T(8,128)(2,1)}, bf16[256,2304]{1,0:T(8,128)(2,1)}), (bf16[256,2304]{1,0:T(8,128)(2,1)}, bf16[256,2304]{1,0:T(8,128)(2,1)})) %all-reduce.11.cloned.1.call-update) | async-done | bytes 2359312 | tf_op jit(solution)/shard_map/psum | solution.py:305
  634.3 6.3 fusion.26
  682.5 6.5 collective-permute-done.27
  728.4 72.0 %all-reduce.9.cloned.1.call-done = bf16[512,2304]{1,0:T(8,128)(2,1)} async-done(((bf16[512,2304]{1,0:T(8,128)(2,1)}), bf16[512,2304]{1,0:T(8,128)(2,1)}) %all-reduce.9.cloned.1.call-update) | async-done | bytes 2359312 | tf_op jit(solution)/shard_map/psum | solution.py:360
  816.6 7.3 concatenate.232
  834.5 9.7 fusion.249
  850.8 11.7 %fusion.248 = (bf16[1152,2304]{1,0:T(8,128)(2,1)}, f32[1152,2304]{1,0:T(8,128)}) fusion(bf16[1152,2304]{1,0:T(8,128)(2,1)} %collective-permute-done.33, bf16[256,2304]{1,0:T(8,128)(2,1)} %copy-done.85, bf16[256,2304]{1,0:T(8,128)(2,1)} %copy-done.83, bf16[256,2304]{1,0:T(8,128)(2,1)S(1)} %get-tuple-element.244, bf16[256,2304]{1,0:T(8,128)(2,1)S(1)} %copy-done.15), kind=kOutput, calls=%fused_computation.592 | convolution fusion | flops 2732949504 | bytes 25952256 | tf_op jit(solution)/shard_map/td,ti->di/dot_general | solution.py:54
  877.0 6.3 collective-permute-done.36
  887.9 8.0 fusion.233
  905.2 43.3 %collective-permute-done.29 = bf16[144,1536]{1,0:T(8,128)(2,1)S(1)} collective-permute-done((bf16[144,1536]{1,0:T(8,128)(2,1)}, bf16[144,1536]{1,0:T(8,128)(2,1)S(1)}, u32[]{:S(2)}, u32[]{:S(2)}) %collective-permute-start.29) | collective-permute-done | bytes 442400 | tf_op jit(solution)/shard_map/ppermute | solution.py:62
  964.4 16.5 %collective-permute-done.40 = bf16[288,2304]{1,0:T(8,128)(2,1)} collective-permute-done((bf16[288,2304]{1,0:T(8,128)(2,1)}, bf16[288,2304]{1,0:T(8,128)(2,1)}, u32[]{:S(2)}, u32[]{:S(2)}) %collective-permute-start.40) | collective-permute-done | bytes 1327136 | tf_op jit(solution)/shard_map/ppermute | solution.py:58
  985.3 24.0 %collective-permute-done.35 = bf16[288,2304]{1,0:T(8,128)(2,1)S(1)} collective-permute-done((bf16[288,2304]{1,0:T(8,128)(2,1)}, bf16[288,2304]{1,0:T(8,128)(2,1)S(1)}, u32[]{:S(2)}, u32[]{:S(2)}) %collective-permute-start.35) | collective-permute-done | bytes 1327136 | tf_op jit(solution)/shard_map/ppermute | solution.py:58
  1014.8 9.9 collective-permute-done.30
  (701 shorter events, 453.6 us)
Async XLA Ops:
  7.2 308.6 %all-reduce.15.cloned.1.call-start = ((), (), s32[]{:S(2)}) async-start(), calls=%async_computation.3 | async-start | bytes 4718592 | tf_op jit(solution)/shard_map/psum | solution.py:278
  13.7 109.4 %collective-permute-start.12 = (bf16[288,2304]{1,0:T(8,128)(2,1)}, bf16[288,2304]{1,0:T(8,128)(2,1)}, u32[]{:S(2)}, u32[]{:S(2)}) collective-permute-start(bf16[288,2304]{1,0:T(8,128)(2,1)} %param.20), channel_id=1, source_target_pairs={{0,4},{4,0},{1,5},{5,1},{2,6},{6,2},{3,7},{7,3},{8,12},{12,8},{9,1... | collective-permute-start | bytes 3981320 | tf_op jit(solution)/shard_map/ppermute | solution.py:58
  46.0 83.0 %collective-permute-start.13 = (bf16[288,2304]{1,0:T(8,128)(2,1)S(1)}, bf16[288,2304]{1,0:T(8,128)(2,1)S(1)}, u32[]{:S(2)}, u32[]{:S(2)}) collective-permute-start(bf16[288,2304]{1,0:T(8,128)(2,1)S(1)} %copy-done.82), channel_id=1, source_target_pairs={{0,16},{16,0},{1,17},{17,1},{2,18},{18,2},{3,19},{19,3},{4,20},{20... | collective-permute-start | bytes 3981320 | tf_op jit(solution)/shard_map/ppermute | solution.py:62
  47.1 79.7 %collective-permute-start.17 = (bf16[288,2304]{1,0:T(8,128)(2,1)S(1)}, bf16[288,2304]{1,0:T(8,128)(2,1)S(1)}, u32[]{:S(2)}, u32[]{:S(2)}) collective-permute-start(bf16[288,2304]{1,0:T(8,128)(2,1)S(1)} %copy-done.80), channel_id=1, source_target_pairs={{0,4},{4,0},{1,5},{5,1},{2,6},{6,2},{3,7},{7,3},{8,12},{12,8},{9,1... | collective-permute-start | bytes 3981320 | tf_op jit(solution)/shard_map/ppermute | solution.py:58
  50.8 77.6 %collective-permute-start.18 = (bf16[288,2304]{1,0:T(8,128)(2,1)S(1)}, bf16[288,2304]{1,0:T(8,128)(2,1)S(1)}, u32[]{:S(2)}, u32[]{:S(2)}) collective-permute-start(bf16[288,2304]{1,0:T(8,128)(2,1)S(1)} %copy-done.80), channel_id=1, source_target_pairs={{0,16},{16,0},{1,17},{17,1},{2,18},{18,2},{3,19},{19,3},{4,20},{20... | collective-permute-start | bytes 3981320 | tf_op jit(solution)/shard_map/ppermute | solution.py:62
  116.9 58.9 %collective-permute-start.4 = (bf16[1216,1024]{1,0:T(8,128)(2,1)}, bf16[1216,1024]{1,0:T(8,128)(2,1)S(1)}, u32[]{:S(2)}, u32[]{:S(2)}) collective-permute-start(bf16[1216,1024]{1,0:T(8,128)(2,1)} %constant_dynamic-update-slice_fusion.3), channel_id=1, source_target_pairs={{0,8},{8,0},{1,9},{9,1},{2,10},{10,2},{3,11},{11,3},{4,12},{12,4},... | collective-permute-start | bytes 7471112 | tf_op jit(solution)/shard_map/ppermute | solution.py:66
  123.2 103.4 %collective-permute-start.22 = (bf16[288,2304]{1,0:T(8,128)(2,1)}, bf16[288,2304]{1,0:T(8,128)(2,1)}, u32[]{:S(2)}, u32[]{:S(2)}) collective-permute-start(bf16[288,2304]{1,0:T(8,128)(2,1)} %param.22), channel_id=1, source_target_pairs={{0,4},{4,0},{1,5},{5,1},{2,6},{6,2},{3,7},{7,3},{8,12},{12,8},{9,1... | collective-permute-start | bytes 3981320 | tf_op jit(solution)/shard_map/ppermute | solution.py:58
  126.8 101.4 %collective-permute-start.23 = (bf16[288,2304]{1,0:T(8,128)(2,1)}, bf16[288,2304]{1,0:T(8,128)(2,1)}, u32[]{:S(2)}, u32[]{:S(2)}) collective-permute-start(bf16[288,2304]{1,0:T(8,128)(2,1)} %param.22), channel_id=1, source_target_pairs={{0,16},{16,0},{1,17},{17,1},{2,18},{18,2},{3,19},{19,3},{4,20},{20... | collective-permute-start | bytes 3981320 | tf_op jit(solution)/shard_map/ppermute | solution.py:62
  212.7 113.1 %collective-permute-start.21 = (bf16[1152,2304]{1,0:T(8,128)(2,1)}, bf16[1152,2304]{1,0:T(8,128)(2,1)}, u32[]{:S(2)}, u32[]{:S(2)}) collective-permute-start(bf16[1152,2304]{1,0:T(8,128)(2,1)} %constant_dynamic-update-slice_fusion.21), channel_id=1, source_target_pairs={{0,8},{8,0},{1,9},{9,1},{2,10},{10,2},{3,11},{11,3},{4,12},{12,4},... | collective-permute-start | bytes 15925256 | tf_op jit(solution)/shard_map/ppermute | solution.py:66
  219.2 256.3 %all-reduce.13.cloned.1.call-start = ((), (), s32[]{:S(2)}) async-start(), calls=%async_computation.2 | async-start | bytes 4718592 | tf_op jit(solution)/shard_map/psum | solution.py:290
  224.0 110.7 %collective-permute-start.16 = (bf16[1152,2304]{1,0:T(8,128)(2,1)}, bf16[1152,2304]{1,0:T(8,128)(2,1)}, u32[]{:S(2)}, u32[]{:S(2)}) collective-permute-start(bf16[1152,2304]{1,0:T(8,128)(2,1)} %constant_dynamic-update-slice_fusion.16), channel_id=1, source_target_pairs={{0,8},{8,0},{1,9},{9,1},{2,10},{10,2},{3,11},{11,3},{4,12},{12,4},... | collective-permute-start | bytes 15925256 | tf_op jit(solution)/shard_map/ppermute | solution.py:66
  247.4 122.3 %collective-permute-start.26 = (bf16[1152,2304]{1,0:T(8,128)(2,1)}, bf16[1152,2304]{1,0:T(8,128)(2,1)}, u32[]{:S(2)}, u32[]{:S(2)}) collective-permute-start(bf16[1152,2304]{1,0:T(8,128)(2,1)} %constant_dynamic-update-slice_fusion.26), channel_id=1, source_target_pairs={{0,8},{8,0},{1,9},{9,1},{2,10},{10,2},{3,11},{11,3},{4,12},{12,4},... | collective-permute-start | bytes 15925256 | tf_op jit(solution)/shard_map/ppermute | solution.py:66
  380.4 253.8 %all-reduce.11.cloned.1.call-start = ((), (), s32[]{:S(2)}) async-start(), calls=%async_computation.1 | async-start | bytes 4718592 | tf_op jit(solution)/shard_map/psum | solution.py:305
  539.0 261.4 %all-reduce.9.cloned.1.call-start = ((), (), s32[]{:S(2)}) async-start(), calls=%async_computation | async-start | bytes 4718592 | tf_op jit(solution)/shard_map/psum | solution.py:360
  550.6 274.7 %collective-permute-start.43 = (bf16[1152,2304]{1,0:T(8,128)(2,1)}, bf16[1152,2304]{1,0:T(8,128)(2,1)}, u32[]{:S(2)}, u32[]{:S(2)}) collective-permute-start(bf16[1152,2304]{1,0:T(8,128)(2,1)} %convolution_convert_fusion), channel_id=1, source_target_pairs={{0,8},{8,0},{1,9},{9,1},{2,10},{10,2},{3,11},{11,3},{4,12},{12,4},... | collective-permute-start | bytes 15925256 | tf_op jit(solution)/shard_map/ppermute | solution.py:66
  555.7 293.8 %collective-permute-start.33 = (bf16[1152,2304]{1,0:T(8,128)(2,1)}, bf16[1152,2304]{1,0:T(8,128)(2,1)}, u32[]{:S(2)}, u32[]{:S(2)}) collective-permute-start(bf16[1152,2304]{1,0:T(8,128)(2,1)} %convolution_convert_fusion.2), channel_id=1, source_target_pairs={{0,8},{8,0},{1,9},{9,1},{2,10},{10,2},{3,11},{11,3},{4,12},{12,4},... | collective-permute-start | bytes 15925256 | tf_op jit(solution)/shard_map/ppermute | solution.py:66
  561.3 272.9 %collective-permute-start.38 = (bf16[1152,2304]{1,0:T(8,128)(2,1)}, bf16[1152,2304]{1,0:T(8,128)(2,1)}, u32[]{:S(2)}, u32[]{:S(2)}) collective-permute-start(bf16[1152,2304]{1,0:T(8,128)(2,1)} %convolution_convert_fusion.1), channel_id=1, source_target_pairs={{0,8},{8,0},{1,9},{9,1},{2,10},{10,2},{3,11},{11,3},{4,12},{12,4},... | collective-permute-start | bytes 15925256 | tf_op jit(solution)/shard_map/ppermute | solution.py:66
  724.7 163.1 %collective-permute-start.28 = (bf16[1152,1536]{0,1:T(8,128)(2,1)}, bf16[1152,1536]{0,1:T(8,128)(2,1)}, u32[]{:S(2)}, u32[]{:S(2)}) collective-permute-start(bf16[1152,1536]{0,1:T(8,128)(2,1)} %pad_maximum_fusion), channel_id=1, source_target_pairs={{0,8},{8,0},{1,9},{9,1},{2,10},{10,2},{3,11},{11,3},{4,12},{12,4},... | collective-permute-start | bytes 10616840 | tf_op jit(solution)/shard_map/ppermute | solution.py:66
  871.6 85.8 %collective-permute-start.47 = (bf16[288,2304]{1,0:T(8,128)(2,1)}, bf16[288,2304]{1,0:T(8,128)(2,1)}, u32[]{:S(2)}, u32[]{:S(2)}) collective-permute-start(bf16[288,2304]{1,0:T(8,128)(2,1)} %pad_maximum_fusion.24), channel_id=1, source_target_pairs={{0,16},{16,0},{1,17},{17,1},{2,18},{18,2},{3,19},{19,3},{4,20},{20... | collective-permute-start | bytes 3981320 | tf_op jit(solution)/shard_map/ppermute | solution.py:62
  872.8 86.1 %collective-permute-start.45 = (bf16[288,2304]{1,0:T(8,128)(2,1)}, bf16[288,2304]{1,0:T(8,128)(2,1)}, u32[]{:S(2)}, u32[]{:S(2)}) collective-permute-start(bf16[288,2304]{1,0:T(8,128)(2,1)} %pad_maximum_fusion.23), channel_id=1, source_target_pairs={{0,4},{4,0},{1,5},{5,1},{2,6},{6,2},{3,7},{7,3},{8,12},{12,8},{9,1... | collective-permute-start | bytes 3981320 | tf_op jit(solution)/shard_map/ppermute | solution.py:58
  883.3 80.6 %collective-permute-start.42 = (bf16[288,2304]{1,0:T(8,128)(2,1)}, bf16[288,2304]{1,0:T(8,128)(2,1)}, u32[]{:S(2)}, u32[]{:S(2)}) collective-permute-start(bf16[288,2304]{1,0:T(8,128)(2,1)} %pad_maximum_fusion.22), channel_id=1, source_target_pairs={{0,16},{16,0},{1,17},{17,1},{2,18},{18,2},{3,19},{19,3},{4,20},{20... | collective-permute-start | bytes 3981320 | tf_op jit(solution)/shard_map/ppermute | solution.py:62
  957.4 51.8 %collective-permute-start.35 = (bf16[288,2304]{1,0:T(8,128)(2,1)}, bf16[288,2304]{1,0:T(8,128)(2,1)S(1)}, u32[]{:S(2)}, u32[]{:S(2)}) collective-permute-start(bf16[288,2304]{1,0:T(8,128)(2,1)} %pad_maximum_fusion.19), channel_id=1, source_target_pairs={{0,4},{4,0},{1,5},{5,1},{2,6},{6,2},{3,7},{7,3},{8,12},{12,8},{9,1... | collective-permute-start | bytes 3981320 | tf_op jit(solution)/shard_map/ppermute | solution.py:58
  959.0 54.2 %collective-permute-start.32 = (bf16[288,1536]{1,0:T(8,128)(2,1)S(1)}, bf16[288,1536]{1,0:T(8,128)(2,1)}, u32[]{:S(2)}, u32[]{:S(2)}) collective-permute-start(bf16[288,1536]{1,0:T(8,128)(2,1)S(1)} %copy.116), channel_id=1, source_target_pairs={{0,16},{16,0},{1,17},{17,1},{2,18},{18,2},{3,19},{19,3},{4,20},{20... | collective-permute-start | bytes 2654216 | tf_op jit(solution)/shard_map/ppermute | solution.py:62
  963.9 60.8 %collective-permute-start.30 = (bf16[288,1536]{1,0:T(8,128)(2,1)S(1)}, bf16[288,1536]{1,0:T(8,128)(2,1)}, u32[]{:S(2)}, u32[]{:S(2)}) collective-permute-start(bf16[288,1536]{1,0:T(8,128)(2,1)S(1)} %copy-done.98), channel_id=1, source_target_pairs={{0,4},{4,0},{1,5},{5,1},{2,6},{6,2},{3,7},{7,3},{8,12},{12,8},{9,1... | collective-permute-start | bytes 2654216 | tf_op jit(solution)/shard_map/ppermute | solution.py:58
  (207 other events, 2573.4 us)
Sparse Core Ops, SparseCore 0:
  219.3 96.4 all-reduce.14
  380.5 95.0 all-reduce.12
  539.1 95.0 all-reduce.10
  705.5 94.8 all-reduce.8

commit v2 on v1

v2 whole, which is shorter than its diff:
```python
import math

import jax
import jax.numpy as jnp
from jax import lax
from jax.experimental import pallas as pl
from jax.experimental.pallas import tpu as pltpu
from jax.sharding import Mesh
from jax.sharding import PartitionSpec as P

HD = 256
NORM_EPSILON = 1e-06
SOFT_CAP = 50.0
MASKED_SCORE = -1e30
SWAP = [(0, 1), (1, 0)]
LOW = jnp.bfloat16
F32 = jnp.float32
VMEM_MB = 56


def wide(a):
    return a.astype(F32)


def after(value, *deps):
    return lax.optimization_barrier((value,) + deps)[0]


class Order:
    def __init__(self):
        self.last = ()

    def __call__(self, *values):
        return after(values, *self.last) if self.last else values

    def run(self, fn, *values, **kw):
        out = fn(*self(*values), **kw)
        self.last = (out,)
        return out

    def send(self, move, value):
        (value,) = self(value)
        self.last = (value,)
        return move(value)


def to_ctx(a):
    return lax.ppermute(a, "ctx", SWAP)


def to_y(a):
    return lax.ppermute(a, "y", SWAP)


def to_core(a):
    return lax.ppermute(a, "core", SWAP)


def hop(bit):
    return lambda a: lax.ppermute(a, "tensor", [(k, k ^ bit) for k in range(4)])


def nn(a, b):
    return jnp.dot(a, b, preferred_element_type=F32)


def nt(a, b):
    return lax.dot_general(a, b, (((1,), (1,)), ((), ())), preferred_element_type=F32)


def tn(a, b):
    return lax.dot_general(a, b, (((0,), (0,)), ((), ())), preferred_element_type=F32)


def norm_factor(v):
    return lax.rsqrt(jnp.mean(v * v, axis=-1, keepdims=True) + NORM_EPSILON)


def norm_back(v, gain, grad):
    r = norm_factor(v)
    w = (1.0 + gain) * grad
    dv = r * w - v * (r * r * r) * jnp.mean(v * w, axis=-1, keepdims=True)
    dg = jnp.sum(grad * v * r, axis=0, keepdims=True)
    return dv, dg


def gelu_parts(u):
    k = math.sqrt(2.0 / math.pi)
    th = jnp.tanh(k * (u + 0.044715 * u * u * u))
    g = 0.5 * u * (1.0 + th)
    dg = 0.5 * (1.0 + th) + 0.5 * u * (1.0 - th * th) * k * (1.0 + 3 * 0.044715 * u * u)
    return g, dg


def turn(v, c, s):
    h = HD // 2
    a, b = v[:, :h], v[:, h:]
    return jnp.concatenate([a * c - b * s, b * c + a * s], axis=1)


def turn_back(v, c, s):
    h = HD // 2
    a, b = v[:, :h], v[:, h:]
    return jnp.concatenate([a * c + b * s, b * c - a * s], axis=1)


def kernel(body, grid, ins, outs, flops=0, scratch=()):
    size = lambda s, d: math.prod(s) * jnp.dtype(d).itemsize
    moved = sum(size(a.shape, a.dtype) for a, _, _ in ins)
    moved += sum(size(s, d) for s, d, _, _ in outs)
    return pl.pallas_call(
        body,
        grid=grid,
        in_specs=[pl.BlockSpec(b, m) for _, b, m in ins],
        out_specs=[pl.BlockSpec(b, m) for _, _, b, m in outs],
        out_shape=[jax.ShapeDtypeStruct(s, d) for s, d, _, _ in outs],
        scratch_shapes=list(scratch),
        cost_estimate=pl.CostEstimate(
            flops=int(flops), bytes_accessed=int(moved), transcendentals=0
        ),
        compiler_params=pltpu.CompilerParams(vmem_limit_bytes=VMEM_MB * 2**20),
    )(*[a for a, _, _ in ins])


def all_of(shape):
    return tuple(shape), lambda *i: (0,) * len(shape)


def qkv_kernel(x, gain, wm, ws, cos, sin, qw):
    toks, width = x.shape
    mid, cols = wm.shape
    kw = (cols - qw) // 2
    scale = 1.0 / math.sqrt(HD)

    def body(x_r, g_r, wm_r, ws_r, c_r, s_r, h_r, q_r, kv_r):
        xv = wide(x_r[...])
        h = (xv * norm_factor(xv) * (1.0 + g_r[...])).astype(LOW)
        h_r[...] = h
        raw = nn(h[:, :mid], wm_r[...]) + nn(h[:, mid:], ws_r[...])
        c, s = c_r[...], s_r[...]
        for j in range(qw // HD):
            cut = slice(j * HD, (j + 1) * HD)
            q_r[:, cut] = (turn(raw[:, cut], c, s) * scale).astype(LOW)
        for j in range(kw // HD):
            cut = slice(j * HD, (j + 1) * HD)
            kv_r[:, cut] = turn(raw[:, qw + j * HD : qw + (j + 1) * HD], c, s).astype(
                LOW
            )
        kv_r[:, kw:] = raw[:, qw + kw :].astype(LOW)

    ins = [(a, *all_of(a.shape)) for a in (x, gain, wm, ws, cos, sin)]
    outs = [
        ((toks, n), LOW, *all_of((toks, n))) for n in (width, qw, 2 * kw)
    ]
    return kernel(body, (1,), ins, outs, 2 * toks * width * cols)


def query_block(rows, length):
    return min(rows, 256 if length <= 2048 else 128)


def attn_kernel(q, kv, allowed, wm, ws):
    rows, qw = q.shape
    length = kv.shape[0]
    mid = wm.shape[0]
    qb = query_block(rows, length)
    heads = qw // HD

    def body(q_r, kv_r, m_r, wm_r, ws_r, o_r, t_r, a_r):
        ok = m_r[...] > 0
        k, v = kv_r[:, :HD], kv_r[:, HD:]
        logs = []
        for j in range(heads):
            cut = slice(j * HD, (j + 1) * HD)
            b = jnp.tanh(nt(q_r[:, cut], k) * (1.0 / SOFT_CAP))
            c = jnp.where(ok, SOFT_CAP * b, MASKED_SCORE)
            peak = jnp.max(c, axis=-1, keepdims=True)
            e = jnp.exp(c - peak)
            total = jnp.sum(e, axis=-1, keepdims=True)
            p = (e / total).astype(LOW)
            o_r[:, cut] = nn(p, v).astype(LOW)
            logs.append(jnp.broadcast_to(peak + jnp.log(total), (qb, 128)))
        t_r[...] = jnp.concatenate(logs, axis=1)
        o = o_r[...]
        a_r[:, :mid] = nt(o, wm_r[...]).astype(LOW)
        a_r[:, mid:] = nt(o, ws_r[...]).astype(LOW)

    row = lambda n: ((qb, n), lambda i: (i, 0))
    ins = [(q, *row(qw)), (kv, *all_of(kv.shape)), (allowed, *row(length))]
    ins += [(w, *all_of(w.shape)) for w in (wm, ws)]
    outs = [
        ((rows, qw), LOW, *row(qw)),
        ((rows, 128 * heads), F32, *row(128 * heads)),
        ((rows, 2 * mid), LOW, *row(2 * mid)),
    ]
    flops = 4 * rows * length * qw + 4 * rows * mid * qw
    return kernel(body, (rows // qb,), ins, outs, flops)


def attn_back_kernel(
    dh3, x2, dy, a, g3, g2, wm, ws, q, kv, allowed, logs, cos, sin, before
):
    rows, width = x2.shape
    qw = q.shape[1]
    length = kv.shape[0]
    mid = wm.shape[0]
    qb = query_block(rows, length)
    heads = qw // HD
    scale = 1.0 / math.sqrt(HD)
    first = before is None

    def body(*refs):
        refs = list(refs)
        d_r, x_r, dy_r, a_r, g3_r, g2_r, wm_r, ws_r = refs[:8]
        q_r, kv_r, m_r, t_r, c_r, s_r = refs[8:14]
        dx_r, da_r, dq_r, dkv_r, dg_r = refs[-5:]
        step = pl.program_id(0)

        @pl.when(step == 0)
        def _():
            dkv_r[...] = jnp.zeros_like(dkv_r) if first else refs[14][...]
            dg_r[...] = jnp.zeros_like(dg_r) if first else refs[15][...]

        dv3, dg3 = norm_back(x_r[...], g3_r[...], wide(d_r[...]))
        dx2 = wide(dy_r[...]) + dv3
        dx_r[...] = dx2
        da, dg2 = norm_back(wide(a_r[...]), g2_r[...], dx2)
        dg_r[0:1] += dg2
        dg_r[1:2] += dg3
        da = da.astype(LOW)
        da_r[...] = da
        do = (nn(da[:, :mid], wm_r[...]) + nn(da[:, mid:], ws_r[...])).astype(LOW)
        ok = m_r[...] > 0
        k, v = kv_r[:, :HD], kv_r[:, HD:]
        c, s = c_r[...], s_r[...]
        dk = dv = 0.0
        for j in range(heads):
            cut = slice(j * HD, (j + 1) * HD)
            qj, doj = q_r[:, cut], do[:, cut]
            b = jnp.tanh(nt(qj, k) * (1.0 / SOFT_CAP))
            logit = jnp.where(ok, SOFT_CAP * b, MASKED_SCORE)
            p = jnp.exp(logit - t_r[:, j * 128 : j * 128 + 1])
            dp = nt(doj, v)
            dc = p * (dp - jnp.sum(p * dp, axis=-1, keepdims=True))
            ds = (dc * (1.0 - b * b)).astype(LOW)
            dq_r[:, cut] = (turn_back(nn(ds, k), c, s) * scale).astype(LOW)
            dk = dk + tn(ds, qj)
            dv = dv + tn(p.astype(LOW), doj)
        dkv_r[:, :HD] += dk
        dkv_r[:, HD:] += dv

    row = lambda n: ((qb, n), lambda i: (i, 0))
    ins = [(v, *row(width)) for v in (dh3, x2, dy, a)]
    ins += [(v, *all_of(v.shape)) for v in (g3, g2, wm, ws)]
    ins += [(q, *row(qw)), (kv, *all_of(kv.shape)), (allowed, *row(length))]
    ins += [(logs, *row(128 * heads)), (cos, *row(HD // 2)), (sin, *row(HD // 2))]
    if not first:
        ins += [(v, *all_of(v.shape)) for v in before]
    outs = [
        ((rows, width), F32, *row(width)),
        ((rows, width), LOW, *row(width)),
        ((rows, qw), LOW, *row(qw)),
        ((length, 2 * HD), F32, *all_of((length, 2 * HD))),
        ((8, width), F32, *all_of((8, width))),
    ]
    flops = 10 * rows * length * qw + 4 * rows * mid * qw
    return kernel(body, (rows // qb,), ins, outs, flops)


def ffn_in_kernel(a, x, g2, g3, gm, gs, um, us):
    rows, width = x.shape
    mid, units = gm.shape
    bn = math.gcd(units, 768)

    def body(a_r, x_r, g2_r, g3_r, gm_r, gs_r, um_r, us_r, x2_r, h_r, g_r, u_r, hid_r):
        @pl.when(pl.program_id(0) == 0)
        def _():
            av = wide(a_r[...])
            x2 = wide(x_r[...]) + av * norm_factor(av) * (1.0 + g2_r[...])
            x2_r[...] = x2
            h_r[...] = (x2 * norm_factor(x2) * (1.0 + g3_r[...])).astype(LOW)

        hm, hs = h_r[:, :mid], h_r[:, mid:]
        gate = nn(hm, gm_r[...]) + nn(hs, gs_r[...])
        up = nn(hm, um_r[...]) + nn(hs, us_r[...])
        g_r[...] = gate
        u_r[...] = up
        hid_r[...] = (gelu_parts(gate)[0] * up).astype(LOW)

    w = ((mid, bn), lambda j: (0, j))
    t = ((rows, bn), lambda j: (0, j))
    ins = [(v, *all_of(v.shape)) for v in (a, x, g2, g3)]
    ins += [(v, *w) for v in (gm, gs, um, us)]
    outs = [
        ((rows, width), F32, *all_of((rows, width))),
        ((rows, width), LOW, *all_of((rows, width))),
        ((rows, units), F32, *t),
        ((rows, units), F32, *t),
        ((rows, units), LOW, *t),
    ]
    return kernel(body, (units // bn,), ins, outs, 4 * rows * width * units)


def project_kernel(u, wm, ws):
    rows, cols = u.shape
    mid = wm.shape[0]
    bd = math.gcd(mid, 384)
    n = mid // bd

    def body(u_r, m_r, s_r, o_r):
        j = pl.program_id(0)

        @pl.when(j < n)
        def _():
            o_r[...] = nt(u_r[...], m_r[...]).astype(LOW)

        @pl.when(j >= n)
        def _():
            o_r[...] = nt(u_r[...], s_r[...]).astype(LOW)

    ins = [
        (u, *all_of(u.shape)),
        (wm, (bd, cols), lambda j: (jnp.minimum(j, n - 1), 0)),
        (ws, (bd, cols), lambda j: (jnp.maximum(j - n, 0), 0)),
    ]
    outs = [((rows, 2 * mid), LOW, (rows, bd), lambda j: (0, j))]
    return kernel(body, (2 * n,), ins, outs, 4 * rows * mid * cols)[0]


def ffn_back_kernel(f, x2, dy, g4, gate, up, dm, ds, gm, gs, um, us):
    rows, width = x2.shape
    mid, units = dm.shape
    bn, bd = math.gcd(units, 768), math.gcd(mid, 384)
    n1, n2 = units // bn, mid // bd

    def body(
        f_r, x2_r, dy_r, g4_r, gate_r, up_r, dm_r, ds_r, gm_r, gs_r, um_r, us_r,
        y_r, df_r, dg_r, du_r, g_r, o_r,
    ):
        j = pl.program_id(0)

        @pl.when(j == 0)
        def _():
            fv, g4v = wide(f_r[...]), g4_r[...]
            y_r[...] = (x2_r[...] + fv * norm_factor(fv) * (1.0 + g4v)).astype(LOW)
            df, dg = norm_back(fv, g4v, wide(dy_r[...]))
            df_r[...] = df.astype(LOW)
            g_r[...] = dg

        for k in range(n1):

            @pl.when(j == k)
            def _():
                dh = nn(df_r[:, :mid], dm_r[...]) + nn(df_r[:, mid:], ds_r[...])
                gl, dgl = gelu_parts(gate_r[...])
                cut = slice(k * bn, (k + 1) * bn)
                dg_r[:, cut] = (dh * up_r[...] * dgl).astype(LOW)
                du_r[:, cut] = (dh * gl).astype(LOW)

        @pl.when((j >= n1) & (j < n1 + n2))
        def _():
            o_r[...] = (nt(dg_r[...], gm_r[...]) + nt(du_r[...], um_r[...])).astype(LOW)

        @pl.when(j >= n1 + n2)
        def _():
            o_r[...] = (nt(dg_r[...], gs_r[...]) + nt(du_r[...], us_r[...])).astype(LOW)

    w = ((mid, bn), lambda j: (0, jnp.minimum(j, n1 - 1)))
    t = ((rows, bn), lambda j: (0, jnp.minimum(j, n1 - 1)))
    lo = ((bd, units), lambda j: (jnp.clip(j - n1, 0, n2 - 1), 0))
    hi = ((bd, units), lambda j: (jnp.clip(j - n1 - n2, 0, n2 - 1), 0))
    ins = [(v, *all_of(v.shape)) for v in (f, x2, dy, g4)]
    ins += [(gate, *t), (up, *t), (dm, *w), (ds, *w)]
    ins += [(gm, *lo), (gs, *hi), (um, *lo), (us, *hi)]
    whole = lambda n, d: ((rows, n), d, *all_of((rows, n)))
    outs = [
        whole(width, LOW),
        whole(width, LOW),
        whole(units, LOW),
        whole(units, LOW),
        ((1, width), F32, *all_of((1, width))),
        ((rows, width), LOW, (rows, bd), lambda j: (0, jnp.maximum(j - n1, 0))),
    ]
    return kernel(body, (n1 + 2 * n2,), ins, outs, 6 * rows * width * units)


def outer_kernel(a, b, start, count, add=None):
    rows, cols = b.shape
    bm = math.gcd(count, 384)
    skip = start // bm

    def body(a_r, b_r, *rest):
        v = tn(a_r[...], b_r[...])
        if add is not None:
            v = v + wide(rest[0][...])
        rest[-1][...] = v.astype(LOW)

    ins = [(a, (rows, bm), lambda j: (0, j + skip)), (b, *all_of(b.shape))]
    tile = ((bm, cols), lambda j: (j, 0))
    if add is not None:
        ins.append((add, *tile))
    return kernel(
        body, (count // bm,), ins, [((count, cols), LOW, *tile)], 2 * rows * count * cols
    )[0]


def last_kernel(x, gain, dh1, dx2):
    rows, width = x.shape
    br = min(rows, 128)

    def body(x_r, g_r, d_r, dx_r, o_r, dg_r):
        dv, dg = norm_back(wide(x_r[...]), g_r[...], wide(d_r[...]))
        o_r[...] = dx_r[...] + dv

        @pl.when(pl.program_id(0) == 0)
        def _():
            dg_r[...] = dg

        @pl.when(pl.program_id(0) > 0)
        def _():
            dg_r[...] += dg

    row = ((br, width), lambda i: (i, 0))
    ins = [(x, *row), (gain, *all_of(gain.shape)), (dh1, *row), (dx2, *row)]
    outs = [((rows, width), F32, *row), ((1, width), F32, *all_of((1, width)))]
    return kernel(body, (rows // br,), ins, outs)


def keys_back_kernel(own, got, cos, sin):
    def body(a_r, b_r, c_r, s_r, o_r):
        v = a_r[...] + wide(b_r[...])
        o_r[:, :HD] = turn_back(v[:, :HD], c_r[...], s_r[...]).astype(LOW)
        o_r[:, HD:] = v[:, HD:].astype(LOW)

    ins = [(v, *all_of(v.shape)) for v in (own, got, cos, sin)]
    return kernel(body, (1,), ins, [(own.shape, LOW, *all_of(own.shape))])[0]


def make_local(ny, nx, nz):
    square = ny == 2 and nx == 2
    plane = ny * nx

    def order(v, back=False):
        blk = v.shape[1] // (2 * plane)
        here = lambda c, y, x: (c * ny + y) * nx + x
        there = lambda c, y, x: (y * 2 + c) * nx + x
        place = here if back else there
        keys = [(c, y, x) for c in range(2) for y in range(ny) for x in range(nx)]
        cut = lambda j: lax.slice_in_dim(v, j * blk, (j + 1) * blk, axis=1)
        parts = {k: cut(place(*k)) for k in keys}
        bits = [(0, lax.axis_index("core"))]
        if square:
            bits += [(1, lax.axis_index("y")), (2, lax.axis_index("ctx"))]
        for pos, bit in bits:
            flip = lambda k: tuple(1 - e if i == pos else e for i, e in enumerate(k))
            parts = {k: jnp.where(bit == 0, parts[k], parts[flip(k)]) for k in keys}
        if back:
            keys = [(c, y, x) for y in range(ny) for c in range(2) for x in range(nx)]
        return jnp.concatenate([parts[k] for k in keys], axis=1)

    def row_order(wm, ws):
        blk = wm.shape[0] // plane
        c = lax.axis_index("core")
        out = jnp.zeros((2 * wm.shape[0], wm.shape[1]), wm.dtype)
        for half, w in ((0, wm), (1, ws)):
            for y in range(ny):
                for x in range(nx):
                    i = y * nx + x
                    gy, gx = y, x
                    if square:
                        gy, gx = y ^ lax.axis_index("y"), x ^ lax.axis_index("ctx")
                    at = ((gy * 2 + (c ^ half)) * nx + gx) * blk
                    piece = lax.slice_in_dim(w, i * blk, (i + 1) * blk, axis=0)
                    out = lax.dynamic_update_slice_in_dim(out, piece, at, 0)
        return out

    def local(
        layer_input,
        query_weight,
        key_weight,
        value_weight,
        output_weight,
        gate_weight,
        up_weight,
        down_weight,
        attn_in_gain,
        attn_out_gain,
        ffn_in_gain,
        ffn_out_gain,
        out_cotangent,
        segment_ids,
        live_mask,
    ):
        rows, toks, width = layer_input.shape
        blk, qw = query_weight.shape
        kw = key_weight.shape[1]
        qkv_w = qw + 2 * kw
        mid = width // 2
        half = toks // 2
        ab = (slice(0, half), slice(half, toks))
        seq = Order()

        b0, b1 = lax.axis_index("tensor") & 1, (lax.axis_index("tensor") >> 1) & 1

        def take(a, k, n):
            return lax.dynamic_slice_in_dim(a, k * n, n, 0)

        def join(a, b, bit):
            return jnp.where(
                bit == 0, jnp.concatenate([a, b], 0), jnp.concatenate([b, a], 0)
            )

        class Exchange:
            def __init__(self, part):
                self.part = part
                if nz != 4:
                    self.out = lax.psum(part, "tensor")
                    return
                n = part.shape[0] // 2
                self.keep = take(part, b0, n)
                self.got = seq.send(hop(1), take(part, 1 - b0, n))

            def two(self):
                if nz != 4:
                    return
                keep, got = seq(self.keep, self.got)
                s = wide(keep) + wide(got)
                n = s.shape[0] // 2
                self.keep = take(s, b1, n)
                self.got = seq.send(hop(2), take(s, 1 - b1, n).astype(LOW))

            def three(self):
                if nz != 4:
                    return
                keep, got = seq(self.keep, self.got)
                self.keep = (keep + wide(got)).astype(LOW)
                self.got = seq.send(hop(2), self.keep)

            def four(self):
                if nz != 4:
                    return
                keep, got = seq(self.keep, self.got)
                self.keep = join(keep, got, b1)
                self.got = seq.send(hop(1), self.keep)

            def end(self):
                if nz == 4:
                    self.out = join(self.keep, self.got, b0)
                return self.out

        gains = jnp.stack([attn_in_gain, attn_out_gain, ffn_in_gain, ffn_out_gain])
        gains = jnp.pad(gains, ((0, 12), (0, qkv_w - blk)))
        qkv_own = jnp.concatenate([query_weight, key_weight, value_weight], axis=1)
        packet = jnp.concatenate([qkv_own, gains], axis=0)
        index = lax.axis_index("ctx") * toks + jnp.arange(toks, dtype=jnp.int32)
        own_info = jnp.concatenate([segment_ids, live_mask, index[None]], axis=0)

        def near(w):
            return seq.send(to_ctx, w), seq.send(to_y, w)

        def far(got):
            h = got[0].shape[0] // 2
            wx, wy = seq(got[0], got[1])
            return seq.send(to_y, wx[:h]), seq.send(to_ctx, wy[h:])

        def whole(w):
            return lax.all_gather(w, ("y", "ctx"), axis=0, tiled=True)

        def stack(*a):
            return seq.run(lambda *v: jnp.concatenate(v, axis=0), *a)

        def positions(info):
            seg_all, live_all, index_all = info[0:1], info[1:2], info[2:3]
            seg_col, index_col = segment_ids.reshape(toks, 1), index.reshape(toks, 1)
            start = jnp.sum((seg_all < seg_col).astype(jnp.int32), axis=1)
            allowed = (
                (index_all <= index_col)
                & (seg_all == seg_col)
                & ((live_all == 1) | (index_all == index_col))
            ).astype(LOW)
            freq = jnp.exp(
                jnp.arange(HD // 2, dtype=F32) * (-2.0 * math.log(10000.0) / HD)
            )
            angle = wide(index - start)[:, None] * freq
            return allowed, jnp.cos(angle), jnp.sin(angle)

        x_raw = layer_input.reshape(toks, width)
        dy_raw = out_cotangent.reshape(toks, width)
        if square:
            n_pk = near(packet)
            n_out = near(output_weight)
            info = jnp.concatenate([own_info, seq.send(to_ctx, own_info)], axis=1)
            x = seq.run(order, x_raw)
            f_pk = far(n_pk)
            f_out = far(n_out)
            half_w = gate_weight.shape[1] // 2
            n_ga = near(gate_weight[:, :half_w])
            allowed, cos, sin = seq.run(positions, info)
            packet4 = stack(packet, *n_pk, *f_pk)
            packet_s = seq.send(to_core, packet4)
            out_m = stack(output_weight, *n_out, *f_out)
            out_s = seq.send(to_core, out_m)
        else:
            info = lax.all_gather(own_info, "ctx", axis=1, tiled=True)
            x = order(x_raw)
            allowed, cos, sin = positions(info)
            packet4, out_m = whole(packet), whole(output_weight)
            packet_s, out_s = to_core(packet4), to_core(out_m)

        def pick(a):
            n = packet.shape[0]
            return (
                jnp.concatenate([a[i * n : i * n + blk] for i in range(plane)], 0),
                jnp.concatenate(
                    [a[i * n + blk : i * n + blk + 4, :blk] for i in range(plane)], 1
                ),
            )

        (qkv_m, gm), (qkv_s, gs) = pick(packet4), pick(packet_s)
        gain = wide(jnp.concatenate([gm, gs], axis=1))
        g1, g2, g3, g4 = [gain[i : i + 1] for i in range(4)]
        h1, q, kv = seq.run(qkv_kernel, x, g1, qkv_m, qkv_s, cos, sin, qw=qw)
        if square:
            kv_got = seq.send(to_ctx, kv)
            n_gb = near(gate_weight[:, half_w:])
            n_up = near(up_weight)
            kv_all = stack(kv, kv_got)
        else:
            kv_all = lax.all_gather(kv, "ctx", axis=0, tiled=True)
        length = kv_all.shape[0]

        def attend(sl):
            return seq.run(attn_kernel, q[sl], kv_all, allowed[sl], out_m, out_s)

        o_a, log_a, part_a = attend(ab[0])
        a_a = lax.psum(part_a, "tensor")
        o_b, log_b, part_b = attend(ab[1])
        ex = Exchange(part_b)
        if square:
            n_gate = [jnp.concatenate(p, 1) for p in zip(n_ga, n_gb)]
            n_gate = seq.run(lambda *v: v, *n_gate)
            f_gate = far(n_gate)
        ex.two()
        if square:
            f_up = far(n_up)
            n_down = near(down_weight)
            gate_m = stack(gate_weight, *n_gate, *f_gate)
        else:
            gate_m = whole(gate_weight)
        gate_s = seq.send(to_core, gate_m)
        ex.three()
        up_m = stack(up_weight, *n_up, *f_up) if square else whole(up_weight)
        up_s = seq.send(to_core, up_m)
        ex.four()
        dy = seq.run(order, dy_raw)
        fw = (g2, g3, gate_m, gate_s, up_m, up_s)
        x2_a, h3_a, gate_a, up_a, hid_a = seq.run(ffn_in_kernel, a_a, x[ab[0]], *fw)
        a_b = ex.end()
        if square:
            f_down = far(n_down)
        x2_b, h3_b, gate_b, up_b, hid_b = seq.run(ffn_in_kernel, a_b, x[ab[1]], *fw)
        down_m = stack(down_weight, *n_down, *f_down) if square else whole(down_weight)
        down_s = seq.send(to_core, down_m)
        fp_a = seq.run(project_kernel, hid_a, down_m, down_s)
        f_a = lax.psum(fp_a, "tensor")
        fp_b = seq.run(project_kernel, hid_b, down_m, down_s)
        ex = Exchange(fp_b)
        qkv_g = row_order(qkv_m, qkv_s)
        g1_g = order(jnp.concatenate([g1, g1], 0), back=True)[:1]
        both = lambda a, b: jnp.concatenate([a, b], 0)
        h3, hid, o = both(h3_a, h3_b), both(hid_a, hid_b), both(o_a, o_b)
        h3, hid, o = seq.run(lambda *v: v, h3, hid, o)
        ex.two()
        ex.three()
        ex.four()
        f_b = ex.end()

        bw = (down_m, down_s, gate_m, gate_s, up_m, up_s)
        y_a, df_a, dg_a, du_a, dg4_a, part_a = seq.run(
            ffn_back_kernel, f_a, x2_a, dy[ab[0]], g4, gate_a, up_a, *bw
        )
        dh3_a = lax.psum(part_a, "tensor")
        y_b, df_b, dg_b, du_b, dg4_b, part_b = seq.run(
            ffn_back_kernel, f_b, x2_b, dy[ab[1]], g4, gate_b, up_b, *bw
        )
        ex = Exchange(part_b)
        df, dgate, dup = both(df_a, df_b), both(dg_a, dg_b), both(du_a, du_b)
        df, dgate, dup = seq.run(lambda *v: v, df, dgate, dup)

        class Scatter:
            def __init__(self, a, b):
                self.ab = a, b
                low = seq.run(outer_kernel, a, b, start=mid, count=mid)
                self.got = seq.send(to_core, low)

            def first(self):
                s = seq.run(
                    outer_kernel, *self.ab, start=0, count=mid, add=self.got
                )
                self.s = s
                if square:
                    h = blk // 2
                    self.gx = seq.send(to_ctx, s[3 * blk : 3 * blk + h])
                    self.gy = seq.send(to_y, s[3 * blk + h :])

            def second(self):
                if not square:
                    self.rest = lax.psum_scatter(
                        self.s, ("y", "ctx"), scatter_dimension=0, tiled=True
                    )
                    return
                h = blk // 2

                def sums(s, gx, gy):
                    t1 = [s[blk : blk + h], wide(s[blk + h : 2 * blk]) + wide(gy)]
                    t2 = [wide(s[2 * blk : 2 * blk + h]) + wide(gx), s[2 * blk + h : 3 * blk]]
                    return [jnp.concatenate([v.astype(LOW) for v in t], 0) for t in (t1, t2)]

                t1, t2 = seq.run(sums, self.s, self.gx, self.gy)
                self.rest = seq.send(to_ctx, t1), seq.send(to_y, t2)

            def end(self):
                if not square:
                    return wide(self.rest)
                rx, ry = self.rest
                return wide(self.s[:blk]) + wide(rx) + wide(ry)

        sd = Scatter(df, hid)
        sg = Scatter(h3, dgate)
        ex.two()
        sd.first()
        su = Scatter(h3, dup)
        ex.three()
        sg.first()
        sd.second()
        ex.four()
        su.first()
        sg.second()
        layer_output = order(both(y_a, y_b), back=True)
        dh3_b = ex.end()

        def back(dh3, x2, sl, a, logs, before):
            return seq.run(
                attn_back_kernel, dh3, x2, dy[sl], a, g3, g2, out_m, out_s,
                q[sl], kv_all, allowed[sl], logs, cos[sl], sin[sl], before=before,
            )

        dx_a, da_a, dq_a, dkv, dg23 = back(dh3_a, x2_a, ab[0], a_a, log_a, None)
        dx_b, da_b, dq_b, dkv, dg23 = back(dh3_b, x2_b, ab[1], a_b, log_b, (dkv, dg23))
        if square:
            got = seq.send(to_ctx, dkv[toks:].astype(LOW))
            own = dkv[:toks]
        else:
            got = lax.psum_scatter(
                dkv.astype(LOW), "ctx", scatter_dimension=0, tiled=True
            )
            own = jnp.zeros((toks, 2 * kw), F32)
        da, dq = both(da_a, da_b), both(dq_a, dq_b)
        da, dq = seq.run(lambda *v: v, da, dq)
        so = Scatter(da, o)
        so.first()
        dkv_low = seq.run(keys_back_kernel, own, got, cos, sin)
        dqkv = jnp.concatenate([dq, dkv_low], axis=1)
        part = seq.run(project_kernel, dqkv, qkv_g[:mid], qkv_g[mid:])
        dh1 = lax.psum(part, "tensor")
        su.second()
        sq = Scatter(h1, dqkv)
        so.second()
        sq.first()
        dx2 = seq.run(lambda v: order(v, back=True), both(dx_a, dx_b))
        sq.second()
        down_grad, gate_grad, up_grad = sd.end(), sg.end(), su.end()
        out_grad, qkv_grad = so.end(), sq.end()
        input_grad, dg1 = last_kernel(x_raw, g1_g, dh1, dx2)
        dg1 = order(jnp.concatenate([dg1, dg1], 0))[:1]
        dgain = jnp.concatenate([dg1, dg23[:2], dg4_a + dg4_b], axis=0)
        dgain = dgain[:, :mid] + to_core(dgain[:, mid:])
        if square:
            s = dgain[:, : mid // 2] + to_y(dgain[:, mid // 2 :])
            dgain = s[:, :blk] + to_ctx(s[:, blk:])
        else:
            dgain = lax.psum_scatter(
                dgain, ("y", "ctx"), scatter_dimension=1, tiled=True
            )
        return (
            layer_output.reshape(rows, toks, width),
            input_grad.reshape(rows, toks, width),
            qkv_grad[:, :qw],
            qkv_grad[:, qw : qw + kw],
            qkv_grad[:, qw + kw :],
            out_grad,
            gate_grad,
            up_grad,
            down_grad,
            dgain[0],
            dgain[1],
            dgain[2],
            dgain[3],
        )

    return local


def solution(mesh):
    dp, nx, nz = (mesh.shape[a] for a in ("dp", "ctx", "tensor"))
    fine = Mesh(
        mesh.devices.reshape(dp // 2, 2, nx, nz), ("y", "core", "ctx", "tensor")
    )
    d = ("y", "core")
    w = P(("y", "core", "ctx"), "tensor")
    g = P(("y", "core", "ctx"))
    t = P(d, "ctx", None)
    return jax.shard_map(
        make_local(dp // 2, nx, nz),
        mesh=fine,
        in_specs=(t, w, w, w, w, w, w, w, g, g, g, g, t, P(d, "ctx"), P(d, "ctx")),
        out_specs=(t, t, w, w, w, w, w, w, w, g, g, g, g),
        check_vma=False,
    )
```

time: 1050 us -> 868 us (0.83)
  Pallas kernels: 0 us -> 228 us
  matrix products: 192 us -> 0 us
  waiting for transfers between devices: 511 us -> 338 us
  other arithmetic: 147 us -> 83.1 us
  starting transfers between devices: 47.5 us -> 73.4 us
    pallas_call x0 -> x24, Pallas kernels: none -> 228 us  [kernel(): pl.pallas_call(body, grid=grid, in_specs=[pl.BlockSpec(b, m) for _, b, m...]
    dot_general x58 -> x0, matrix products: 192 us -> none  [the longest x18 63.9 us: dot(): return jnp.dot(a, b, preferred_element_type=F32)]
    psum x4, waiting for transfers between devices: 292 us -> 112 us  [the longest x1 65.1 us: local(): dh1 = lax.psum(part, 'tensor')]
    ppermute x0 -> x12, waiting for transfers between devices: none -> 124 us  [hop(): return lambda a: lax.ppermute(a, 'tensor', [(k, k ^ bit) for k in range(4)])]
    ppermute x19 -> x22, waiting for transfers between devices: 103 us -> 26.3 us  [to_y(): return lax.ppermute(a, 'y', SWAP)]
    ppermute x22 -> x25, waiting for transfers between devices: 117 us -> 68.3 us  [to_ctx(): return lax.ppermute(a, 'ctx', SWAP)]
    reduce_sum x13 -> x1, other arithmetic: 30.7 us -> 0.36 us  [positions(): start = jnp.sum((seg_all < seg_col).astype(jnp.int32), axis=1)]
    ppermute x0 -> x12, starting transfers between devices: none -> 20.6 us  [hop(): return lambda a: lax.ppermute(a, 'tensor', [(k, k ^ bit) for k in range(4)])]
  transfers between devices with their start and end apart: 55 -> 74, of which waited for: 21 -> 31; matrix products, arithmetic and copies ran while one was open for 36% -> 19% of each run, Pallas kernels for 0% -> 17%
where the time goes in v2:
time: 868 us; the launch traced here: 861 us
  waiting for transfers between devices  338 us (39%)
  Pallas kernels  228 us (26%)
  local copies, waits for them, and re-layouts  123 us (14%)
  other arithmetic  83.1 us (10%)
  starting transfers between devices  73.4 us (8%)
  between operations  15 us (2%)
    pallas_call x24, Pallas kernels, kernel(): pl.pallas_call(body, grid=grid, in_specs=[pl.BlockSpec(b, m) for _, b, m...  228 us
    ppermute x12, waiting for transfers between devices, hop(): return lambda a: lax.ppermute(a, 'tensor', [(k, k ^ bit) for k in range(4)])  124 us
    ppermute x25, waiting for transfers between devices, to_ctx(): return lax.ppermute(a, 'ctx', SWAP)  68.3 us
    psum x1, waiting for transfers between devices, local(): dh1 = lax.psum(part, 'tensor')  65.1 us
    unnamed x130, local copies, waits for them, and re-layouts  34.1 us
    ppermute x25, starting transfers between devices, to_ctx(): return lax.ppermute(a, 'ctx', SWAP)  30.6 us
    ppermute x22, waiting for transfers between devices, to_y(): return lax.ppermute(a, 'y', SWAP)  26.3 us
    psum x1, waiting for transfers between devices, local(): a_a = lax.psum(part_a, 'tensor')  25.1 us
  transfers between devices with their start and end apart: 74, of which 31 were waited for; matrix products, arithmetic and copies ran while one was open for 19% of the time, Pallas kernels for 17%

profile of v2, /device:TPU:0, one launch (start us, length us, event | category | flops | bytes accessed | tf_op | source)
XLA Modules:
  0.0 860.9 jit_solution(3323601213471795327)
XLA Ops:
  98.7 9.0 %collective-permute-done.10 = bf16[512,512]{1,0:T(8,128)(2,1)S(1)} collective-permute-done((bf16[512,512]{1,0:T(8,128)(2,1)}, bf16[512,512]{1,0:T(8,128)(2,1)S(1)}, u32[]{:S(2)}, u32[]{:S(2)}) %collective-permute-start.10) | collective-permute-done | bytes 524320 | tf_op jit(solution)/shard_map/ppermute | solution.py:48
  143.1 11.5 %collective-permute-done.19 = bf16[288,2304]{1,0:T(8,128)(2,1)S(1)} collective-permute-done((bf16[288,2304]{1,0:T(8,128)(2,1)}, bf16[288,2304]{1,0:T(8,128)(2,1)S(1)}, u32[]{:S(2)}, u32[]{:S(2)}) %collective-permute-start.19) | collective-permute-done | bytes 1327136 | tf_op jit(solution)/shard_map/ppermute | solution.py:52
  154.6 9.9 %collective-permute-done.18 = bf16[288,2304]{1,0:T(8,128)(2,1)S(1)} collective-permute-done((bf16[288,2304]{1,0:T(8,128)(2,1)}, bf16[288,2304]{1,0:T(8,128)(2,1)S(1)}, u32[]{:S(2)}, u32[]{:S(2)}) %collective-permute-start.18) | collective-permute-done | bytes 1327136 | tf_op jit(solution)/shard_map/ppermute | solution.py:48
  166.9 11.9 %collective-permute-done.17 = bf16[144,2304]{1,0:T(8,128)(2,1)S(1)} collective-permute-done((bf16[144,2304]{1,0:T(8,128)(2,1)S(1)}, bf16[144,2304]{1,0:T(8,128)(2,1)S(1)}, u32[]{:S(2)}, u32[]{:S(2)}) %collective-permute-start.17) | collective-permute-done | bytes 663584 | tf_op jit(solution)/shard_map/ppermute | solution.py:48
  184.2 8.4 collective-permute-done.23
  205.4 22.5 %collective-permute-done.26 = bf16[64,2304]{1,0:T(8,128)(2,1)} collective-permute-done((bf16[64,2304]{1,0:T(8,128)(2,1)S(1)}, bf16[64,2304]{1,0:T(8,128)(2,1)}, u32[]{:S(2)}, u32[]{:S(2)}) %collective-permute-start.26) | collective-permute-done | bytes 294944 | tf_op jit(solution)/shard_map/ppermute | solution.py:60
  241.3 25.1 %all-reduce.6.cloned.1.call-done.a_r.refs_3_ = bf16[256,2304]{1,0:T(8,128)(2,1)} async-done(((bf16[256,2304]{1,0:T(8,128)(2,1)}), bf16[256,2304]{1,0:T(8,128)(2,1)}) %all-reduce.6.cloned.1.call-update) | async-done | bytes 1179664 | tf_op jit(solution)/shard_map/psum | solution.py:636
  266.5 15.5 %shard_map.249 = (f32[256,2304]{1,0:T(8,128)}, bf16[256,2304]{1,0:T(8,128)(2,1)}, f32[256,2304]{1,0:T(8,128)}, f32[256,2304]{1,0:T(8,128)}, bf16[256,2304]{1,0:T(8,128)(2,1)}) custom-call(bf16[256,2304]{1,0:T(8,128)(2,1)} %all-reduce.6.cloned.1.call-done.a_r.refs_3_, bf16[256,2304]{1,0:T(8,128)(2,1)} %get-tuple-element.412.x_r, ...), custom_call_target="tpu_custom_call" | custom-call | flops 5435817984 | bytes 33048576 | tf_op jit(solution)/shard_map/pallas_call | solution.py:111
  288.6 15.6 %shard_map.250 = (f32[256,2304]{1,0:T(8,128)}, bf16[256,2304]{1,0:T(8,128)(2,1)}, f32[256,2304]{1,0:T(8,128)}, f32[256,2304]{1,0:T(8,128)}, bf16[256,2304]{1,0:T(8,128)(2,1)}) custom-call(bf16[256,2304]{1,0:T(8,128)(2,1)} %maximum_select_fusion.a_r.refs_3_, bf16[256,2304]{1,0:T(8,128)(2,1)} %get-tuple-element.429.x_r, ...), custom_call_target="tpu_custom_call" | custom-call | flops 5435817984 | bytes 33048576 | tf_op jit(solution)/shard_map/pallas_call | solution.py:111
  318.8 9.5 %shard_map.251 = bf16[256,2304]{1,0:T(8,128)(2,1)} custom-call(bf16[256,2304]{1,0:T(8,128)(2,1)} %get-tuple-element.447.u_r, bf16[1152,2304]{1,0:T(8,128)(2,1)} %copy-done, bf16[1152,2304]{1,0:T(8,128)(2,1)} %collective-permute-done.32.s_r.ds_r), custom_call_target="tpu_custom_call" | custom-call | flops 2717908992 | bytes 12976128 | tf_op jit(solution)/shard_map/pallas_call | solution.py:111
  328.3 9.5 %shard_map.252 = bf16[256,2304]{1,0:T(8,128)(2,1)} custom-call(bf16[256,2304]{1,0:T(8,128)(2,1)} %get-tuple-element.450.u_r, bf16[1152,2304]{1,0:T(8,128)(2,1)} %copy-done, bf16[1152,2304]{1,0:T(8,128)(2,1)} %collective-permute-done.32.s_r.ds_r), custom_call_target="tpu_custom_call" | custom-call | flops 2717908992 | bytes 12976128 | tf_op jit(solution)/shard_map/pallas_call | solution.py:111
  346.0 20.7 %collective-permute-done.33 = bf16[128,2304]{1,0:T(8,128)(2,1)} collective-permute-done((bf16[128,2304]{1,0:T(8,128)(2,1)}, bf16[128,2304]{1,0:T(8,128)(2,1)}, u32[]{:S(2)}, u32[]{:S(2)}) %collective-permute-start.33) | collective-permute-done | bytes 589856 | tf_op jit(solution)/shard_map/ppermute | solution.py:60
  371.3 17.0 %collective-permute-done.34 = bf16[64,2304]{1,0:T(8,128)(2,1)S(1)} collective-permute-done((bf16[64,2304]{1,0:T(8,128)(2,1)S(1)}, bf16[64,2304]{1,0:T(8,128)(2,1)S(1)}, u32[]{:S(2)}, u32[]{:S(2)}) %collective-permute-start.34) | collective-permute-done | bytes 294944 | tf_op jit(solution)/shard_map/ppermute | solution.py:60
  390.1 28.3 %collective-permute-done.35 = bf16[64,2304]{1,0:T(8,128)(2,1)S(1)} collective-permute-done((bf16[64,2304]{1,0:T(8,128)(2,1)S(1)}, bf16[64,2304]{1,0:T(8,128)(2,1)S(1)}, u32[]{:S(2)}, u32[]{:S(2)}) %collective-permute-start.35) | collective-permute-done | bytes 294944 | tf_op jit(solution)/shard_map/ppermute | solution.py:60
  422.9 26.4 %shard_map.253 = (bf16[256,2304]{1,0:T(8,128)(2,1)}, bf16[256,2304]{1,0:T(8,128)(2,1)}, bf16[256,2304]{1,0:T(8,128)(2,1)}, bf16[256,2304]{1,0:T(8,128)(2,1)}, f3...) custom-call(bf16[256,2304]{1,0:T(8,128)(2,1)} %all-reduce.8.cloned.1.call-done.f_r, ...), custom_call_target="tpu_custom_call" | custom-call | flops 8153726976 | bytes 47204352 | tf_op jit(solution)/shard_map/pallas_call | solution.py:111
  450.5 26.6 %shard_map.254 = (bf16[256,2304]{1,0:T(8,128)(2,1)}, bf16[256,2304]{1,0:T(8,128)(2,1)}, bf16[256,2304]{1,0:T(8,128)(2,1)}, bf16[256,2304]{1,0:T(8,128)(2,1)}, f3...) custom-call(bf16[256,2304]{1,0:T(8,128)(2,1)} %maximum_select_fusion.1.f_r, f32[256,2304]{1,0:T(8,128)} %get-tuple-element.563.x2_r.refs_1_, ...), custom_call_target="tpu_custom_call" | custom-call | flops 8153726976 | bytes 47204352 | tf_op jit(solution)/shard_map/pallas_call | solution.py:111
  502.1 12.7 %collective-permute-done.37 = bf16[128,2304]{1,0:T(8,128)(2,1)S(1)} collective-permute-done((bf16[128,2304]{1,0:T(8,128)(2,1)S(1)}, bf16[128,2304]{1,0:T(8,128)(2,1)S(1)}, u32[]{:S(2)}, u32[]{:S(2)}) %collective-permute-start.37) | collective-permute-done | bytes 589856 | tf_op jit(solution)/shard_map/ppermute | solution.py:60
  563.0 20.3 %collective-permute-done.47 = bf16[128,2304]{1,0:T(8,128)(2,1)} collective-permute-done((bf16[128,2304]{1,0:T(8,128)(2,1)S(1)}, bf16[128,2304]{1,0:T(8,128)(2,1)}, u32[]{:S(2)}, u32[]{:S(2)}) %collective-permute-start.47) | collective-permute-done | bytes 589856 | tf_op jit(solution)/shard_map/ppermute | solution.py:60
  586.0 8.7 %shard_map.260 = bf16[1152,2304]{1,0:T(8,128)(2,1)} custom-call(bf16[512,2304]{1,0:T(8,128)(2,1)} %pad_maximum_fusion.3.a_r, bf16[512,2304]{1,0:T(8,128)(2,1)} %pad_maximum_fusion.7.b_r, bf16[1152,2304]{1,0:T(8,128)(2,1)} %collective-permute-done.46.rest_0_), custom_call_target="tpu_custom_call" | custom-call | flops 2717908992 | bytes 15335424 | tf_op jit(solution)/shard_map/pallas_call | solution.py:111
  599.9 17.7 %all-reduce.10.cloned.1.call-done.refs_0_ = bf16[256,2304]{1,0:T(8,128)(2,1)} async-done(((bf16[256,2304]{1,0:T(8,128)(2,1)}), bf16[256,2304]{1,0:T(8,128)(2,1)}) %all-reduce.10.cloned.1.call-update) | async-done | bytes 1179664 | tf_op jit(solution)/shard_map/psum | solution.py:682
  617.6 11.1 %shard_map.261 = (f32[256,2304]{1,0:T(8,128)}, bf16[256,2304]{1,0:T(8,128)(2,1)}, bf16[256,512]{1,0:T(8,128)(2,1)}, f32[1024,512]{1,0:T(8,128)}, f32[8,2304]{1,0:T(8,128)}) custom-call(bf16[256,2304]{1,0:T(8,128)(2,1)} %all-reduce.10.cloned.1.call-done.refs_0_, f32[256,2304]{1,0:T(8,128)} %get-tuple-element.544.x2_r.refs_1_, ...), custom_call_target="tpu_custom_call" | custom-call | flops 1946157056 | bytes 16607232 | tf_op jit(solution)/shard_map/pallas_call | solution.py:111
  628.8 12.0 %shard_map.262 = (f32[256,2304]{1,0:T(8,128)}, bf16[256,2304]{1,0:T(8,128)(2,1)}, bf16[256,512]{1,0:T(8,128)(2,1)}, f32[1024,512]{1,0:T(8,128)}, f32[8,2304]{1,0:T(8,128)}) custom-call(bf16[256,2304]{1,0:T(8,128)(2,1)} %maximum_select_fusion.2.refs_0_, f32[256,2304]{1,0:T(8,128)} %get-tuple-element.563.x2_r.refs_1_, ...), custom_call_target="tpu_custom_call" | custom-call | flops 1946157056 | bytes 18778112 | tf_op jit(solution)/shard_map/pallas_call | solution.py:111
  699.0 10.0 %collective-permute-done.65 = bf16[288,2304]{1,0:T(8,128)(2,1)} collective-permute-done((bf16[288,2304]{1,0:T(8,128)(2,1)}, bf16[288,2304]{1,0:T(8,128)(2,1)}, u32[]{:S(2)}, u32[]{:S(2)}) %collective-permute-start.65) | collective-permute-done | bytes 1327136 | tf_op jit(solution)/shard_map/ppermute | solution.py:48
  744.5 65.1 %all-reduce.12.cloned.1.call-done.d_r = bf16[512,2304]{1,0:T(8,128)(2,1)} async-done(((bf16[512,2304]{1,0:T(8,128)(2,1)}), bf16[512,2304]{1,0:T(8,128)(2,1)}) %all-reduce.12.cloned.1.call-update) | async-done | bytes 2359312 | tf_op jit(solution)/shard_map/psum | solution.py:765
  (446 shorter events, 420.7 us)
Async XLA Ops:
  7.2 259.3 %all-reduce.6.cloned.1.call-start = ((), (), s32[]{:S(2)}) async-start(), calls=%async_computation | async-start | bytes 2359296 | tf_op jit(solution)/shard_map/psum | solution.py:636
  69.1 39.9 %collective-permute-start.11 = (bf16[1152,512]{1,0:T(8,128)(2,1)}, bf16[1152,512]{1,0:T(8,128)(2,1)}, u32[]{:S(2)}, u32[]{:S(2)}) collective-permute-start(bf16[1152,512]{1,0:T(8,128)(2,1)} %constant_dynamic-update-slice_fusion.5.wm_r.refs_6_), channel_id=1, source_target_pairs={{0,8},{8,0},{1,9},{9,1},{2,10},{10,2},{3,11},{11,3},{4,12},{12,4},... | collective-permute-start | bytes 3538952 | tf_op jit(solution)/shard_map/ppermute | solution.py:56
  109.1 45.6 %collective-permute-start.19 = (bf16[288,2304]{1,0:T(8,128)(2,1)}, bf16[288,2304]{1,0:T(8,128)(2,1)S(1)}, u32[]{:S(2)}, u32[]{:S(2)}) collective-permute-start(bf16[288,2304]{1,0:T(8,128)(2,1)} %param.21), channel_id=1, source_target_pairs={{0,16},{16,0},{1,17},{17,1},{2,18},{18,2},{3,19},{19,3},{4,20},{20... | collective-permute-start | bytes 3981320 | tf_op jit(solution)/shard_map/ppermute | solution.py:52
  122.6 42.0 %collective-permute-start.18 = (bf16[288,2304]{1,0:T(8,128)(2,1)}, bf16[288,2304]{1,0:T(8,128)(2,1)S(1)}, u32[]{:S(2)}, u32[]{:S(2)}) collective-permute-start(bf16[288,2304]{1,0:T(8,128)(2,1)} %param.21), channel_id=1, source_target_pairs={{0,4},{4,0},{1,5},{5,1},{2,6},{6,2},{3,7},{7,3},{8,12},{12,8},{9,1... | collective-permute-start | bytes 3981320 | tf_op jit(solution)/shard_map/ppermute | solution.py:48
  137.7 41.1 %collective-permute-start.16 = (bf16[144,2304]{1,0:T(8,128)(2,1)S(1)}, bf16[144,2304]{1,0:T(8,128)(2,1)S(1)}, u32[]{:S(2)}, u32[]{:S(2)}) collective-permute-start(bf16[144,2304]{1,0:T(8,128)(2,1)S(1)} %slice.499), channel_id=1, source_target_pairs={{0,16},{16,0},{1,17},{17,1},{2,18},{18,2},{3,19},{19,3},{4,20},{20... | collective-permute-start | bytes 1990664 | tf_op jit(solution)/shard_map/ppermute | solution.py:52
  138.3 40.5 %collective-permute-start.17 = (bf16[144,2304]{1,0:T(8,128)(2,1)S(1)}, bf16[144,2304]{1,0:T(8,128)(2,1)S(1)}, u32[]{:S(2)}, u32[]{:S(2)}) collective-permute-start(bf16[144,2304]{1,0:T(8,128)(2,1)S(1)} %slice.500), channel_id=1, source_target_pairs={{0,4},{4,0},{1,5},{5,1},{2,6},{6,2},{3,7},{7,3},{8,12},{12,8},{9,1... | collective-permute-start | bytes 1990664 | tf_op jit(solution)/shard_map/ppermute | solution.py:48
  140.4 43.7 %collective-permute-start.24 = (bf16[64,2304]{1,0:T(8,128)(2,1)S(1)}, bf16[64,2304]{1,0:T(8,128)(2,1)S(1)}, u32[]{:S(2)}, u32[]{:S(2)}) collective-permute-start(bf16[64,2304]{1,0:T(8,128)(2,1)S(1)} %dynamic-slice_convert_fusion.2), channel_id=1, source_target_pairs={{0,2},{1,3},{2,0},{3,1},{4,6},{5,7},{6,4},{7,5},{8,10},{9,11},{10,... | collective-permute-start | bytes 884744 | tf_op jit(solution)/shard_map/ppermute | solution.py:60
  184.1 82.3 %collective-permute-start.21 = (bf16[1152,2304]{1,0:T(8,128)(2,1)}, bf16[1152,2304]{1,0:T(8,128)(2,1)}, u32[]{:S(2)}, u32[]{:S(2)}) collective-permute-start(bf16[1152,2304]{1,0:T(8,128)(2,1)} %constant_dynamic-update-slice_fusion.12.gm_r), channel_id=1, source_target_pairs={{0,8},{8,0},{1,9},{9,1},{2,10},{10,2},{3,11},{11,3},{4,12},{12,4},... | collective-permute-start | bytes 15925256 | tf_op jit(solution)/shard_map/ppermute | solution.py:56
  199.3 67.1 %collective-permute-start.25 = (bf16[1152,2304]{1,0:T(8,128)(2,1)}, bf16[1152,2304]{1,0:T(8,128)(2,1)}, u32[]{:S(2)}, u32[]{:S(2)}) collective-permute-start(bf16[1152,2304]{1,0:T(8,128)(2,1)} %constant_dynamic-update-slice_fusion.17.um_r), channel_id=1, source_target_pairs={{0,8},{8,0},{1,9},{9,1},{2,10},{10,2},{3,11},{11,3},{4,12},{12,4},... | collective-permute-start | bytes 15925256 | tf_op jit(solution)/shard_map/ppermute | solution.py:56
  203.5 219.4 %all-reduce.8.cloned.1.call-start = ((), (), s32[]{:S(2)}) async-start(), calls=%async_computation.1 | async-start | bytes 2359296 | tf_op jit(solution)/shard_map/psum | solution.py:665
  203.6 78.4 %collective-permute-start.28 = (bf16[288,2304]{1,0:T(8,128)(2,1)}, bf16[288,2304]{1,0:T(8,128)(2,1)}, u32[]{:S(2)}, u32[]{:S(2)}) collective-permute-start(bf16[288,2304]{1,0:T(8,128)(2,1)} %param.22), channel_id=1, source_target_pairs={{0,16},{16,0},{1,17},{17,1},{2,18},{18,2},{3,19},{19,3},{4,20},{20... | collective-permute-start | bytes 3981320 | tf_op jit(solution)/shard_map/ppermute | solution.py:52
  204.1 77.9 %collective-permute-start.27 = (bf16[288,2304]{1,0:T(8,128)(2,1)}, bf16[288,2304]{1,0:T(8,128)(2,1)}, u32[]{:S(2)}, u32[]{:S(2)}) collective-permute-start(bf16[288,2304]{1,0:T(8,128)(2,1)} %param.22), channel_id=1, source_target_pairs={{0,4},{4,0},{1,5},{5,1},{2,6},{6,2},{3,7},{7,3},{8,12},{12,8},{9,1... | collective-permute-start | bytes 3981320 | tf_op jit(solution)/shard_map/ppermute | solution.py:48
  229.1 57.0 %collective-permute-start.31 = (bf16[128,2304]{1,0:T(8,128)(2,1)S(1)}, bf16[128,2304]{1,0:T(8,128)(2,1)}, u32[]{:S(2)}, u32[]{:S(2)}) collective-permute-start(bf16[128,2304]{1,0:T(8,128)(2,1)S(1)} %maximum_select_fusion.3), channel_id=1, source_target_pairs={{0,1},{1,0},{2,3},{3,2},{4,5},{5,4},{6,7},{7,6},{8,9},{9,8},{10,11... | collective-permute-start | bytes 1769480 | tf_op jit(solution)/shard_map/ppermute | solution.py:60
  346.0 271.6 %all-reduce.10.cloned.1.call-start = ((), (), s32[]{:S(2)}) async-start(), calls=%async_computation.2 | async-start | bytes 2359296 | tf_op jit(solution)/shard_map/psum | solution.py:682
  499.1 41.8 %collective-permute-start.40 = (bf16[1152,2304]{1,0:T(8,128)(2,1)}, bf16[1152,2304]{1,0:T(8,128)(2,1)}, u32[]{:S(2)}, u32[]{:S(2)}) collective-permute-start(bf16[1152,2304]{1,0:T(8,128)(2,1)} %shard_map.256), channel_id=1, source_target_pairs={{0,8},{8,0},{1,9},{9,1},{2,10},{10,2},{3,11},{11,3},{4,12},{12,4},... | collective-permute-start | bytes 15925256 | tf_op jit(solution)/shard_map/ppermute | solution.py:56
  539.3 46.7 %collective-permute-start.46 = (bf16[1152,2304]{1,0:T(8,128)(2,1)}, bf16[1152,2304]{1,0:T(8,128)(2,1)}, u32[]{:S(2)}, u32[]{:S(2)}) collective-permute-start(bf16[1152,2304]{1,0:T(8,128)(2,1)} %shard_map.258), channel_id=1, source_target_pairs={{0,8},{8,0},{1,9},{9,1},{2,10},{10,2},{3,11},{11,3},{4,12},{12,4},... | collective-permute-start | bytes 15925256 | tf_op jit(solution)/shard_map/ppermute | solution.py:56
  561.4 248.2 %all-reduce.12.cloned.1.call-start = ((), (), s32[]{:S(2)}) async-start(), calls=%async_computation.3 | async-start | bytes 4718592 | tf_op jit(solution)/shard_map/psum | solution.py:765
  657.3 41.7 %collective-permute-start.66 = (bf16[288,2304]{1,0:T(8,128)(2,1)}, bf16[288,2304]{1,0:T(8,128)(2,1)}, u32[]{:S(2)}, u32[]{:S(2)}) collective-permute-start(bf16[288,2304]{1,0:T(8,128)(2,1)} %pad_maximum_fusion.11), channel_id=1, source_target_pairs={{0,16},{16,0},{1,17},{17,1},{2,18},{18,2},{3,19},{19,3},{4,20},{20... | collective-permute-start | bytes 3981320 | tf_op jit(solution)/shard_map/ppermute | solution.py:52
  659.0 50.0 %collective-permute-start.65 = (bf16[288,2304]{1,0:T(8,128)(2,1)}, bf16[288,2304]{1,0:T(8,128)(2,1)}, u32[]{:S(2)}, u32[]{:S(2)}) collective-permute-start(bf16[288,2304]{1,0:T(8,128)(2,1)} %pad_maximum_fusion.12), channel_id=1, source_target_pairs={{0,4},{4,0},{1,5},{5,1},{2,6},{6,2},{3,7},{7,3},{8,12},{12,8},{9,1... | collective-permute-start | bytes 3981320 | tf_op jit(solution)/shard_map/ppermute | solution.py:48
  719.6 100.2 %collective-permute-start.62 = (bf16[288,2304]{1,0:T(8,128)(2,1)}, bf16[288,2304]{1,0:T(8,128)(2,1)}, u32[]{:S(2)}, u32[]{:S(2)}) collective-permute-start(bf16[288,2304]{1,0:T(8,128)(2,1)} %pad_maximum_fusion.13), channel_id=1, source_target_pairs={{0,16},{16,0},{1,17},{17,1},{2,18},{18,2},{3,19},{19,3},{4,20},{20... | collective-permute-start | bytes 3981320 | tf_op jit(solution)/shard_map/ppermute | solution.py:52
  720.2 101.2 %collective-permute-start.61 = (bf16[288,2304]{1,0:T(8,128)(2,1)}, bf16[288,2304]{1,0:T(8,128)(2,1)}, u32[]{:S(2)}, u32[]{:S(2)}) collective-permute-start(bf16[288,2304]{1,0:T(8,128)(2,1)} %pad_maximum_fusion.14), channel_id=1, source_target_pairs={{0,4},{4,0},{1,5},{5,1},{2,6},{6,2},{3,7},{7,3},{8,12},{12,8},{9,1... | collective-permute-start | bytes 3981320 | tf_op jit(solution)/shard_map/ppermute | solution.py:48
  721.3 117.9 %collective-permute-start.64 = (bf16[288,2304]{1,0:T(8,128)(2,1)}, bf16[288,2304]{1,0:T(8,128)(2,1)}, u32[]{:S(2)}, u32[]{:S(2)}) collective-permute-start(bf16[288,2304]{1,0:T(8,128)(2,1)} %pad_maximum_fusion.15), channel_id=1, source_target_pairs={{0,16},{16,0},{1,17},{17,1},{2,18},{18,2},{3,19},{19,3},{4,20},{20... | collective-permute-start | bytes 3981320 | tf_op jit(solution)/shard_map/ppermute | solution.py:52
  722.2 116.9 %collective-permute-start.63 = (bf16[288,2304]{1,0:T(8,128)(2,1)}, bf16[288,2304]{1,0:T(8,128)(2,1)}, u32[]{:S(2)}, u32[]{:S(2)}) collective-permute-start(bf16[288,2304]{1,0:T(8,128)(2,1)} %pad_maximum_fusion.16), channel_id=1, source_target_pairs={{0,4},{4,0},{1,5},{5,1},{2,6},{6,2},{3,7},{7,3},{8,12},{12,8},{9,1... | collective-permute-start | bytes 3981320 | tf_op jit(solution)/shard_map/ppermute | solution.py:48
  726.3 100.8 %collective-permute-start.60 = (bf16[288,512]{1,0:T(8,128)(2,1)}, bf16[288,512]{1,0:T(8,128)(2,1)}, u32[]{:S(2)}, u32[]{:S(2)}) collective-permute-start(bf16[288,512]{1,0:T(8,128)(2,1)} %pad_maximum_fusion.24), channel_id=1, source_target_pairs={{0,16},{16,0},{1,17},{17,1},{2,18},{18,2},{3,19},{19,3},{4,20},{20... | collective-permute-start | bytes 884744 | tf_op jit(solution)/shard_map/ppermute | solution.py:52
  (104 other events, 1520.6 us)
Sparse Core Ops, SparseCore 0:
  203.6 62.7 all-reduce.5
  346.1 76.7 all-reduce.7
  561.5 56.0 all-reduce.9
  716.2 93.3 all-reduce.11

commit v3 on v2

v3 whole, which is shorter than its diff:
```python
import math

import jax
import jax.numpy as jnp
from jax import lax
from jax.experimental import pallas as pl
from jax.experimental.pallas import tpu as pltpu
from jax.sharding import Mesh
from jax.sharding import PartitionSpec as P

HD = 256
NORM_EPSILON = 1e-06
SOFT_CAP = 50.0
MASKED_SCORE = -1e30
SWAP = [(0, 1), (1, 0)]
LOW = jnp.bfloat16
F32 = jnp.float32
VMEM_MB = 56
NO_COST = pl.CostEstimate(flops=0, bytes_accessed=0, transcendentals=0)
LONG = pl.CostEstimate(flops=10**12, bytes_accessed=0, transcendentals=0)


def wide(a):
    return a.astype(F32)


def after(value, *deps):
    return lax.optimization_barrier((value,) + deps)[0]


class Order:
    def __init__(self):
        self.last = ()

    def __call__(self, *values):
        return after(values, *self.last) if self.last else values

    def run(self, fn, *values, **kw):
        out = fn(*self(*values), **kw)
        self.last = (out,)
        return out

    def send(self, move, value):
        (value,) = self(value)
        self.last = (value,)
        return move(value)


def to_ctx(a):
    return lax.ppermute(a, "ctx", SWAP)


def to_y(a):
    return lax.ppermute(a, "y", SWAP)


def to_core(a):
    return lax.ppermute(a, "core", SWAP)


def nn(a, b):
    return jnp.dot(a, b, preferred_element_type=F32)


def nt(a, b):
    return lax.dot_general(a, b, (((1,), (1,)), ((), ())), preferred_element_type=F32)


def tn(a, b):
    return lax.dot_general(a, b, (((0,), (0,)), ((), ())), preferred_element_type=F32)


def norm_factor(v):
    return lax.rsqrt(jnp.mean(v * v, axis=-1, keepdims=True) + NORM_EPSILON)


def over_rows(rows, step, carry=None, block=64):
    block = math.gcd(rows, block)
    at = lambda i: pl.ds(pl.multiple_of(i * block, block), block)
    return lax.fori_loop(0, rows // block, lambda i, c: step(at(i), c), carry)


def fold(v):
    return sum(v[i : i + 8] for i in range(0, v.shape[0], 8))


def norm_back_rows(v, gain, grad):
    r = norm_factor(v)
    w = (1.0 + gain) * grad
    vr = v * r
    dv = r * (w - vr * jnp.mean(vr * w, axis=-1, keepdims=True))
    return dv, fold(grad * vr)


def gelu_parts(u):
    k = math.sqrt(2.0 / math.pi)
    th = jnp.tanh(k * (u + 0.044715 * u * u * u))
    g = 0.5 * u * (1.0 + th)
    dg = 0.5 * (1.0 + th) + 0.5 * u * (1.0 - th * th) * k * (1.0 + 3 * 0.044715 * u * u)
    return g, dg


def turn(v, c, s):
    h = HD // 2
    a, b = v[:, :h], v[:, h:]
    return jnp.concatenate([a * c - b * s, b * c + a * s], axis=1)


def turn_back(v, c, s):
    h = HD // 2
    a, b = v[:, :h], v[:, h:]
    return jnp.concatenate([a * c + b * s, b * c - a * s], axis=1)


def spec(block, index, mode=None):
    return pl.BlockSpec(block, index, pipeline_mode=mode)


def kernel(body, grid, ins, outs, scratch=(), cost=NO_COST):
    return pl.pallas_call(
        body,
        grid=grid,
        in_specs=[spec(*e[1:]) for e in ins],
        out_specs=[spec(*e[2:]) for e in outs],
        out_shape=[jax.ShapeDtypeStruct(*e[:2]) for e in outs],
        scratch_shapes=list(scratch),
        cost_estimate=cost,
        compiler_params=pltpu.CompilerParams(vmem_limit_bytes=VMEM_MB * 2**20),
    )(*[e[0] for e in ins])


def all_of(shape):
    return tuple(shape), lambda *i: (0,) * len(shape), pl.Buffered(1)


def stack_kernel(*pieces, outs, plan, cost=NO_COST):
    sets, n = len(plan), len(pieces)
    widths = [pieces[p[0][0]].shape[1] for p in plan]
    bc = math.gcd(*widths, 768)
    first = [sum(widths[:i]) // bc for i in range(sets + 1)]

    def body(*refs):
        for i, copies in enumerate(plan):

            @pl.when((pl.program_id(0) >= first[i]) & (pl.program_id(0) < first[i + 1]))
            def _(copies=copies):
                for p, o, r0, r, at in copies:
                    refs[n + o][at : at + r, :] = refs[p][r0 : r0 + r, :]

    ins = []
    for i, copies in enumerate(plan):
        lo, count = first[i], first[i + 1] - first[i]
        for p in sorted({e[0] for e in copies}):
            tile = (pieces[p].shape[0], bc)
            ins.append((p, tile, lambda j, lo=lo, c=count: (0, jnp.clip(j - lo, 0, c - 1))))
    ins = [(pieces[p], t, m) for p, t, m in sorted(ins, key=lambda e: e[0])]
    tile = lambda r: ((r, bc), lambda j: (0, j))
    outs = [((r, sum(widths)), LOW, *tile(r)) for r in outs]
    return kernel(body, (first[-1],), ins, outs, cost=cost)


def first_kernel(x, r, cos, sin, *pieces, plan, blk, qw, kw):
    toks, width = x.shape
    wide_w = pieces[0].shape[1]
    cols = qw + 2 * kw
    devices = width // blk
    lanes = -(-blk // 128) * 128
    scale = 1.0 / math.sqrt(HD)
    n = len(pieces)

    def body(x_r, r_r, c_r, s_r, *refs):
        piece_h = refs[:n]
        h_h, q_r, kv_r, g_r, w_h, o_h = refs[n : n + 6]
        h_r, w_r, raw_g_r, sems = refs[n + 6 :]
        c = Copies(sems)
        for k, (p, r0, rows, at, gain_at) in enumerate(plan):
            if at is None:
                src = piece_h[p].at[pl.ds(r0, rows), pl.ds(0, lanes)]
                c.start(("g", k), src, raw_g_r.at[pl.ds(gain_at, rows)])
        for k, (p, r0, rows, at, gain_at) in enumerate(plan):
            if at is not None:
                c.start(("w", k), piece_h[p].at[pl.ds(r0, rows)], w_r.at[pl.ds(at, rows)])
        c.wait(*[k for k in c.known if k[0] == "g"])
        rows16 = raw_g_r[...]
        gains = [rows16[d * 16 : d * 16 + 8, :blk] for d in range(devices)]
        gains = wide(jnp.concatenate(gains, axis=1))
        g_r[...] = gains
        g1 = 1.0 + gains[0:1]

        def normed(at, _):
            h_r[at, :] = (wide(x_r[at, :]) * r_r[at, 0:1] * g1).astype(LOW)

        over_rows(toks, normed)
        c.start("h", h_r, h_h)
        c.wait(*[k for k in c.known if k[0] == "w"])
        c.start("qkv", w_r.at[:, pl.ds(0, cols)], w_h)
        c.start("out", w_r.at[:, pl.ds(cols, wide_w - cols)], o_h)
        raw = nn(h_r[...], w_r[:, :cols])
        co, si = c_r[...], s_r[...]
        for j in range(qw // HD):
            cut = slice(j * HD, (j + 1) * HD)
            q_r[:, cut] = (turn(raw[:, cut], co, si) * scale).astype(LOW)
        for j in range(kw // HD):
            cut = slice(j * HD, (j + 1) * HD)
            k = turn(raw[:, qw + j * HD : qw + (j + 1) * HD], co, si)
            kv_r[:, cut] = k.astype(LOW)
        kv_r[:, kw:] = raw[:, qw + kw :].astype(LOW)
        c.wait("h", "qkv", "out")

    ins = [(v, "vmem") for v in (x, r, cos, sin)] + [(p, "hbm") for p in pieces]
    outs = [
        ((toks, width), LOW, "hbm"),
        ((toks, qw), LOW, "vmem"),
        ((toks, 2 * kw), LOW, "vmem"),
        ((8, width), F32, "vmem"),
        ((width, cols), LOW, "hbm"),
        ((width, wide_w - cols), LOW, "hbm"),
    ]
    scratch = [((toks, width), LOW), ((width, wide_w), LOW), ((16 * devices, lanes), LOW)]
    return streaming(body, ins, outs, scratch, len(plan) + 3, LONG)


def query_block(rows, length):
    return min(rows, 256 if length <= 2048 else 128)


def attn_kernel(q, kv, allowed, w):
    rows, qw = q.shape
    length = kv.shape[0]
    width = w.shape[0]
    qb = query_block(rows, length)
    heads = qw // HD

    def body(q_r, kv_r, m_r, w_r, o_r, t_r, a_r):
        ok = m_r[...] > 0
        k, v = kv_r[:, :HD], kv_r[:, HD:]
        logs = []
        for j in range(heads):
            cut = slice(j * HD, (j + 1) * HD)
            b = jnp.tanh(nt(q_r[:, cut], k) * (1.0 / SOFT_CAP))
            c = jnp.where(ok, SOFT_CAP * b, MASKED_SCORE)
            peak = jnp.max(c, axis=-1, keepdims=True)
            e = jnp.exp(c - peak)
            total = jnp.sum(e, axis=-1, keepdims=True)
            p = (e / total).astype(LOW)
            o_r[:, cut] = nn(p, v).astype(LOW)
            logs.append(jnp.broadcast_to(peak + jnp.log(total), (qb, 128)))
        t_r[...] = jnp.concatenate(logs, axis=1)
        a_r[...] = nt(o_r[...], w_r[...]).astype(LOW)

    row = lambda n: ((qb, n), lambda i: (i, 0))
    ins = [(q, *row(qw)), (kv, *all_of(kv.shape)), (allowed, *row(length))]
    ins += [(w, *all_of(w.shape))]
    outs = [
        ((rows, qw), LOW, *row(qw)),
        ((rows, 128 * heads), F32, *row(128 * heads)),
        ((rows, width), LOW, *row(width)),
    ]
    return kernel(body, (rows // qb,), ins, outs)


def attn_back_kernel(
    dh3, x2, dy, a, g3, g2, w, q, kv, allowed, logs, cos, sin
):
    rows, width = x2.shape
    qw = q.shape[1]
    length = kv.shape[0]
    qb = query_block(rows, length)
    heads = qw // HD
    scale = 1.0 / math.sqrt(HD)

    def body(
        d_r, x_r, dy_r, a_r, g3_r, g2_r, w_r, q_r, kv_r, m_r, t_r, c_r, s_r,
        dx_r, da_r, dq_r, dkv_r, dg_r,
    ):
        @pl.when(pl.program_id(0) == 0)
        def _():
            dkv_r[...] = jnp.zeros_like(dkv_r)
            dg_r[...] = jnp.zeros_like(dg_r)

        def step(at, total):
            dv3, dg3 = norm_back_rows(x_r[at, :], g3_r[...], wide(d_r[at, :]))
            dx2 = wide(dy_r[at, :]) + dv3
            dx_r[at, :] = dx2
            da, dg2 = norm_back_rows(wide(a_r[at, :]), g2_r[...], dx2)
            da_r[at, :] = da.astype(LOW)
            return total[0] + dg2, total[1] + dg3

        none = jnp.zeros((8, width), F32)
        dg2, dg3 = over_rows(qb, step, (none, none))
        dg_r[0:1] += jnp.sum(dg2, axis=0, keepdims=True)
        dg_r[1:2] += jnp.sum(dg3, axis=0, keepdims=True)
        do = nn(da_r[...], w_r[...]).astype(LOW)
        ok = m_r[...] > 0
        k, v = kv_r[:, :HD], kv_r[:, HD:]
        c, s = c_r[...], s_r[...]
        dk = dv = 0.0
        for j in range(heads):
            cut = slice(j * HD, (j + 1) * HD)
            qj, doj = q_r[:, cut], do[:, cut]
            b = jnp.tanh(nt(qj, k) * (1.0 / SOFT_CAP))
            logit = jnp.where(ok, SOFT_CAP * b, MASKED_SCORE)
            p = jnp.exp(logit - t_r[:, j * 128 : j * 128 + 1])
            dp = nt(doj, v)
            dc = p * (dp - jnp.sum(p * dp, axis=-1, keepdims=True))
            ds = (dc * (1.0 - b * b)).astype(LOW)
            dq_r[:, cut] = (turn_back(nn(ds, k), c, s) * scale).astype(LOW)
            dk = dk + tn(ds, qj)
            dv = dv + tn(p.astype(LOW), doj)
        dkv_r[:, :HD] += dk
        dkv_r[:, HD:] += dv

    row = lambda n: ((qb, n), lambda i: (i, 0))
    ins = [(v, *row(width)) for v in (dh3, x2, dy, a)]
    ins += [(v, *all_of(v.shape)) for v in (g3, g2, w)]
    ins += [(q, *row(qw)), (kv, *all_of(kv.shape)), (allowed, *row(length))]
    ins += [(logs, *row(128 * heads)), (cos, *row(HD // 2)), (sin, *row(HD // 2))]
    outs = [
        ((rows, width), F32, *row(width)),
        ((rows, width), LOW, *row(width)),
        ((rows, qw), LOW, *row(qw)),
        ((length, 2 * HD), F32, *all_of((length, 2 * HD))),
        ((8, width), F32, *all_of((8, width))),
    ]
    return kernel(body, (rows // qb,), ins, outs, cost=LONG)


class Copies:
    def __init__(self, sems):
        self.sems, self.known = sems, {}

    def start(self, name, src, dst):
        self.known[name] = pltpu.make_async_copy(src, dst, self.sems.at[len(self.known)])
        self.known[name].start()

    def wait(self, *names):
        for name in names:
            self.known[name].wait()


def streaming(body, ins, outs, scratch, copies, cost=NO_COST):
    place = {"vmem": pl.BlockSpec(memory_space=pltpu.VMEM), "hbm": pl.BlockSpec(memory_space=pl.ANY)}
    return pl.pallas_call(
        body,
        in_specs=[place[p] for _, p in ins],
        out_specs=[place[p] for _, _, p in outs],
        out_shape=[jax.ShapeDtypeStruct(s, d) for s, d, _ in outs],
        scratch_shapes=[pltpu.VMEM(*v) for v in scratch]
        + [pltpu.SemaphoreType.DMA((copies,))],
        cost_estimate=cost,
        compiler_params=pltpu.CompilerParams(vmem_limit_bytes=VMEM_MB * 2**20),
    )(*[a for a, _ in ins])


def row_parts(rows, block=128):
    return [pl.ds(i, min(block, rows)) for i in range(0, rows, min(block, rows))]


def row_tiles(mid, tile=384):
    t = math.gcd(mid, tile)
    tiles = [(k, i, k * mid + i, t) for k in range(2) for i in range(0, mid, t)]
    return [tiles[i : i + 2] for i in range(0, len(tiles), 2)]


def ffn_in_kernel(a, x, g2, g3, gm, gs, um, us):
    rows, width = x.shape
    mid, units = um.shape
    bn = math.gcd(units, 768)
    parts, cols = row_parts(rows), [pl.ds(i, bn) for i in range(0, units, bn)]

    def body(
        a_h, x_h, g2_r, g3_r, gm_h, gs_h, um_h, us_h,
        x2_h, h_h, g_h, u_h, hid_h,
        a_r, x_r, x2_r, h_r, wg_r, wu_r, g_r, u_r, hid_r, sems,
    ):
        c = Copies(sems)
        for i, at in enumerate(parts):
            c.start(("a", i), a_h.at[at], a_r.at[at])
            c.start(("x", i), x_h.at[at], x_r.at[at])
        for j, at in enumerate(cols):
            for name, m, s, w in (("g", gm_h, gs_h, wg_r), ("u", um_h, us_h, wu_r)):
                c.start((name, "m", j), m.at[:, at], w.at[pl.ds(0, mid), at])
                c.start((name, "s", j), s.at[:, at], w.at[pl.ds(mid, mid), at])
        out = []

        def send(src, dst, at):
            out.append(len(out))
            c.start(("out", out[-1]), src.at[at], dst.at[at])

        for i, part in enumerate(parts):
            c.wait(("a", i), ("x", i))

            def normed(at, _, first=part.start):
                at = pl.ds(pl.multiple_of(first + at.start, 16), at.size)
                av = wide(a_r[at, :])
                x2 = wide(x_r[at, :]) + av * norm_factor(av) * (1.0 + g2_r[...])
                x2_r[at, :] = x2
                h_r[at, :] = (x2 * norm_factor(x2) * (1.0 + g3_r[...])).astype(LOW)

            over_rows(part.size, normed)
            send(x2_r, x2_h, (part,))
            send(h_r, h_h, (part,))
        for j, at in enumerate(cols):
            c.wait(("g", "m", j), ("g", "s", j), ("u", "m", j), ("u", "s", j))
            h = h_r[...]
            gate, up = nn(h, wg_r[:, at]), nn(h, wu_r[:, at])
            g_r[:, at] = gate.astype(LOW)
            u_r[:, at] = up.astype(LOW)
            hid_r[:, at] = (gelu_parts(gate)[0] * up).astype(LOW)
            for src, dst in ((g_r, g_h), (u_r, u_h), (hid_r, hid_h)):
                send(src, dst, (slice(None), at))
        c.wait(*[("out", i) for i in out])

    t, n = (rows, width), (rows, units)
    ins = [(a, "hbm"), (x, "hbm"), (g2, "vmem"), (g3, "vmem")]
    ins += [(w, "hbm") for w in (gm, gs, um, us)]
    outs = [(t, F32, "hbm"), (t, LOW, "hbm"), (n, LOW, "hbm"), (n, LOW, "hbm"), (n, LOW, "hbm")]
    w = (2 * mid, units)
    scratch = [(t, LOW), (t, LOW), (t, F32), (t, LOW), (w, LOW), (w, LOW)]
    scratch += [(n, LOW)] * 3
    return streaming(body, ins, outs, scratch, 4 * len(parts) + 7 * len(cols))


def project_kernel(u, wm, ws):
    rows, cols = u.shape
    mid = wm.shape[0]
    groups = row_tiles(mid)

    def body(u_r, m_h, s_h, o_h, w_r, o_r, sems):
        c = Copies(sems)
        for g, tiles in enumerate(groups):
            for k, i, at, n in tiles:
                src = (m_h, s_h)[k].at[pl.ds(i, n)]
                c.start((g, at), src, w_r.at[pl.ds(at, n)])
        for g, tiles in enumerate(groups):
            c.wait(*[(g, t[2]) for t in tiles])
            at = pl.ds(tiles[0][2], sum(t[3] for t in tiles))
            o_r[:, at] = nt(u_r[...], w_r[at, :]).astype(LOW)
            c.start(("out", g), o_r.at[:, at], o_h.at[:, at])
        c.wait(*[("out", g) for g in range(len(groups))])

    ins = [(u, "vmem"), (wm, "hbm"), (ws, "hbm")]
    outs = [((rows, 2 * mid), LOW, "hbm")]
    scratch = [((2 * mid, cols), LOW), ((rows, 2 * mid), LOW)]
    n = sum(map(len, groups)) + len(groups)
    return streaming(body, ins, outs, scratch, n)[0]


def ffn_back_kernel(f, x2, dy, g4, gate, up, dm, ds):
    rows, width = x2.shape
    mid, units = dm.shape
    bn = math.gcd(units, 768)
    parts, cols = row_parts(rows), [pl.ds(i, bn) for i in range(0, units, bn)]

    def body(
        f_h, x2_h, dy_h, g4_r, gate_h, up_h, dm_h, ds_h,
        y_h, df_h, dg_h, du_h, g_r,
        f_r, x2_r, dy_r, gate_r, up_r, w_r, y_r, df_r, dg_r, du_r, sems,
    ):
        c = Copies(sems)
        for i, at in enumerate(parts):
            for name, src, dst in (("f", f_h, f_r), ("x", x2_h, x2_r), ("d", dy_h, dy_r)):
                c.start((name, i), src.at[at], dst.at[at])
        for j, at in enumerate(cols):
            c.start(("m", j), dm_h.at[:, at], w_r.at[pl.ds(0, mid), at])
            c.start(("s", j), ds_h.at[:, at], w_r.at[pl.ds(mid, mid), at])
            c.start(("gate", j), gate_h.at[:, at], gate_r.at[:, at])
            c.start(("up", j), up_h.at[:, at], up_r.at[:, at])
        out = []

        def send(src, dst, at):
            out.append(len(out))
            c.start(("out", out[-1]), src.at[at], dst.at[at])

        total = jnp.zeros((8, width), F32)
        for i, part in enumerate(parts):
            c.wait(("f", i), ("x", i), ("d", i))

            def step(at, total, first=part.start):
                at = pl.ds(pl.multiple_of(first + at.start, 16), at.size)
                fv, g4v, x2v = wide(f_r[at, :]), g4_r[...], x2_r[at, :]
                y_r[at, :] = (x2v + fv * norm_factor(fv) * (1.0 + g4v)).astype(LOW)
                df, dg = norm_back_rows(fv, g4v, wide(dy_r[at, :]))
                df_r[at, :] = df.astype(LOW)
                return total + dg

            total = over_rows(part.size, step, total)
            send(y_r, y_h, (part,))
            send(df_r, df_h, (part,))
        g_r[...] = jnp.sum(total, axis=0, keepdims=True)
        for j, at in enumerate(cols):
            c.wait(("m", j), ("s", j), ("gate", j), ("up", j))
            dh = nn(df_r[...], w_r[:, at])
            gl, dgl = gelu_parts(wide(gate_r[:, at]))
            dg_r[:, at] = (dh * wide(up_r[:, at]) * dgl).astype(LOW)
            du_r[:, at] = (dh * gl).astype(LOW)
            send(dg_r, dg_h, (slice(None), at))
            send(du_r, du_h, (slice(None), at))
        c.wait(*[("out", i) for i in out])

    t, n = (rows, width), (rows, units)
    ins = [(v, "hbm") for v in (f, x2, dy)] + [(g4, "vmem")]
    ins += [(v, "hbm") for v in (gate, up, dm, ds)]
    outs = [(t, LOW, "hbm"), (t, LOW, "hbm"), (n, LOW, "hbm"), (n, LOW, "hbm")]
    outs += [((1, width), F32, "vmem")]
    scratch = [(t, LOW), (t, F32), (t, LOW), (n, LOW), (n, LOW), ((2 * mid, units), LOW)]
    scratch += [(t, LOW), (t, LOW), (n, LOW), (n, LOW)]
    return streaming(body, ins, outs, scratch, 5 * len(parts) + 6 * len(cols))


def ffn_inputs_kernel(dg, du, gm, gs, um, us):
    rows, units = dg.shape
    mid = um.shape[0]
    groups = row_tiles(mid)

    def body(dg_r, du_r, gm_h, gs_h, um_h, us_h, o_h, wg_r, wu_r, o_r, sems):
        c = Copies(sems)
        for g, tiles in enumerate(groups):
            for k, i, at, n in tiles:
                for name, src, dst in (("g", (gm_h, gs_h), wg_r), ("u", (um_h, us_h), wu_r)):
                    c.start((name, g, at), src[k].at[pl.ds(i, n)], dst.at[pl.ds(at, n)])
        for g, tiles in enumerate(groups):
            c.wait(*[(name, g, t[2]) for t in tiles for name in "gu"])
            at = pl.ds(tiles[0][2], sum(t[3] for t in tiles))
            v = nt(dg_r[...], wg_r[at, :]) + nt(du_r[...], wu_r[at, :])
            o_r[:, at] = v.astype(LOW)
            c.start(("out", g), o_r.at[:, at], o_h.at[:, at])
        c.wait(*[("out", g) for g in range(len(groups))])

    ins = [(dg, "vmem"), (du, "vmem")] + [(w, "hbm") for w in (gm, gs, um, us)]
    outs = [((rows, 2 * mid), LOW, "hbm")]
    w = ((2 * mid, units), LOW)
    n = 2 * sum(map(len, groups)) + len(groups)
    return streaming(body, ins, outs, [w, w, ((rows, 2 * mid), LOW)], n)[0]


def outer_kernel(a, b, *got, side, cuts, cost=NO_COST):
    toks, cols = b.shape
    mid = a.shape[1] // 2
    bn = math.gcd(cols, 768)
    chunks = [pl.ds(i, bn) for i in range(0, cols, bn)]
    n, m = len(got), len(cuts)
    at = [sum(cuts[:i]) for i in range(m)]
    step = mid // n if n else 0

    def body(a_h, b_h, *refs):
        got_h, out_h = refs[:n], refs[n : n + m]
        a_r, b_r, got_r, out_r, sems = refs[n + m :]
        c = Copies(sems)
        c.start("a", a_h.at[:, pl.ds(side * mid, mid)], a_r)
        for j, part in enumerate(chunks):
            c.start(("b", j), b_h.at[:, part], b_r.at[:, part])
        for i in range(n):
            c.start(("got", i), got_h[i], got_r.at[pl.ds(i * step, step)])
        c.wait("a")
        for j, part in enumerate(chunks):
            c.wait(("b", j))
            v = tn(a_r[...], b_r[:, part])
            if n:
                if j == 0:
                    c.wait(*[("got", i) for i in range(n)])
                v = v + wide(got_r[:, part])
            out_r[:, part] = v.astype(LOW)
            for i in range(m):
                c.start(
                    ("out", i, j),
                    out_r.at[pl.ds(at[i], cuts[i]), part],
                    out_h[i].at[:, part],
                )
        c.wait(*[("out", i, j) for i in range(m) for j in range(len(chunks))])

    ins = [(v, "hbm") for v in (a, b, *got)]
    outs = [((r, cols), LOW, "hbm") for r in cuts]
    full = (mid, cols)
    scratch = [((toks, mid), LOW), ((toks, cols), LOW)]
    scratch += [(full if n else (16, 128), LOW), (full, LOW)]
    copies = 1 + len(chunks) * (1 + m) + n
    return streaming(body, ins, outs, scratch, copies, cost)


def sum_kernel(s, ra, rb, qa, qb):
    rows, cols = s.shape
    h = ra.shape[0]
    bc = math.gcd(cols, 768)

    def body(s_r, ra_r, rb_r, qa_r, qb_r, o_r):
        o_r[:h] = wide(s_r[:h]) + wide(ra_r[...]) + wide(qa_r[...])
        o_r[h:] = wide(s_r[h:]) + wide(rb_r[...]) + wide(qb_r[...])

    tile = lambda r: ((r, bc), lambda j: (0, j))
    ins = [(v, *tile(v.shape[0])) for v in (s, ra, rb, qa, qb)]
    return kernel(body, (cols // bc,), ins, [((rows, cols), F32, *tile(rows))])[0]


def add_kernel(a, b):
    rows, cols = a.shape
    bc = math.gcd(cols, 1152)

    def body(a_r, b_r, o_r):
        o_r[...] = (wide(a_r[...]) + wide(b_r[...])).astype(LOW)

    tile = ((rows, bc), lambda j: (0, j))
    return kernel(body, (cols // bc,), [(a, *tile), (b, *tile)], [(a.shape, LOW, *tile)])[0]


def last_kernel(x, gain, dh1, dx2):
    rows, width = x.shape
    br = min(rows, 128)

    def body(x_r, g_r, d_r, dx_r, o_r, dg_r):
        def step(at, total):
            dv, dg = norm_back_rows(wide(x_r[at, :]), g_r[...], wide(d_r[at, :]))
            o_r[at, :] = dx_r[at, :] + dv
            return total + dg

        @pl.when(pl.program_id(0) == 0)
        def _():
            dg_r[...] = jnp.zeros_like(dg_r)

        total = over_rows(br, step, jnp.zeros((8, width), F32))
        dg_r[...] += jnp.sum(total, axis=0, keepdims=True)

    row = ((br, width), lambda i: (i, 0))
    ins = [(x, *row), (gain, *all_of(gain.shape)), (dh1, *row), (dx2, *row)]
    outs = [((rows, width), F32, *row), ((1, width), F32, *all_of((1, width)))]
    return kernel(body, (rows // br,), ins, outs)


def order_kernel(v, bits, back, ny, nx, factors=False):
    rows, width = v.shape
    blk = width // (2 * ny * nx)
    br = min(rows, 128)
    here = lambda c, y, x: (c * ny + y) * nx + x
    there = lambda c, y, x: (y * 2 + c) * nx + x
    keys = [(c, y, x) for c in range(2) for y in range(ny) for x in range(nx)]
    src, dst = (here, there) if back else (there, here)
    flips = 3 if ny == 2 and nx == 2 else 1

    def body(b_r, v_r, o_r, *f_r):
        def step(at, _):
            rows_ = v_r[at, :]
            if factors:
                f = norm_factor(wide(rows_))
                f_r[0][at, :] = jnp.broadcast_to(f, (f.shape[0], 128))
            cut = lambda j: rows_[:, j * blk : (j + 1) * blk]
            parts = {k: cut(src(*k)) for k in keys}
            for pos in range(flips):
                on = b_r[pos] == 0
                flip = lambda k: tuple(1 - e if i == pos else e for i, e in enumerate(k))
                parts = {k: jnp.where(on, parts[k], parts[flip(k)]) for k in keys}
            o_r[at, :] = jnp.concatenate([parts[k] for k in sorted(keys, key=lambda k: dst(*k))], axis=1)

        over_rows(br, step)

    tile = pl.BlockSpec((br, width), lambda i: (i, 0))
    return pl.pallas_call(
        body,
        grid=(rows // br,),
        in_specs=[pl.BlockSpec(memory_space=pltpu.SMEM), tile],
        out_specs=[tile, pl.BlockSpec((br, 128), lambda i: (i, 0))][: 1 + factors],
        out_shape=[
            jax.ShapeDtypeStruct(v.shape, v.dtype),
            jax.ShapeDtypeStruct((rows, 128), F32),
        ][: 1 + factors],
        cost_estimate=NO_COST,
    )(bits, v)


def keys_back_kernel(own, got, cos, sin):
    def body(a_r, b_r, c_r, s_r, o_r):
        v = a_r[...] + wide(b_r[...])
        o_r[:, :HD] = turn_back(v[:, :HD], c_r[...], s_r[...]).astype(LOW)
        o_r[:, HD:] = v[:, HD:].astype(LOW)

    ins = [(v, *all_of(v.shape)) for v in (own, got, cos, sin)]
    return kernel(body, (1,), ins, [(own.shape, LOW, *all_of(own.shape))])[0]


def make_local(ny, nx, nz):
    square = ny == 2 and nx == 2
    plane = ny * nx

    def order(v, back=False, factors=False):
        bits = jnp.stack([lax.axis_index(a) for a in ("core", "y", "ctx")])
        out = order_kernel(v, bits.astype(jnp.int32), back, ny, nx, factors)
        return out if factors else out[0]

    def row_order(w):
        blk = w.shape[0] // (2 * plane)
        c = lax.axis_index("core")
        out = jnp.zeros_like(w)
        for half in range(2):
            for y in range(ny):
                for x in range(nx):
                    i = (half * ny + y) * nx + x
                    gy, gx = y, x
                    if square:
                        gy, gx = y ^ lax.axis_index("y"), x ^ lax.axis_index("ctx")
                    at = ((gy * 2 + (c ^ half)) * nx + gx) * blk
                    piece = lax.slice_in_dim(w, i * blk, (i + 1) * blk, axis=0)
                    out = lax.dynamic_update_slice_in_dim(out, piece, at, 0)
        return out

    def local(
        layer_input,
        query_weight,
        key_weight,
        value_weight,
        output_weight,
        gate_weight,
        up_weight,
        down_weight,
        attn_in_gain,
        attn_out_gain,
        ffn_in_gain,
        ffn_out_gain,
        out_cotangent,
        segment_ids,
        live_mask,
    ):
        rows, toks, width = layer_input.shape
        blk, qw = query_weight.shape
        kw = key_weight.shape[1]
        qkv_w = qw + 2 * kw
        mid = width // 2
        seq = Order()

        class ZSum:
            def __init__(self, part):
                self.own = lax.psum_scatter(
                    part, "tensor", scatter_dimension=0, tiled=True
                )

            def middle(self):
                (own,) = seq(self.own)
                seq.last = (own,)
                self.out = lax.all_gather(own, "tensor", axis=0, tiled=True)

        class Weight:
            def __init__(self, w):
                self.w = w
                if not square:
                    m = lax.all_gather(w, ("y", "ctx"), axis=0, tiled=True)
                    self.mine, self.other = [m], [to_core(m)]

            def near(self):
                if square:
                    w = self.w
                    self.mine = [w, seq.send(to_ctx, w), seq.send(to_y, w)]
                    self.other = [seq.send(to_core, w)]

            def far(self):
                if square:
                    h = blk // 2
                    wx, wy = seq(*self.mine[1:])
                    self.mine += [seq.send(to_y, wx[:h]), seq.send(to_ctx, wy[h:])]
                    self.other += [seq.send(to_core, wx), seq.send(to_core, wy)]

            def core(self):
                if square:
                    self.mine[3:] = seq(*self.mine[3:])
                    self.other += [seq.send(to_core, d) for d in self.mine[3:]]

        def stack(*weights, cost=NO_COST):
            pieces, plans = [], []
            for weight in weights:
                plan = []
                for o, side in enumerate((weight.mine, weight.other)):
                    at = 0
                    for p in side:
                        plan.append((len(pieces), o, 0, p.shape[0], at))
                        at += p.shape[0]
                        pieces.append(p)
                plans.append(plan)
            return seq.run(
                stack_kernel, *pieces, outs=[plane * blk] * 2, plan=plans, cost=cost
            )

        def packet_plan():
            pieces, plan, full, device = [], [], packet.w.shape[0], 0
            for side in (packet.mine, packet.other):
                at = 0
                for p in side:
                    i, r = 0, p.shape[0]
                    while i < r:
                        d, inside = divmod(at + i, full)
                        d += device
                        if inside < blk:
                            k = min(r - i, blk - inside)
                            plan.append((len(pieces), i, k, d * blk + inside, None))
                        else:
                            k = min(r - i, full - inside)
                            plan.append((len(pieces), i, k, None, d * 16))
                        i += k
                    at += r
                    pieces.append(p)
                device += plane
            return pieces, plan

        gains = jnp.stack([attn_in_gain, attn_out_gain, ffn_in_gain, ffn_out_gain])
        own = [query_weight, key_weight, value_weight, output_weight]
        own = jnp.concatenate(own, axis=1)
        gains = jnp.pad(gains, ((0, 12), (0, own.shape[1] - blk)))
        packet = Weight(jnp.concatenate([own, gains], axis=0))
        index = lax.axis_index("ctx") * toks + jnp.arange(toks, dtype=jnp.int32)
        own_info = jnp.concatenate([segment_ids, live_mask, index[None]], axis=0)

        def positions(info):
            seg_all, live_all, index_all = info[0:1], info[1:2], info[2:3]
            seg_col, index_col = segment_ids.reshape(toks, 1), index.reshape(toks, 1)
            start = jnp.sum((seg_all < seg_col).astype(jnp.int32), axis=1)
            allowed = (
                (index_all <= index_col)
                & (seg_all == seg_col)
                & ((live_all == 1) | (index_all == index_col))
            ).astype(LOW)
            freq = jnp.exp(
                jnp.arange(HD // 2, dtype=F32) * (-2.0 * math.log(10000.0) / HD)
            )
            angle = wide(index - start)[:, None] * freq
            return allowed, jnp.cos(angle), jnp.sin(angle)

        x_raw = layer_input.reshape(toks, width)
        dy_raw = out_cotangent.reshape(toks, width)
        half_w = gate_weight.shape[1] * 4 // 9 // 128 * 128
        wga, wgb = Weight(gate_weight[:, :half_w]), Weight(gate_weight[:, half_w:])
        wu, wd = Weight(up_weight), Weight(down_weight)

        packet.near()
        if square:
            info = jnp.concatenate([own_info, seq.send(to_ctx, own_info)], axis=1)
        else:
            info = lax.all_gather(own_info, "ctx", axis=1, tiled=True)
        x, factors = seq.run(order, x_raw, factors=True)
        packet.far()
        allowed, cos, sin = seq.run(positions, info)
        packet.core()
        wga.near()
        pieces, plan = packet_plan()
        h1, q, kv, gain, w_qkv, w_out = seq.run(
            first_kernel, x, factors, cos, sin, *pieces, plan=plan, blk=blk, qw=qw, kw=kw
        )
        g1, g2, g3, g4 = [gain[i : i + 1] for i in range(4)]
        if square:
            kv_got = seq.send(to_ctx, kv)
            wga.far()
            wgb.near()
            kv_all = seq.run(lambda a, b: jnp.concatenate([a, b], 0), kv, kv_got)
        else:
            kv_all = lax.all_gather(kv, "ctx", axis=0, tiled=True)
        length = kv_all.shape[0]

        o, logs, part = seq.run(attn_kernel, q, kv_all, allowed, w_out)
        za = ZSum(part)
        wgb.far()
        wu.near()
        wga.core()
        wgb.core()
        gate_w = stack(wga, wgb)
        wd.near()
        wu.far()
        za.middle()
        wu.core()
        up_m, up_s = stack(wu)
        dy = seq.run(order, dy_raw)
        wd.far()
        x2, h3, gate, up, hid = seq.run(
            ffn_in_kernel, za.out, x, g2, g3, *gate_w, up_m, up_s
        )
        wd.core()
        down_m, down_s = stack(wd)
        part = seq.run(project_kernel, hid, down_m, down_s)
        zf = ZSum(part)
        zf.middle()
        qkv_g = seq.run(row_order, w_qkv)
        g1_g = seq.run(order, jnp.broadcast_to(g1, (16, width)), back=True)[:1]

        y, df, dgate, dup, dg4 = seq.run(
            ffn_back_kernel, zf.out, x2, dy, g4, gate, up, down_m, down_s
        )
        part = seq.run(ffn_inputs_kernel, dgate, dup, *gate_w, up_m, up_s)
        zd = ZSum(part)

        class Scatter:
            def __init__(self, a, b):
                self.ab = a, b

            def low(self, cost=NO_COST):
                cuts = [blk] * 4 if square else [mid]
                low = seq.run(outer_kernel, *self.ab, side=1, cuts=cuts, cost=cost)
                self.got = [seq.send(to_core, v) for v in low]

            def first(self, cost=NO_COST):
                h = blk // 2
                cuts = [blk] + [h] * 6 if square else [mid]
                self.s = seq.run(
                    outer_kernel, *self.ab, *self.got, side=0, cuts=cuts, cost=cost
                )
                if square:
                    self.gx = seq.send(to_ctx, self.s[5])
                    self.gy = seq.send(to_y, self.s[6])

            def plain(self):
                if square:
                    self.xa = seq.send(to_ctx, self.s[1])
                    self.yb = seq.send(to_y, self.s[4])

            def wait(self):
                if square:
                    self.xa, self.yb = seq(self.xa, self.yb)
                    seq.last = (self.xa, self.yb)

            def second(self):
                if not square:
                    self.rest = lax.psum_scatter(
                        self.s[0], ("y", "ctx"), scatter_dimension=0, tiled=True
                    )
                    return
                t1 = seq.run(add_kernel, self.s[2], self.gy)
                self.xb = seq.send(to_ctx, t1)
                t2 = seq.run(add_kernel, self.s[3], self.gx)
                self.ya = seq.send(to_y, t2)

            def end(self):
                if not square:
                    return wide(self.rest)
                return seq.run(
                    sum_kernel, self.s[0], self.xa, self.xb, self.ya, self.yb
                )

        sd, sg, su = Scatter(df, hid), Scatter(h3, dgate), Scatter(h3, dup)
        sd.low()
        sg.low()
        sd.first()
        sd.plain()
        su.low(cost=LONG)
        sg.first()
        sg.plain()
        sd.second()
        sd.wait()
        zd.middle()
        su.first(cost=LONG)
        sg.second()
        sg.wait()
        down_grad = sd.end()
        layer_output = seq.run(order, y, back=True)

        dx2, da, dq, dkv, dg23 = seq.run(
            attn_back_kernel, zd.out, x2, dy, za.out, g3, g2, w_out,
            q, kv_all, allowed, logs, cos, sin,
        )
        if square:
            got = seq.send(to_ctx, dkv[toks:].astype(LOW))
            own = dkv[:toks]
        else:
            got = lax.psum_scatter(
                dkv.astype(LOW), "ctx", scatter_dimension=0, tiled=True
            )
            own = jnp.zeros((toks, 2 * kw), F32)
        su.plain()
        so = Scatter(da, o)
        so.low(cost=LONG)
        su.second()
        dkv_low = seq.run(keys_back_kernel, own, got, cos, sin)
        dqkv = seq.run(lambda a, b: jnp.concatenate([a, b], 1), dq, dkv_low)
        part = seq.run(project_kernel, dqkv, qkv_g[:mid], qkv_g[mid:])
        z1 = ZSum(part)
        sq = Scatter(h1, dqkv)
        sq.low()
        so.first()
        so.plain()
        sq.first(cost=LONG)
        su.wait()
        sq.plain()
        gate_grad = sg.end()
        dx2 = seq.run(order, dx2, back=True)
        so.second()
        up_grad = su.end()
        z1.middle()
        so.wait()
        sq.second()
        out_grad = so.end()
        sq.wait()
        qkv_grad = sq.end()
        input_grad, dg1 = seq.run(last_kernel, x_raw, g1_g, z1.out, dx2)
        dg1 = order(jnp.broadcast_to(dg1, (16, width)))[:1]
        dgain = jnp.concatenate([dg1, dg23[:2], dg4], axis=0)
        dgain = dgain[:, :mid] + to_core(dgain[:, mid:])
        if square:
            s = dgain[:, : mid // 2] + to_y(dgain[:, mid // 2 :])
            dgain = s[:, :blk] + to_ctx(s[:, blk:])
        else:
            dgain = lax.psum_scatter(
                dgain, ("y", "ctx"), scatter_dimension=1, tiled=True
            )
        return (
            layer_output.reshape(rows, toks, width),
            input_grad.reshape(rows, toks, width),
            qkv_grad[:, :qw],
            qkv_grad[:, qw : qw + kw],
            qkv_grad[:, qw + kw :],
            out_grad,
            gate_grad,
            up_grad,
            down_grad,
            dgain[0],
            dgain[1],
            dgain[2],
            dgain[3],
        )

    return local


def solution(mesh):
    dp, nx, nz = (mesh.shape[a] for a in ("dp", "ctx", "tensor"))
    fine = Mesh(
        mesh.devices.reshape(dp // 2, 2, nx, nz), ("y", "core", "ctx", "tensor")
    )
    d = ("y", "core")
    w = P(("y", "core", "ctx"), "tensor")
    g = P(("y", "core", "ctx"))
    t = P(d, "ctx", None)
    return jax.shard_map(
        make_local(dp // 2, nx, nz),
        mesh=fine,
        in_specs=(t, w, w, w, w, w, w, w, g, g, g, g, t, P(d, "ctx"), P(d, "ctx")),
        out_specs=(t, t, w, w, w, w, w, w, w, g, g, g, g),
        check_vma=False,
    )
```

time: 868 us -> 735 us (0.85)
  other arithmetic: 83.1 us -> 7.31 us
  Pallas kernels: 228 us -> 301 us
  local copies, waits for them, and re-layouts: 123 us -> 51.6 us
  waiting for transfers between devices: 338 us -> 279 us
    ppermute x12 -> x0, waiting for transfers between devices: 124 us -> none  [hop(): return lambda a: lax.ppermute(a, 'tensor', [(k, k ^ bit) for k in range(4)])]
    psum x4 -> x0, waiting for transfers between devices: 112 us -> none  [the longest x1 65.1 us: local(): dh1 = lax.psum(part, 'tensor')]
    pallas_call x24 -> x44, Pallas kernels: 228 us -> 301 us  [the longest x16 157 us: streaming(): pl.pallas_call(body, in_specs=[place[p] for _, p in ins], out_specs=[plac...]
    ppermute x22 -> x26, waiting for transfers between devices: 26.3 us -> 94.8 us  [to_y(): return lax.ppermute(a, 'y', SWAP)]
    reduce_scatter x0 -> x4, waiting for transfers between devices: none -> 48.1 us  [__init__(): self.own = lax.psum_scatter(part, 'tensor', scatter_dimension=0, tiled=True)]
    all_gather x0 -> x4, waiting for transfers between devices: none -> 41.4 us  [middle(): self.out = lax.all_gather(own, 'tensor', axis=0, tiled=True)]
    concatenate x26 -> x2, other arithmetic: 32.7 us -> 1.29 us  [the longest x1 1.26 us: local(): packet = Weight(jnp.concatenate([own, gains], axis=0))]
    concatenate x14 -> x2, local copies, waits for them, and re-layouts: 26.6 us -> 1.15 us  [the longest x1 1.11 us: local(): dqkv = seq.run(lambda a, b: jnp.concatenate([a, b], 1), dq, dkv_low)]
  transfers between devices with their start and end apart: 74 -> 109, of which waited for: 31 -> 42; matrix products, arithmetic and copies ran while one was open for 19% -> 6% of each run, Pallas kernels for 17% -> 30%
where the time goes in v3:
time: 735 us; the launch traced here: 725 us
  Pallas kernels  301 us (41%)
  waiting for transfers between devices  279 us (38%)
  starting transfers between devices  70.8 us (10%)
  local copies, waits for them, and re-layouts  51.6 us (7%)
  between operations  15.8 us (2%)
    pallas_call x16, Pallas kernels, streaming(): pl.pallas_call(body, in_specs=[place[p] for _, p in ins], out_specs=[plac...  157 us
    pallas_call x22, Pallas kernels, kernel(): pl.pallas_call(body, grid=grid, in_specs=[spec(*e[1:]) for e in ins], out...  114 us
    ppermute x26, waiting for transfers between devices, to_y(): return lax.ppermute(a, 'y', SWAP)  94.8 us
    ppermute x29, waiting for transfers between devices, to_ctx(): return lax.ppermute(a, 'ctx', SWAP)  80.9 us
    reduce_scatter x4, waiting for transfers between devices, __init__(): self.own = lax.psum_scatter(part, 'tensor', scatter_dimension=0, tiled=True)  48.1 us
    all_gather x4, waiting for transfers between devices, middle(): self.out = lax.all_gather(own, 'tensor', axis=0, tiled=True)  41.4 us
    ppermute x29, starting transfers between devices, to_ctx(): return lax.ppermute(a, 'ctx', SWAP)  31.7 us
    pallas_call x6, Pallas kernels, order_kernel(): pl.pallas_call(body, grid=(rows // br,), in_specs=[pl.BlockSpec(memory_sp...  29.4 us
  transfers between devices with their start and end apart: 109, of which 42 were waited for; matrix products, arithmetic and copies ran while one was open for 6% of the time, Pallas kernels for 30%

profile of v3, /device:TPU:0, one launch (start us, length us, event | category | flops | bytes accessed | tf_op | source)
XLA Modules:
  0.0 725.2 jit_solution(6384319519442109571)
XLA Ops:
  24.2 12.4 %collective-permute-done = s32[3,512]{1,0:T(4,128)S(1)} collective-permute-done((s32[3,512]{1,0:T(4,128)S(1)}, s32[3,512]{1,0:T(4,128)S(1)}, u32[]{:S(2)}, u32[]{:S(2)}) %collective-permute-start) | collective-permute-done | bytes 6176 | tf_op jit(solution)/shard_map/ppermute | solution.py:50
  55.2 9.7 %shard_map.247 = (bf16[512,2304]{1,0:T(8,128)(2,1)}, bf16[512,512]{1,0:T(8,128)(2,1)}, bf16[512,512]{1,0:T(8,128)(2,1)}, f32[8,2304]{1,0:T(8,128)}, bf16[2304,10...) custom-call(bf16[512,2304]{1,0:T(8,128)(2,1)} %get-tuple-element.558.x_r.x_h, f32[512,128]{1,0:T(8,128)} %get-tuple-element.447.r_r, ...), custom_call_target="tpu_custom_call" | custom-call | flops 999999995904 | tf_op jit(solution)/shard_map/pallas_call | solution.py:343
  69.2 9.3 %collective-permute-done.10 = bf16[512,512]{1,0:T(8,128)(2,1)S(1)} collective-permute-done((bf16[512,512]{1,0:T(8,128)(2,1)}, bf16[512,512]{1,0:T(8,128)(2,1)S(1)}, u32[]{:S(2)}, u32[]{:S(2)}) %collective-permute-start.10) | collective-permute-done | bytes 524320 | tf_op jit(solution)/shard_map/ppermute | solution.py:50
  92.3 12.1 %collective-permute-done.14.refs_12_ = bf16[288,1280]{1,0:T(8,128)(2,1)S(1)} collective-permute-done((bf16[288,1280]{1,0:T(8,128)(2,1)S(1)}, bf16[288,1280]{1,0:T(8,128)(2,1)S(1)}, u32[]{:S(2)}, u32[]{:S(2)}) %collective-permute-start.14) | collective-permute-done | bytes 737312 | tf_op jit(solution)/shard_map/ppermute | solution.py:54
  133.4 10.9 %shard_map.249 = (bf16[1152,2304]{1,0:T(8,128)(2,1)}, bf16[1152,2304]{1,0:T(8,128)(2,1)}) custom-call(bf16[288,1024]{1,0:T(8,128)(2,1)} %slice.147.refs_0_, bf16[288,1024]{1,0:T(8,128)(2,1)} %collective-permute-done.11.refs_1_, bf16[288,1024]{1,0:T(8,128)(2,1)} %collective-permute-done.12.refs_2_, bf16[144,1024]{1,0:T(8,128)(2,1)} %copy-done.50, ...), custom_call_target="tpu_custom_call" | custom-call | tf_op jit(solution)/shard_map/pallas_call | solution.py:120
  144.3 9.4 %collective-permute-done.16.refs_2_ = bf16[288,2304]{1,0:T(8,128)(2,1)S(1)} collective-permute-done((bf16[288,2304]{1,0:T(8,128)(2,1)}, bf16[288,2304]{1,0:T(8,128)(2,1)S(1)}, u32[]{:S(2)}, u32[]{:S(2)}) %collective-permute-start.16) | collective-permute-done | bytes 1327136 | tf_op jit(solution)/shard_map/ppermute | solution.py:54
  157.4 15.7 %collective-permute-done.32.refs_4_ = bf16[144,2304]{1,0:T(8,128)(2,1)S(1)} collective-permute-done((bf16[144,2304]{1,0:T(8,128)(2,1)}, bf16[144,2304]{1,0:T(8,128)(2,1)S(1)}, u32[]{:S(2)}, u32[]{:S(2)}) %collective-permute-start.32) | collective-permute-done | bytes 663584 | tf_op jit(solution)/shard_map/ppermute | solution.py:50
  177.8 9.0 %shard_map.250 = (bf16[1152,2304]{1,0:T(8,128)(2,1)}, bf16[1152,2304]{1,0:T(8,128)(2,1)}) custom-call(bf16[288,2304]{1,0:T(8,128)(2,1)} %refs_0_, bf16[288,2304]{1,0:T(8,128)(2,1)} %copy-done.3, bf16[288,2304]{1,0:T(8,128)(2,1)} %copy-done.2, bf16[144,2304]{1,0:T(8,128)(2,1)} %copy-done.27, bf16[144,2304]{1,0:T(8,128)(2,1)} %copy-done.26, ...), custom_call_target="tpu_custom_call" | custom-call | tf_op jit(solution)/shard_map/pallas_call | solution.py:120
  192.9 10.8 %collective-permute-done.39.refs_2_ = bf16[288,2304]{1,0:T(8,128)(2,1)} collective-permute-done((bf16[288,2304]{1,0:T(8,128)(2,1)}, bf16[288,2304]{1,0:T(8,128)(2,1)}, u32[]{:S(2)}, u32[]{:S(2)}) %collective-permute-start.39) | collective-permute-done | bytes 1327136 | tf_op jit(solution)/shard_map/ppermute | solution.py:54
  210.7 20.7 %shard_map.252 = (f32[512,2304]{1,0:T(8,128)}, bf16[512,2304]{1,0:T(8,128)(2,1)}, bf16[512,2304]{1,0:T(8,128)(2,1)}, bf16[512,2304]{1,0:T(8,128)(2,1)}, bf16[512,2304]{1,0:T(8,128)(2,1)}) custom-call(bf16[512,2304]{1,0:T(8,128)(2,1)} %all-gather.5.cloned.1.call-done.a_h.a_r, bf16[512,2304]{1,0:T(8,128)(2,1)} %get-tuple-element.558.x_r.x_h, ...), custom_call_target="tpu_custom_call" | custom-call | tf_op jit(solution)/shard_map/pallas_call | solution.py:343
  235.8 9.2 %shard_map.253 = (bf16[1152,2304]{1,0:T(8,128)(2,1)}, bf16[1152,2304]{1,0:T(8,128)(2,1)}) custom-call(bf16[288,2304]{1,0:T(8,128)(2,1)} %refs_0_.1, bf16[288,2304]{1,0:T(8,128)(2,1)} %collective-permute-done.38.refs_1_, bf16[288,2304]{1,0:T(8,128)(2,1)} %collective-permute-done.39.refs_2_, bf16[144,2304]{1,0:T(8,128)(2,1)} %collective-permute-done.40.refs_3_, ...), custom_call_target="tpu_custom_call" | custom-call | tf_op jit(solution)/shard_map/pallas_call | solution.py:120
  245.0 11.9 %shard_map.254 = bf16[512,2304]{1,0:T(8,128)(2,1)} custom-call(bf16[512,2304]{1,0:T(8,128)(2,1)} %get-tuple-element.630.u_r.b_h, bf16[1152,2304]{1,0:T(8,128)(2,1)} %get-tuple-element.598.m_h.dm_h, bf16[1152,2304]{1,0:T(8,128)(2,1)} %get-tuple-element.599.s_h.ds_h), custom_call_target="tpu_custom_call" | custom-call | tf_op jit(solution)/shard_map/pallas_call | solution.py:343
  257.0 48.1 %reduce-scatter.7.cloned.1.call-done = bf16[128,2304]{1,0:T(8,128)(2,1)} async-done(((bf16[512,2304]{1,0:T(8,128)(2,1)}), bf16[128,2304]{1,0:T(8,128)(2,1)}) %reduce-scatter.7.cloned.1.call-update) | async-done | bytes 589840 | tf_op jit(solution)/shard_map/reduce_scatter | solution.py:730
  320.9 35.7 %all-gather.7.cloned.1.call-done.f_h = bf16[512,2304]{1,0:T(8,128)(2,1)} async-done(((bf16[128,2304]{1,0:T(8,128)(2,1)}), bf16[512,2304]{1,0:T(8,128)(2,1)}) %all-gather.7.cloned.1.call-update) | async-done | bytes 2359312 | tf_op jit(solution)/shard_map/all_gather | solution.py:737
  356.5 18.6 %shard_map.256 = (bf16[512,2304]{1,0:T(8,128)(2,1)}, bf16[512,2304]{1,0:T(8,128)(2,1)}, bf16[512,2304]{1,0:T(8,128)(2,1)}, bf16[512,2304]{1,0:T(8,128)(2,1)}, f32[1,2304]{1,0:T(1,128)}) custom-call(bf16[512,2304]{1,0:T(8,128)(2,1)} %all-gather.7.cloned.1.call-done.f_h, f32[512,2304]{1,0:T(8,128)} %get-tuple-element.707.x2_h.x_r, ...), custom_call_target="tpu_custom_call" | custom-call | tf_op jit(solution)/shard_map/pallas_call | solution.py:343
  375.1 20.8 %shard_map.257 = bf16[512,2304]{1,0:T(8,128)(2,1)} custom-call(bf16[512,2304]{1,0:T(8,128)(2,1)} %get-tuple-element.656.dg_r.b_h, bf16[512,2304]{1,0:T(8,128)(2,1)} %get-tuple-element.680.du_r.b_h, bf16[1152,2304]{1,0:T(8,128)(2,1)} %get-tuple-element.607.gm_h, bf16[1152,2304]{1,0:T(8,128)(2,1)} %get-tuple-element.608.gs_h, ...), custom_call_target="tpu_custom_call" | custom-call | tf_op jit(solution)/shard_map/pallas_call | solution.py:343
  412.3 9.2 %shard_map.260 = (bf16[288,2304]{1,0:T(8,128)(2,1)}, bf16[144,2304]{1,0:T(8,128)(2,1)}, bf16[144,2304]{1,0:T(8,128)(2,1)}, bf16[144,2304]{1,0:T(8,128)(2,1)}, bf...) custom-call(bf16[512,2304]{1,0:T(8,128)(2,1)} %get-tuple-element.629.a_h, ...), custom_call_target="tpu_custom_call" | custom-call | tf_op jit(solution)/shard_map/pallas_call | solution.py:343
  441.1 11.8 %collective-permute-done.52.qb_r = bf16[144,2304]{1,0:T(8,128)(2,1)} collective-permute-done((bf16[144,2304]{1,0:T(8,128)(2,1)}, bf16[144,2304]{1,0:T(8,128)(2,1)}, u32[]{:S(2)}, u32[]{:S(2)}) %collective-permute-start.52) | collective-permute-done | bytes 663584 | tf_op jit(solution)/shard_map/ppermute | solution.py:54
  452.9 9.1 %shard_map.262 = (bf16[288,2304]{1,0:T(8,128)(2,1)}, bf16[144,2304]{1,0:T(8,128)(2,1)}, bf16[144,2304]{1,0:T(8,128)(2,1)}, bf16[144,2304]{1,0:T(8,128)(2,1)}, bf...) custom-call(bf16[512,2304]{1,0:T(8,128)(2,1)} %get-tuple-element.679.a_h, ...), custom_call_target="tpu_custom_call" | custom-call | tf_op jit(solution)/shard_map/pallas_call | solution.py:343
  481.6 9.1 %shard_map.265 = (bf16[288,2304]{1,0:T(8,128)(2,1)}, bf16[144,2304]{1,0:T(8,128)(2,1)}, bf16[144,2304]{1,0:T(8,128)(2,1)}, bf16[144,2304]{1,0:T(8,128)(2,1)}, bf...) custom-call(bf16[512,2304]{1,0:T(8,128)(2,1)} %get-tuple-element.679.a_h, ...), custom_call_target="tpu_custom_call" | custom-call | flops 999999995904 | tf_op jit(solution)/shard_map/pallas_call | solution.py:343
  497.0 8.5 %collective-permute-done.61.ra_r = bf16[144,2304]{1,0:T(8,128)(2,1)} collective-permute-done((bf16[144,2304]{1,0:T(8,128)(2,1)}, bf16[144,2304]{1,0:T(8,128)(2,1)}, u32[]{:S(2)}, u32[]{:S(2)}) %collective-permute-start.61) | collective-permute-done | bytes 663584 | tf_op jit(solution)/shard_map/ppermute | solution.py:50
  508.6 11.1 %collective-permute-done.59.rb_r = bf16[144,2304]{1,0:T(8,128)(2,1)} collective-permute-done((bf16[144,2304]{1,0:T(8,128)(2,1)}, bf16[144,2304]{1,0:T(8,128)(2,1)}, u32[]{:S(2)}, u32[]{:S(2)}) %collective-permute-start.59) | collective-permute-done | bytes 663584 | tf_op jit(solution)/shard_map/ppermute | solution.py:50
  530.1 19.1 %shard_map.270 = (f32[512,2304]{1,0:T(8,128)}, bf16[512,2304]{1,0:T(8,128)(2,1)}, bf16[512,512]{1,0:T(8,128)(2,1)}, f32[1024,512]{1,0:T(8,128)}, f32[8,2304]{1,0:T(8,128)}) custom-call(bf16[512,2304]{1,0:T(8,128)(2,1)} %all-gather.9.cloned.1.call-done.d_r, f32[512,2304]{1,0:T(8,128)} %get-tuple-element.707.x2_h.x_r, bf16[512,2304]{1,0:T(8,128)(2,1)} %shard_map.251.dy_h.dy_r, ...), custom_call_target="tpu_custom_call" | custom-call | flops 999999995904 | tf_op jit(solution)/shard_map/pallas_call | solution.py:120
  603.7 12.8 %collective-permute-done.73.qb_r = bf16[144,2304]{1,0:T(8,128)(2,1)S(1)} collective-permute-done((bf16[144,2304]{1,0:T(8,128)(2,1)}, bf16[144,2304]{1,0:T(8,128)(2,1)S(1)}, u32[]{:S(2)}, u32[]{:S(2)}) %collective-permute-start.73) | collective-permute-done | bytes 663584 | tf_op jit(solution)/shard_map/ppermute | solution.py:54
  (478 shorter events, 354.4 us)
Async XLA Ops:
  7.2 147.6 %reduce-scatter.5.cloned.1.call-start = ((), (), s32[]{:S(2)}) async-start(), calls=%async_computation.4 | async-start | bytes 2949120 | tf_op jit(solution)/shard_map/reduce_scatter | solution.py:730
  15.8 35.5 %collective-permute-start.5 = (bf16[304,1536]{1,0:T(8,128)(2,1)S(1)}, bf16[304,1536]{1,0:T(8,128)(2,1)}, u32[]{:S(2)}, u32[]{:S(2)}) collective-permute-start(bf16[304,1536]{1,0:T(8,128)(2,1)S(1)} %pad_maximum_fusion.refs_0_), channel_id=1, source_target_pairs={{0,8},{8,0},{1,9},{9,1},{2,10},{10,2},{3,11},{11,3},{4,12},{12,4},... | collective-permute-start | bytes 2801672 | tf_op jit(solution)/shard_map/ppermute | solution.py:58
  87.3 123.4 %all-gather.5.cloned.1.call-start = ((), (), s32[]{:S(2)}) async-start(), calls=%async_computation.5 | async-start | bytes 2949120 | tf_op jit(solution)/shard_map/all_gather | solution.py:737
  115.8 38.0 %collective-permute-start.16 = (bf16[288,2304]{1,0:T(8,128)(2,1)}, bf16[288,2304]{1,0:T(8,128)(2,1)S(1)}, u32[]{:S(2)}, u32[]{:S(2)}) collective-permute-start(bf16[288,2304]{1,0:T(8,128)(2,1)} %refs_0_), channel_id=1, source_target_pairs={{0,16},{16,0},{1,17},{17,1},{2,18},{18,2},{3,19},{19,3},{4,20},{20... | collective-permute-start | bytes 3981320 | tf_op jit(solution)/shard_map/ppermute | solution.py:54
  117.3 36.5 %collective-permute-start.15 = (bf16[288,2304]{1,0:T(8,128)(2,1)}, bf16[288,2304]{1,0:T(8,128)(2,1)S(1)}, u32[]{:S(2)}, u32[]{:S(2)}) collective-permute-start(bf16[288,2304]{1,0:T(8,128)(2,1)} %refs_0_), channel_id=1, source_target_pairs={{0,4},{4,0},{1,5},{5,1},{2,6},{6,2},{3,7},{7,3},{8,12},{12,8},{9,1... | collective-permute-start | bytes 3981320 | tf_op jit(solution)/shard_map/ppermute | solution.py:50
  154.8 150.3 %reduce-scatter.7.cloned.1.call-start = ((), (), s32[]{:S(2)}) async-start(), calls=%async_computation.6 | async-start | bytes 2949120 | tf_op jit(solution)/shard_map/reduce_scatter | solution.py:730
  173.1 30.7 %collective-permute-start.39 = (bf16[288,2304]{1,0:T(8,128)(2,1)}, bf16[288,2304]{1,0:T(8,128)(2,1)}, u32[]{:S(2)}, u32[]{:S(2)}) collective-permute-start(bf16[288,2304]{1,0:T(8,128)(2,1)} %refs_0_.1), channel_id=1, source_target_pairs={{0,16},{16,0},{1,17},{17,1},{2,18},{18,2},{3,19},{19,3},{4,20},{20... | collective-permute-start | bytes 3981320 | tf_op jit(solution)/shard_map/ppermute | solution.py:54
  257.0 99.6 %all-gather.7.cloned.1.call-start = ((), (), s32[]{:S(2)}) async-start(), calls=%async_computation.7 | async-start | bytes 2949120 | tf_op jit(solution)/shard_map/all_gather | solution.py:737
  305.1 167.7 %reduce-scatter.9.cloned.1.call-start = ((), (), s32[]{:S(2)}) async-start(), calls=%async_computation.8 | async-start | bytes 2949120 | tf_op jit(solution)/shard_map/reduce_scatter | solution.py:730
  411.5 118.5 %all-gather.9.cloned.1.call-start = ((), (), s32[]{:S(2)}) async-start(), calls=%async_computation.9 | async-start | bytes 2949120 | tf_op jit(solution)/shard_map/all_gather | solution.py:737
  425.0 37.1 %collective-permute-start.51 = (bf16[144,2304]{1,0:T(8,128)(2,1)}, bf16[144,2304]{1,0:T(8,128)(2,1)}, u32[]{:S(2)}, u32[]{:S(2)}) collective-permute-start(bf16[144,2304]{1,0:T(8,128)(2,1)} %get-tuple-element.644), channel_id=1, source_target_pairs={{0,4},{4,0},{1,5},{5,1},{2,6},{6,2},{3,7},{7,3},{8,12},{12,8},{9,1... | collective-permute-start | bytes 1990664 | tf_op jit(solution)/shard_map/ppermute | solution.py:50
  432.5 40.6 %collective-permute-start.68 = (bf16[288,2304]{1,0:T(8,128)(2,1)}, bf16[288,2304]{1,0:T(8,128)(2,1)S(1)}, u32[]{:S(2)}, u32[]{:S(2)}) collective-permute-start(bf16[288,2304]{1,0:T(8,128)(2,1)} %get-tuple-element.654), channel_id=1, source_target_pairs={{0,8},{8,0},{1,9},{9,1},{2,10},{10,2},{3,11},{11,3},{4,12},{12,4},... | collective-permute-start | bytes 3981320 | tf_op jit(solution)/shard_map/ppermute | solution.py:58
  439.6 35.1 %collective-permute-start.67 = (bf16[288,2304]{1,0:T(8,128)(2,1)}, bf16[288,2304]{1,0:T(8,128)(2,1)S(1)}, u32[]{:S(2)}, u32[]{:S(2)}) collective-permute-start(bf16[288,2304]{1,0:T(8,128)(2,1)} %get-tuple-element.653), channel_id=1, source_target_pairs={{0,8},{8,0},{1,9},{9,1},{2,10},{10,2},{3,11},{11,3},{4,12},{12,4},... | collective-permute-start | bytes 3981320 | tf_op jit(solution)/shard_map/ppermute | solution.py:58
  441.1 34.1 %collective-permute-start.66 = (bf16[288,2304]{1,0:T(8,128)(2,1)}, bf16[288,2304]{1,0:T(8,128)(2,1)}, u32[]{:S(2)}, u32[]{:S(2)}) collective-permute-start(bf16[288,2304]{1,0:T(8,128)(2,1)} %get-tuple-element.652), channel_id=1, source_target_pairs={{0,8},{8,0},{1,9},{9,1},{2,10},{10,2},{3,11},{11,3},{4,12},{12,4},... | collective-permute-start | bytes 3981320 | tf_op jit(solution)/shard_map/ppermute | solution.py:58
  472.9 174.9 %reduce-scatter.11.cloned.1.call-start = ((), (), s32[]{:S(2)}) async-start(), calls=%async_computation.10 | async-start | bytes 2949120 | tf_op jit(solution)/shard_map/reduce_scatter | solution.py:730
  475.8 32.8 %collective-permute-start.60 = (bf16[144,2304]{1,0:T(8,128)(2,1)}, bf16[144,2304]{1,0:T(8,128)(2,1)}, u32[]{:S(2)}, u32[]{:S(2)}) collective-permute-start(bf16[144,2304]{1,0:T(8,128)(2,1)} %shard_map.264), channel_id=1, source_target_pairs={{0,16},{16,0},{1,17},{17,1},{2,18},{18,2},{3,19},{19,3},{4,20},{20... | collective-permute-start | bytes 1990664 | tf_op jit(solution)/shard_map/ppermute | solution.py:54
  480.1 39.6 %collective-permute-start.59 = (bf16[144,2304]{1,0:T(8,128)(2,1)}, bf16[144,2304]{1,0:T(8,128)(2,1)}, u32[]{:S(2)}, u32[]{:S(2)}) collective-permute-start(bf16[144,2304]{1,0:T(8,128)(2,1)} %shard_map.263), channel_id=1, source_target_pairs={{0,4},{4,0},{1,5},{5,1},{2,6},{6,2},{3,7},{7,3},{8,12},{12,8},{9,1... | collective-permute-start | bytes 1990664 | tf_op jit(solution)/shard_map/ppermute | solution.py:50
  492.9 64.9 %collective-permute-start.71 = (bf16[144,2304]{1,0:T(8,128)(2,1)}, bf16[144,2304]{1,0:T(8,128)(2,1)}, u32[]{:S(2)}, u32[]{:S(2)}) collective-permute-start(bf16[144,2304]{1,0:T(8,128)(2,1)} %get-tuple-element.693), channel_id=1, source_target_pairs={{0,16},{16,0},{1,17},{17,1},{2,18},{18,2},{3,19},{19,3},{4,20},{20... | collective-permute-start | bytes 1990664 | tf_op jit(solution)/shard_map/ppermute | solution.py:54
  496.5 63.4 %collective-permute-start.70 = (bf16[144,2304]{1,0:T(8,128)(2,1)}, bf16[144,2304]{1,0:T(8,128)(2,1)}, u32[]{:S(2)}, u32[]{:S(2)}) collective-permute-start(bf16[144,2304]{1,0:T(8,128)(2,1)} %get-tuple-element.692), channel_id=1, source_target_pairs={{0,4},{4,0},{1,5},{5,1},{2,6},{6,2},{3,7},{7,3},{8,12},{12,8},{9,1... | collective-permute-start | bytes 1990664 | tf_op jit(solution)/shard_map/ppermute | solution.py:50
  585.8 30.7 %collective-permute-start.73 = (bf16[144,2304]{1,0:T(8,128)(2,1)}, bf16[144,2304]{1,0:T(8,128)(2,1)S(1)}, u32[]{:S(2)}, u32[]{:S(2)}) collective-permute-start(bf16[144,2304]{1,0:T(8,128)(2,1)} %get-tuple-element.726), channel_id=1, source_target_pairs={{0,16},{16,0},{1,17},{17,1},{2,18},{18,2},{3,19},{19,3},{4,20},{20... | collective-permute-start | bytes 1990664 | tf_op jit(solution)/shard_map/ppermute | solution.py:54
  588.5 107.8 %all-gather.11.cloned.1.call-start = ((), (), s32[]{:S(2)}) async-start(), calls=%async_computation.11 | async-start | bytes 2949120 | tf_op jit(solution)/shard_map/all_gather | solution.py:737
  593.0 32.1 %collective-permute-start.86 = (bf16[144,2304]{1,0:T(8,128)(2,1)}, bf16[144,2304]{1,0:T(8,128)(2,1)}, u32[]{:S(2)}, u32[]{:S(2)}) collective-permute-start(bf16[144,2304]{1,0:T(8,128)(2,1)} %shard_map.266), channel_id=1, source_target_pairs={{0,4},{4,0},{1,5},{5,1},{2,6},{6,2},{3,7},{7,3},{8,12},{12,8},{9,1... | collective-permute-start | bytes 1990664 | tf_op jit(solution)/shard_map/ppermute | solution.py:50
  593.6 49.4 %collective-permute-start.83 = (bf16[144,2304]{1,0:T(8,128)(2,1)}, bf16[144,2304]{1,0:T(8,128)(2,1)}, u32[]{:S(2)}, u32[]{:S(2)}) collective-permute-start(bf16[144,2304]{1,0:T(8,128)(2,1)} %shard_map.273), channel_id=1, source_target_pairs={{0,16},{16,0},{1,17},{17,1},{2,18},{18,2},{3,19},{19,3},{4,20},{20... | collective-permute-start | bytes 1990664 | tf_op jit(solution)/shard_map/ppermute | solution.py:54
  602.2 40.8 %collective-permute-start.82 = (bf16[144,2304]{1,0:T(8,128)(2,1)}, bf16[144,2304]{1,0:T(8,128)(2,1)}, u32[]{:S(2)}, u32[]{:S(2)}) collective-permute-start(bf16[144,2304]{1,0:T(8,128)(2,1)} %shard_map.272), channel_id=1, source_target_pairs={{0,4},{4,0},{1,5},{5,1},{2,6},{6,2},{3,7},{7,3},{8,12},{12,8},{9,1... | collective-permute-start | bytes 1990664 | tf_op jit(solution)/shard_map/ppermute | solution.py:50
  (169 other events, 2073.9 us)
Sparse Core Ops, SparseCore 0:
  87.4 48.8 reduce-scatter.4
  154.9 50.2 all-gather.4
  257.1 47.9 reduce-scatter.6
  306.5 49.9 all-gather.6
  411.7 46.9 reduce-scatter.8
  473.0 48.3 all-gather.8
  588.7 45.7 reduce-scatter.10
  647.9 48.3 all-gather.10

commit v4 on v3

--- a/solution.py
+++ b/solution.py
@@ -125,38 +125,13 @@
         out_shape=[jax.ShapeDtypeStruct(*e[:2]) for e in outs],
         scratch_shapes=list(scratch),
         cost_estimate=cost,
+        name=body.__qualname__.split(".")[0],
         compiler_params=pltpu.CompilerParams(vmem_limit_bytes=VMEM_MB * 2**20),
     )(*[e[0] for e in ins])
 
 
 def all_of(shape):
     return tuple(shape), lambda *i: (0,) * len(shape), pl.Buffered(1)
-
-
-def stack_kernel(*pieces, outs, plan, cost=NO_COST):
-    sets, n = len(plan), len(pieces)
-    widths = [pieces[p[0][0]].shape[1] for p in plan]
-    bc = math.gcd(*widths, 768)
-    first = [sum(widths[:i]) // bc for i in range(sets + 1)]
-
-    def body(*refs):
-        for i, copies in enumerate(plan):
-
-            @pl.when((pl.program_id(0) >= first[i]) & (pl.program_id(0) < first[i + 1]))
-            def _(copies=copies):
-                for p, o, r0, r, at in copies:
-                    refs[n + o][at : at + r, :] = refs[p][r0 : r0 + r, :]
-
-    ins = []
-    for i, copies in enumerate(plan):
-        lo, count = first[i], first[i + 1] - first[i]
-        for p in sorted({e[0] for e in copies}):
-            tile = (pieces[p].shape[0], bc)
-            ins.append((p, tile, lambda j, lo=lo, c=count: (0, jnp.clip(j - lo, 0, c - 1))))
-    ins = [(pieces[p], t, m) for p, t, m in sorted(ins, key=lambda e: e[0])]
-    tile = lambda r: ((r, bc), lambda j: (0, j))
-    outs = [((r, sum(widths)), LOW, *tile(r)) for r in outs]
-    return kernel(body, (first[-1],), ins, outs, cost=cost)
 
 
 def first_kernel(x, r, cos, sin, *pieces, plan, blk, qw, kw):
@@ -256,7 +231,7 @@
         ((rows, 128 * heads), F32, *row(128 * heads)),
         ((rows, width), LOW, *row(width)),
     ]
-    return kernel(body, (rows // qb,), ins, outs)
+    return kernel(body, (rows // qb,), ins, outs, cost=LONG)
 
 
 def attn_back_kernel(
@@ -339,7 +314,7 @@
 
 
 def streaming(body, ins, outs, scratch, copies, cost=NO_COST):
-    place = {"vmem": pl.BlockSpec(memory_space=pltpu.VMEM), "hbm": pl.BlockSpec(memory_space=pl.ANY)}
+    place = {"vmem": pl.BlockSpec(memory_space=pltpu.VMEM), "hbm": pl.BlockSpec(memory_space=pltpu.HBM)}
     return pl.pallas_call(
         body,
         in_specs=[place[p] for _, p in ins],
@@ -348,6 +323,7 @@
         scratch_shapes=[pltpu.VMEM(*v) for v in scratch]
         + [pltpu.SemaphoreType.DMA((copies,))],
         cost_estimate=cost,
+        name=body.__qualname__.split(".")[0],
         compiler_params=pltpu.CompilerParams(vmem_limit_bytes=VMEM_MB * 2**20),
     )(*[a for a, _ in ins])
 
@@ -356,36 +332,73 @@
     return [pl.ds(i, min(block, rows)) for i in range(0, rows, min(block, rows))]
 
 
-def row_tiles(mid, tile=384):
-    t = math.gcd(mid, tile)
-    tiles = [(k, i, k * mid + i, t) for k in range(2) for i in range(0, mid, t)]
-    return [tiles[i : i + 2] for i in range(0, len(tiles), 2)]
-
-
-def ffn_in_kernel(a, x, g2, g3, gm, gs, um, us):
+def col_chunks(where, total, most=768):
+    starts = sorted({c for _, c in where}) + [total]
+    chunks = []
+    for lo, hi in zip(starts, starts[1:]):
+        while lo < hi:
+            n = hi - lo if hi - lo <= most else min(most, -(-(hi - lo) // 2 // 128) * 128)
+            chunks.append((lo, n))
+            lo += n
+    return chunks
+
+
+def start_cols(c, name, j, chunk, pieces, shapes, where, dst):
+    names, (lo, n) = [], chunk
+    for i, (p, s, (row, col)) in enumerate(zip(pieces, shapes, where)):
+        if col <= lo < col + s[1]:
+            src = p.at[:, pl.ds(lo - col, n)]
+            c.start((name, j, i), src, dst.at[pl.ds(row, s[0]), pl.ds(lo, n)])
+            names.append((name, j, i))
+    return names
+
+
+def start_rows(c, name, pieces, shapes, where, dst):
+    names = []
+    for i in sorted(range(len(pieces)), key=lambda i: where[i]):
+        (row, col), s = where[i], shapes[i]
+        c.start((name, i), pieces[i], dst.at[pl.ds(row, s[0]), pl.ds(col, s[1])])
+        names.append((row, row + s[0], (name, i)))
+    return names
+
+
+def wait_rows(c, names, lo, hi, seen):
+    for first, last, name in names:
+        if first < hi and last > lo and name not in seen:
+            seen.add(name)
+            c.wait(name)
+
+
+def row_groups(rows, most=768):
+    return [(i, min(most, rows - i)) for i in range(0, rows, most)]
+
+
+def ffn_in_kernel(a, x, g2, g3, *weights, gate_at, up_at):
     rows, width = x.shape
-    mid, units = um.shape
-    bn = math.gcd(units, 768)
-    parts, cols = row_parts(rows), [pl.ds(i, bn) for i in range(0, units, bn)]
-
-    def body(
-        a_h, x_h, g2_r, g3_r, gm_h, gs_h, um_h, us_h,
-        x2_h, h_h, g_h, u_h, hid_h,
-        a_r, x_r, x2_r, h_r, wg_r, wu_r, g_r, u_r, hid_r, sems,
-    ):
+    ng = len(gate_at)
+    shapes = [w.shape for w in weights]
+    units = shapes[-1][1]
+    parts = row_parts(rows)
+    chunks = col_chunks(gate_at, units)
+
+    def body(a_h, x_h, g2_r, g3_r, *refs):
+        w_h, refs = refs[: len(shapes)], refs[len(shapes) :]
+        x2_h, h_h, g_h, u_h, hid_h = refs[:5]
+        a_r, x_r, x2_r, h_r, wg_r, wu_r, g_r, u_r, hid_r, sems = refs[5:]
         c = Copies(sems)
         for i, at in enumerate(parts):
             c.start(("a", i), a_h.at[at], a_r.at[at])
             c.start(("x", i), x_h.at[at], x_r.at[at])
-        for j, at in enumerate(cols):
-            for name, m, s, w in (("g", gm_h, gs_h, wg_r), ("u", um_h, us_h, wu_r)):
-                c.start((name, "m", j), m.at[:, at], w.at[pl.ds(0, mid), at])
-                c.start((name, "s", j), s.at[:, at], w.at[pl.ds(mid, mid), at])
+        need = []
+        for j, chunk in enumerate(chunks):
+            names = start_cols(c, "g", j, chunk, w_h[:ng], shapes[:ng], gate_at, wg_r)
+            names += start_cols(c, "u", j, chunk, w_h[ng:], shapes[ng:], up_at, wu_r)
+            need.append(names)
         out = []
 
         def send(src, dst, at):
-            out.append(len(out))
-            c.start(("out", out[-1]), src.at[at], dst.at[at])
+            out.append(("out", len(out)))
+            c.start(out[-1], src.at[at], dst.at[at])
 
         for i, part in enumerate(parts):
             c.wait(("a", i), ("x", i))
@@ -400,8 +413,9 @@
             over_rows(part.size, normed)
             send(x2_r, x2_h, (part,))
             send(h_r, h_h, (part,))
-        for j, at in enumerate(cols):
-            c.wait(("g", "m", j), ("g", "s", j), ("u", "m", j), ("u", "s", j))
+        for names, (lo, n) in zip(need, chunks):
+            c.wait(*names)
+            at = pl.ds(lo, n)
             h = h_r[...]
             gate, up = nn(h, wg_r[:, at]), nn(h, wu_r[:, at])
             g_r[:, at] = gate.astype(LOW)
@@ -409,129 +423,138 @@
             hid_r[:, at] = (gelu_parts(gate)[0] * up).astype(LOW)
             for src, dst in ((g_r, g_h), (u_r, u_h), (hid_r, hid_h)):
                 send(src, dst, (slice(None), at))
-        c.wait(*[("out", i) for i in out])
+        c.wait(*out)
 
     t, n = (rows, width), (rows, units)
     ins = [(a, "hbm"), (x, "hbm"), (g2, "vmem"), (g3, "vmem")]
-    ins += [(w, "hbm") for w in (gm, gs, um, us)]
-    outs = [(t, F32, "hbm"), (t, LOW, "hbm"), (n, LOW, "hbm"), (n, LOW, "hbm"), (n, LOW, "hbm")]
-    w = (2 * mid, units)
+    ins += [(w, "hbm") for w in weights]
+    outs = [(t, F32, "hbm"), (t, LOW, "hbm")] + [(n, LOW, "hbm")] * 3
+    w = (width, units)
     scratch = [(t, LOW), (t, LOW), (t, F32), (t, LOW), (w, LOW), (w, LOW)]
     scratch += [(n, LOW)] * 3
-    return streaming(body, ins, outs, scratch, 4 * len(parts) + 7 * len(cols))
-
-
-def project_kernel(u, wm, ws):
+    copies = 4 * len(parts) + (3 + len(weights)) * len(chunks)
+    return streaming(body, ins, outs, scratch, copies)
+
+
+def project_kernel(u, *weights, at):
     rows, cols = u.shape
-    mid = wm.shape[0]
-    groups = row_tiles(mid)
-
-    def body(u_r, m_h, s_h, o_h, w_r, o_r, sems):
+    shapes = [w.shape for w in weights]
+    width = sum(s[0] for s in shapes)
+    groups = row_groups(width)
+
+    def body(u_r, *refs):
+        w_h, (o_h, w_r, o_r, sems) = refs[: len(shapes)], refs[len(shapes) :]
         c = Copies(sems)
-        for g, tiles in enumerate(groups):
-            for k, i, at, n in tiles:
-                src = (m_h, s_h)[k].at[pl.ds(i, n)]
-                c.start((g, at), src, w_r.at[pl.ds(at, n)])
-        for g, tiles in enumerate(groups):
-            c.wait(*[(g, t[2]) for t in tiles])
-            at = pl.ds(tiles[0][2], sum(t[3] for t in tiles))
-            o_r[:, at] = nt(u_r[...], w_r[at, :]).astype(LOW)
-            c.start(("out", g), o_r.at[:, at], o_h.at[:, at])
+        names, seen = start_rows(c, "w", w_h, shapes, at, w_r), set()
+        for g, (lo, n) in enumerate(groups):
+            wait_rows(c, names, lo, lo + n, seen)
+            cut = pl.ds(lo, n)
+            o_r[:, cut] = nt(u_r[...], w_r[cut, :]).astype(LOW)
+            c.start(("out", g), o_r.at[:, cut], o_h.at[:, cut])
         c.wait(*[("out", g) for g in range(len(groups))])
 
-    ins = [(u, "vmem"), (wm, "hbm"), (ws, "hbm")]
-    outs = [((rows, 2 * mid), LOW, "hbm")]
-    scratch = [((2 * mid, cols), LOW), ((rows, 2 * mid), LOW)]
-    n = sum(map(len, groups)) + len(groups)
-    return streaming(body, ins, outs, scratch, n)[0]
-
-
-def ffn_back_kernel(f, x2, dy, g4, gate, up, dm, ds):
+    ins = [(u, "vmem")] + [(w, "hbm") for w in weights]
+    outs = [((rows, width), LOW, "hbm")]
+    scratch = [((width, cols), LOW), ((rows, width), LOW)]
+    return streaming(body, ins, outs, scratch, len(weights) + len(groups))[0]
+
+
+def ffn_back_kernel(f, x2, dy, g4, gate, up, *weights, at):
     rows, width = x2.shape
-    mid, units = dm.shape
-    bn = math.gcd(units, 768)
-    parts, cols = row_parts(rows), [pl.ds(i, bn) for i in range(0, units, bn)]
-
-    def body(
-        f_h, x2_h, dy_h, g4_r, gate_h, up_h, dm_h, ds_h,
-        y_h, df_h, dg_h, du_h, g_r,
-        f_r, x2_r, dy_r, gate_r, up_r, w_r, y_r, df_r, dg_r, du_r, sems,
-    ):
+    units = gate.shape[1]
+    shapes = [w.shape for w in weights]
+    parts = row_parts(rows)
+    chunks = col_chunks(at, units)
+
+    def body(f_h, x2_h, dy_h, g4_r, gate_h, up_h, *refs):
+        w_h, refs = refs[: len(shapes)], refs[len(shapes) :]
+        y_h, df_h, dg_h, du_h, g_r = refs[:5]
+        f_r, x2_r, dy_r, gate_r, up_r, w_r, y_r, df_r, dg_r, du_r, sems = refs[5:]
         c = Copies(sems)
-        for i, at in enumerate(parts):
+        for i, part in enumerate(parts):
             for name, src, dst in (("f", f_h, f_r), ("x", x2_h, x2_r), ("d", dy_h, dy_r)):
-                c.start((name, i), src.at[at], dst.at[at])
-        for j, at in enumerate(cols):
-            c.start(("m", j), dm_h.at[:, at], w_r.at[pl.ds(0, mid), at])
-            c.start(("s", j), ds_h.at[:, at], w_r.at[pl.ds(mid, mid), at])
-            c.start(("gate", j), gate_h.at[:, at], gate_r.at[:, at])
-            c.start(("up", j), up_h.at[:, at], up_r.at[:, at])
+                c.start((name, i), src.at[part], dst.at[part])
+        need = []
+        for j, (lo, n) in enumerate(chunks):
+            names = start_cols(c, "w", j, (lo, n), w_h, shapes, at, w_r)
+            cut = pl.ds(lo, n)
+            c.start(("gate", j), gate_h.at[:, cut], gate_r.at[:, cut])
+            c.start(("up", j), up_h.at[:, cut], up_r.at[:, cut])
+            need.append(names + [("gate", j), ("up", j)])
         out = []
 
-        def send(src, dst, at):
-            out.append(len(out))
-            c.start(("out", out[-1]), src.at[at], dst.at[at])
+        def send(src, dst, cut):
+            out.append(("out", len(out)))
+            c.start(out[-1], src.at[cut], dst.at[cut])
 
         total = jnp.zeros((8, width), F32)
         for i, part in enumerate(parts):
             c.wait(("f", i), ("x", i), ("d", i))
 
-            def step(at, total, first=part.start):
-                at = pl.ds(pl.multiple_of(first + at.start, 16), at.size)
-                fv, g4v, x2v = wide(f_r[at, :]), g4_r[...], x2_r[at, :]
-                y_r[at, :] = (x2v + fv * norm_factor(fv) * (1.0 + g4v)).astype(LOW)
-                df, dg = norm_back_rows(fv, g4v, wide(dy_r[at, :]))
-                df_r[at, :] = df.astype(LOW)
+            def step(cut, total, first=part.start):
+                cut = pl.ds(pl.multiple_of(first + cut.start, 16), cut.size)
+                fv, g4v, x2v = wide(f_r[cut, :]), g4_r[...], x2_r[cut, :]
+                y_r[cut, :] = (x2v + fv * norm_factor(fv) * (1.0 + g4v)).astype(LOW)
+                df, dg = norm_back_rows(fv, g4v, wide(dy_r[cut, :]))
+                df_r[cut, :] = df.astype(LOW)
                 return total + dg
 
             total = over_rows(part.size, step, total)
             send(y_r, y_h, (part,))
             send(df_r, df_h, (part,))
         g_r[...] = jnp.sum(total, axis=0, keepdims=True)
-        for j, at in enumerate(cols):
-            c.wait(("m", j), ("s", j), ("gate", j), ("up", j))
-            dh = nn(df_r[...], w_r[:, at])
-            gl, dgl = gelu_parts(wide(gate_r[:, at]))
-            dg_r[:, at] = (dh * wide(up_r[:, at]) * dgl).astype(LOW)
-            du_r[:, at] = (dh * gl).astype(LOW)
-            send(dg_r, dg_h, (slice(None), at))
-            send(du_r, du_h, (slice(None), at))
-        c.wait(*[("out", i) for i in out])
+        for names, (lo, n) in zip(need, chunks):
+            c.wait(*names)
+            cut = pl.ds(lo, n)
+            dh = nn(df_r[...], w_r[:, cut])
+            gl, dgl = gelu_parts(wide(gate_r[:, cut]))
+            dg_r[:, cut] = (dh * wide(up_r[:, cut]) * dgl).astype(LOW)
+            du_r[:, cut] = (dh * gl).astype(LOW)
+            send(dg_r, dg_h, (slice(None), cut))
+            send(du_r, du_h, (slice(None), cut))
+        c.wait(*out)
 
     t, n = (rows, width), (rows, units)
     ins = [(v, "hbm") for v in (f, x2, dy)] + [(g4, "vmem")]
-    ins += [(v, "hbm") for v in (gate, up, dm, ds)]
+    ins += [(v, "hbm") for v in (gate, up, *weights)]
     outs = [(t, LOW, "hbm"), (t, LOW, "hbm"), (n, LOW, "hbm"), (n, LOW, "hbm")]
     outs += [((1, width), F32, "vmem")]
-    scratch = [(t, LOW), (t, F32), (t, LOW), (n, LOW), (n, LOW), ((2 * mid, units), LOW)]
+    scratch = [(t, LOW), (t, F32), (t, LOW), (n, LOW), (n, LOW), ((width, units), LOW)]
     scratch += [(t, LOW), (t, LOW), (n, LOW), (n, LOW)]
-    return streaming(body, ins, outs, scratch, 5 * len(parts) + 6 * len(cols))
-
-
-def ffn_inputs_kernel(dg, du, gm, gs, um, us):
+    copies = 5 * len(parts) + (4 + len(weights)) * len(chunks)
+    return streaming(body, ins, outs, scratch, copies)
+
+
+def ffn_inputs_kernel(dg, du, *weights, gate_at, up_at):
     rows, units = dg.shape
-    mid = um.shape[0]
-    groups = row_tiles(mid)
-
-    def body(dg_r, du_r, gm_h, gs_h, um_h, us_h, o_h, wg_r, wu_r, o_r, sems):
+    ng = len(gate_at)
+    shapes = [w.shape for w in weights]
+    width = sum(s[0] for s in shapes[ng:])
+    groups = row_groups(width)
+
+    def body(dg_r, du_r, *refs):
+        w_h, (o_h, wg_r, wu_r, o_r, sems) = refs[: len(shapes)], refs[len(shapes) :]
         c = Copies(sems)
-        for g, tiles in enumerate(groups):
-            for k, i, at, n in tiles:
-                for name, src, dst in (("g", (gm_h, gs_h), wg_r), ("u", (um_h, us_h), wu_r)):
-                    c.start((name, g, at), src[k].at[pl.ds(i, n)], dst.at[pl.ds(at, n)])
-        for g, tiles in enumerate(groups):
-            c.wait(*[(name, g, t[2]) for t in tiles for name in "gu"])
-            at = pl.ds(tiles[0][2], sum(t[3] for t in tiles))
-            v = nt(dg_r[...], wg_r[at, :]) + nt(du_r[...], wu_r[at, :])
-            o_r[:, at] = v.astype(LOW)
-            c.start(("out", g), o_r.at[:, at], o_h.at[:, at])
+        order = sorted(range(len(shapes)), key=lambda i: (gate_at + up_at)[i][0])
+        names, seen = [], set()
+        for i in order:
+            (row, col), s = (gate_at + up_at)[i], shapes[i]
+            dst = (wg_r if i < ng else wu_r).at[pl.ds(row, s[0]), pl.ds(col, s[1])]
+            c.start(("w", i), w_h[i], dst)
+            names.append((row, row + s[0], ("w", i)))
+        for g, (lo, n) in enumerate(groups):
+            wait_rows(c, names, lo, lo + n, seen)
+            cut = pl.ds(lo, n)
+            v = nt(dg_r[...], wg_r[cut, :]) + nt(du_r[...], wu_r[cut, :])
+            o_r[:, cut] = v.astype(LOW)
+            c.start(("out", g), o_r.at[:, cut], o_h.at[:, cut])
         c.wait(*[("out", g) for g in range(len(groups))])
 
-    ins = [(dg, "vmem"), (du, "vmem")] + [(w, "hbm") for w in (gm, gs, um, us)]
-    outs = [((rows, 2 * mid), LOW, "hbm")]
-    w = ((2 * mid, units), LOW)
-    n = 2 * sum(map(len, groups)) + len(groups)
-    return streaming(body, ins, outs, [w, w, ((rows, 2 * mid), LOW)], n)[0]
+    ins = [(dg, "vmem"), (du, "vmem")] + [(w, "hbm") for w in weights]
+    outs = [((rows, width), LOW, "hbm")]
+    w = ((width, units), LOW)
+    scratch = [w, w, ((rows, width), LOW)]
+    return streaming(body, ins, outs, scratch, len(weights) + len(groups))[0]
 
 
 def outer_kernel(a, b, *got, side, cuts, cost=NO_COST):
@@ -578,29 +601,32 @@
     return streaming(body, ins, outs, scratch, copies, cost)
 
 
-def sum_kernel(s, ra, rb, qa, qb):
+def sum_kernel(s, rx, ry):
     rows, cols = s.shape
-    h = ra.shape[0]
     bc = math.gcd(cols, 768)
 
-    def body(s_r, ra_r, rb_r, qa_r, qb_r, o_r):
-        o_r[:h] = wide(s_r[:h]) + wide(ra_r[...]) + wide(qa_r[...])
-        o_r[h:] = wide(s_r[h:]) + wide(rb_r[...]) + wide(qb_r[...])
-
-    tile = lambda r: ((r, bc), lambda j: (0, j))
-    ins = [(v, *tile(v.shape[0])) for v in (s, ra, rb, qa, qb)]
-    return kernel(body, (cols // bc,), ins, [((rows, cols), F32, *tile(rows))])[0]
-
-
-def add_kernel(a, b):
-    rows, cols = a.shape
-    bc = math.gcd(cols, 1152)
-
-    def body(a_r, b_r, o_r):
-        o_r[...] = (wide(a_r[...]) + wide(b_r[...])).astype(LOW)
+    def body(s_r, x_r, y_r, o_r):
+        o_r[...] = wide(s_r[...]) + wide(x_r[...]) + wide(y_r[...])
 
     tile = ((rows, bc), lambda j: (0, j))
-    return kernel(body, (cols // bc,), [(a, *tile), (b, *tile)], [(a.shape, LOW, *tile)])[0]
+    ins = [(v, *tile) for v in (s, rx, ry)]
+    return kernel(body, (cols // bc,), ins, [((rows, cols), F32, *tile)])[0]
+
+
+def pass_kernel(s1, s2, gx, gy):
+    rows, cols = s1.shape
+    h = rows // 2
+    bc = math.gcd(cols, 768)
+
+    def body(s1_r, s2_r, gx_r, gy_r, t1_r, t2_r):
+        t1_r[:h] = s1_r[:h]
+        t1_r[h:] = (wide(s1_r[h:]) + wide(gy_r[...])).astype(LOW)
+        t2_r[:h] = (wide(s2_r[:h]) + wide(gx_r[...])).astype(LOW)
+        t2_r[h:] = s2_r[h:]
+
+    full, part = ((rows, bc), lambda j: (0, j)), ((h, bc), lambda j: (0, j))
+    ins = [(s1, *full), (s2, *full), (gx, *part), (gy, *part)]
+    return kernel(body, (cols // bc,), ins, [(s1.shape, LOW, *full)] * 2)
 
 
 def last_kernel(x, gain, dh1, dx2):
@@ -761,20 +787,21 @@
                     self.mine[3:] = seq(*self.mine[3:])
                     self.other += [seq.send(to_core, d) for d in self.mine[3:]]
 
-        def stack(*weights, cost=NO_COST):
-            pieces, plans = [], []
-            for weight in weights:
-                plan = []
-                for o, side in enumerate((weight.mine, weight.other)):
-                    at = 0
-                    for p in side:
-                        plan.append((len(pieces), o, 0, p.shape[0], at))
-                        at += p.shape[0]
-                        pieces.append(p)
-                plans.append(plan)
-            return seq.run(
-                stack_kernel, *pieces, outs=[plane * blk] * 2, plan=plans, cost=cost
-            )
+        def settle(*values):
+            values = seq(*values)
+            seq.last = tuple(values)
+            return list(values)
+
+        def placed(*weights):
+            pieces, where, col = [], [], 0
+            for w in weights:
+                at = 0
+                for p in w.mine + w.other:
+                    pieces.append(p)
+                    where.append((at, col))
+                    at += p.shape[0]
+                col += w.w.shape[1]
+            return pieces, where
 
         def packet_plan():
             pieces, plan, full, device = [], [], packet.w.shape[0], 0
@@ -822,9 +849,7 @@
 
         x_raw = layer_input.reshape(toks, width)
         dy_raw = out_cotangent.reshape(toks, width)
-        half_w = gate_weight.shape[1] * 4 // 9 // 128 * 128
-        wga, wgb = Weight(gate_weight[:, :half_w]), Weight(gate_weight[:, half_w:])
-        wu, wd = Weight(up_weight), Weight(down_weight)
+        wg, wu, wd = Weight(gate_weight), Weight(up_weight), Weight(down_weight)
 
         packet.near()
         if square:
@@ -835,7 +860,7 @@
         packet.far()
         allowed, cos, sin = seq.run(positions, info)
         packet.core()
-        wga.near()
+        wg.near()
         pieces, plan = packet_plan()
         h1, q, kv, gain, w_qkv, w_out = seq.run(
             first_kernel, x, factors, cos, sin, *pieces, plan=plan, blk=blk, qw=qw, kw=kw
@@ -843,8 +868,7 @@
         g1, g2, g3, g4 = [gain[i : i + 1] for i in range(4)]
         if square:
             kv_got = seq.send(to_ctx, kv)
-            wga.far()
-            wgb.near()
+            wg.far()
             kv_all = seq.run(lambda a, b: jnp.concatenate([a, b], 0), kv, kv_got)
         else:
             kv_all = lax.all_gather(kv, "ctx", axis=0, tiled=True)
@@ -852,63 +876,54 @@
 
         o, logs, part = seq.run(attn_kernel, q, kv_all, allowed, w_out)
         za = ZSum(part)
-        wgb.far()
+        if square:
+            wg.mine[3:] = settle(*wg.mine[3:])
         wu.near()
-        wga.core()
-        wgb.core()
-        gate_w = stack(wga, wgb)
-        wd.near()
+        wg.core()
         wu.far()
         za.middle()
+        dy = seq.run(order, dy_raw)
+        if square:
+            wu.mine[3:] = settle(*wu.mine[3:])
+        wd.near()
         wu.core()
-        up_m, up_s = stack(wu)
-        dy = seq.run(order, dy_raw)
         wd.far()
+        gate_p, gate_at = placed(wg)
+        up_p, up_at = placed(wu)
         x2, h3, gate, up, hid = seq.run(
-            ffn_in_kernel, za.out, x, g2, g3, *gate_w, up_m, up_s
+            ffn_in_kernel, za.out, x, g2, g3, *gate_p, *up_p, gate_at=gate_at, up_at=up_at
         )
         wd.core()
-        down_m, down_s = stack(wd)
-        part = seq.run(project_kernel, hid, down_m, down_s)
+        down_p, down_at = placed(wd)
+        part = seq.run(project_kernel, hid, *down_p, at=down_at)
         zf = ZSum(part)
         zf.middle()
         qkv_g = seq.run(row_order, w_qkv)
         g1_g = seq.run(order, jnp.broadcast_to(g1, (16, width)), back=True)[:1]
 
         y, df, dgate, dup, dg4 = seq.run(
-            ffn_back_kernel, zf.out, x2, dy, g4, gate, up, down_m, down_s
+            ffn_back_kernel, zf.out, x2, dy, g4, gate, up, *down_p, at=down_at
         )
-        part = seq.run(ffn_inputs_kernel, dgate, dup, *gate_w, up_m, up_s)
+        part = seq.run(
+            ffn_inputs_kernel, dgate, dup, *gate_p, *up_p, gate_at=gate_at, up_at=up_at
+        )
         zd = ZSum(part)
 
         class Scatter:
             def __init__(self, a, b):
                 self.ab = a, b
 
-            def low(self, cost=NO_COST):
-                cuts = [blk] * 4 if square else [mid]
-                low = seq.run(outer_kernel, *self.ab, side=1, cuts=cuts, cost=cost)
+            def low(self):
+                low = seq.run(outer_kernel, *self.ab, side=1, cuts=[mid // 2] * 2)
                 self.got = [seq.send(to_core, v) for v in low]
 
-            def first(self, cost=NO_COST):
+            def first(self):
                 h = blk // 2
-                cuts = [blk] + [h] * 6 if square else [mid]
-                self.s = seq.run(
-                    outer_kernel, *self.ab, *self.got, side=0, cuts=cuts, cost=cost
-                )
+                cuts = [blk] * 3 + [h, h] if square else [mid]
+                self.s = seq.run(outer_kernel, *self.ab, *self.got, side=0, cuts=cuts)
                 if square:
-                    self.gx = seq.send(to_ctx, self.s[5])
-                    self.gy = seq.send(to_y, self.s[6])
-
-            def plain(self):
-                if square:
-                    self.xa = seq.send(to_ctx, self.s[1])
-                    self.yb = seq.send(to_y, self.s[4])
-
-            def wait(self):
-                if square:
-                    self.xa, self.yb = seq(self.xa, self.yb)
-                    seq.last = (self.xa, self.yb)
+                    self.gx = seq.send(to_ctx, self.s[3])
+                    self.gy = seq.send(to_y, self.s[4])
 
             def second(self):
                 if not square:
@@ -916,34 +931,23 @@
                         self.s[0], ("y", "ctx"), scatter_dimension=0, tiled=True
                     )
                     return
-                t1 = seq.run(add_kernel, self.s[2], self.gy)
-                self.xb = seq.send(to_ctx, t1)
-                t2 = seq.run(add_kernel, self.s[3], self.gx)
-                self.ya = seq.send(to_y, t2)
+                s1, s2 = seq.run(pass_kernel, *self.s[1:3], self.gx, self.gy)
+                self.rest = seq.send(to_ctx, s1), seq.send(to_y, s2)
 
             def end(self):
                 if not square:
                     return wide(self.rest)
-                return seq.run(
-                    sum_kernel, self.s[0], self.xa, self.xb, self.ya, self.yb
-                )
+                return seq.run(sum_kernel, self.s[0], *self.rest)
 
         sd, sg, su = Scatter(df, hid), Scatter(h3, dgate), Scatter(h3, dup)
         sd.low()
         sg.low()
         sd.first()
-        sd.plain()
-        su.low(cost=LONG)
+        su.low()
+        zd.middle()
         sg.first()
-        sg.plain()
         sd.second()
-        sd.wait()
-        zd.middle()
-        su.first(cost=LONG)
-        sg.second()
-        sg.wait()
-        down_grad = sd.end()
-        layer_output = seq.run(order, y, back=True)
+        su.got = settle(*su.got)
 
         dx2, da, dq, dkv, dg23 = seq.run(
             attn_back_kernel, zd.out, x2, dy, za.out, g3, g2, w_out,
@@ -957,32 +961,29 @@
                 dkv.astype(LOW), "ctx", scatter_dimension=0, tiled=True
             )
             own = jnp.zeros((toks, 2 * kw), F32)
-        su.plain()
-        so = Scatter(da, o)
-        so.low(cost=LONG)
-        su.second()
+        sg.second()
+        down_grad = sd.end()
         dkv_low = seq.run(keys_back_kernel, own, got, cos, sin)
         dqkv = seq.run(lambda a, b: jnp.concatenate([a, b], 1), dq, dkv_low)
-        part = seq.run(project_kernel, dqkv, qkv_g[:mid], qkv_g[mid:])
+        part = seq.run(project_kernel, dqkv, qkv_g, at=[(0, 0)])
         z1 = ZSum(part)
-        sq = Scatter(h1, dqkv)
+        so, sq = Scatter(da, o), Scatter(h1, dqkv)
+        su.first()
+        so.low()
         sq.low()
+        dx2 = seq.run(order, dx2, back=True)
+        gate_grad = sg.end()
+        su.second()
+        z1.middle()
         so.first()
-        so.plain()
-        sq.first(cost=LONG)
-        su.wait()
-        sq.plain()
-        gate_grad = sg.end()
-        dx2 = seq.run(order, dx2, back=True)
+        sq.first()
         so.second()
         up_grad = su.end()
-        z1.middle()
-        so.wait()
         sq.second()
+        input_grad, dg1 = seq.run(last_kernel, x_raw, g1_g, z1.out, dx2)
+        layer_output = seq.run(order, y, back=True)
         out_grad = so.end()
-        sq.wait()
         qkv_grad = sq.end()
-        input_grad, dg1 = seq.run(last_kernel, x_raw, g1_g, z1.out, dx2)
         dg1 = order(jnp.broadcast_to(dg1, (16, width)))[:1]
         dgain = jnp.concatenate([dg1, dg23[:2], dg4], axis=0)
         dgain = dgain[:, :mid] + to_core(dgain[:, mid:])

time: 735 us -> 707 us (0.962)
  Pallas kernels: 301 us -> 271 us
  starting transfers between devices: 70.8 us -> 53.3 us
  local copies, waits for them, and re-layouts: 51.6 us -> 62.5 us
  waiting for transfers between devices: 279 us -> 287 us
    pallas_call x22 -> x14, Pallas kernels: 114 us -> 75.1 us  [kernel(): pl.pallas_call(body, grid=grid, in_specs=[spec(*e[1:]) for e in ins], out...]
    ppermute x29 -> x22, waiting for transfers between devices: 80.9 us -> 55.5 us  [to_ctx(): return lax.ppermute(a, 'ctx', SWAP)]
    all_gather x4, waiting for transfers between devices: 41.4 us -> 53.9 us  [middle(): self.out = lax.all_gather(own, 'tensor', axis=0, tiled=True)]
    reduce_scatter x4, waiting for transfers between devices: 48.1 us -> 60.3 us  [__init__(): self.own = lax.psum_scatter(part, 'tensor', scatter_dimension=0, tiled=True)]
    unnamed x170 -> x130, local copies, waits for them, and re-layouts: 10.6 us -> 22.1 us
    pallas_call x16, Pallas kernels: 157 us -> 166 us  [streaming(): pl.pallas_call(body, in_specs=[place[p] for _, p in ins], out_specs=[plac...]
    ppermute x26 -> x19, starting transfers between devices: 29 us -> 21.6 us  [to_y(): return lax.ppermute(a, 'y', SWAP)]
    ppermute x29 -> x22, starting transfers between devices: 31.7 us -> 25.5 us  [to_ctx(): return lax.ppermute(a, 'ctx', SWAP)]
  transfers between devices with their start and end apart: 109 -> 80, of which waited for: 42 -> 33; matrix products, arithmetic and copies ran while one was open for 6% -> 6% of each run, Pallas kernels for 30% -> 28%
where the time goes in v4:
time: 707 us; the launch traced here: 697 us
  waiting for transfers between devices  287 us (41%)
  Pallas kernels  271 us (38%)
  local copies, waits for them, and re-layouts  62.5 us (9%)
  starting transfers between devices  53.3 us (8%)
  between operations  15.3 us (2%)
  other arithmetic  7.41 us (1%)
    pallas_call x16, Pallas kernels, streaming(): pl.pallas_call(body, in_specs=[place[p] for _, p in ins], out_specs=[plac...  166 us
    ppermute x19, waiting for transfers between devices, to_y(): return lax.ppermute(a, 'y', SWAP)  101 us
    pallas_call x14, Pallas kernels, kernel(): pl.pallas_call(body, grid=grid, in_specs=[spec(*e[1:]) for e in ins], out...  75.1 us
    reduce_scatter x4, waiting for transfers between devices, __init__(): self.own = lax.psum_scatter(part, 'tensor', scatter_dimension=0, tiled=True)  60.3 us
    ppermute x22, waiting for transfers between devices, to_ctx(): return lax.ppermute(a, 'ctx', SWAP)  55.5 us
    all_gather x4, waiting for transfers between devices, middle(): self.out = lax.all_gather(own, 'tensor', axis=0, tiled=True)  53.9 us
    pallas_call x6, Pallas kernels, order_kernel(): pl.pallas_call(body, grid=(rows // br,), in_specs=[pl.BlockSpec(memory_sp...  29.6 us
    ppermute x22, starting transfers between devices, to_ctx(): return lax.ppermute(a, 'ctx', SWAP)  25.5 us
  transfers between devices with their start and end apart: 80, of which 33 were waited for; matrix products, arithmetic and copies ran while one was open for 6% of the time, Pallas kernels for 28%

profile of v4, /device:TPU:0, one launch (start us, length us, event | category | flops | bytes accessed | tf_op | source)
XLA Modules:
  0.0 696.8 jit_solution(7555920819427022957)
XLA Ops:
  24.2 12.4 %collective-permute-done = s32[3,512]{1,0:T(4,128)S(1)} collective-permute-done((s32[3,512]{1,0:T(4,128)S(1)}, s32[3,512]{1,0:T(4,128)S(1)}, u32[]{:S(2)}, u32[]{:S(2)}) %collective-permute-start) | collective-permute-done | bytes 6176 | tf_op jit(solution)/shard_map/ppermute | solution.py:50
  54.5 9.6 %first_kernel.1 = (bf16[512,2304]{1,0:T(8,128)(2,1)}, bf16[512,512]{1,0:T(8,128)(2,1)}, bf16[512,512]{1,0:T(8,128)(2,1)}, f32[8,2304]{1,0:T(8,128)}, bf16[2304,1...) custom-call(bf16[512,2304]{1,0:T(8,128)(2,1)} %get-tuple-element.459.x_r.x_h, f32[512,128]{1,0:T(8,128)} %get-tuple-element.391.r_r, ...), custom_call_target="tpu_custom_call" | custom-call | flops 999999995904 | tf_op jit(solution)/shard_map/first_kernel/pallas_call | solution.py:318
  64.7 16.3 %collective-permute-done.12.refs_2_ = bf16[288,2304]{1,0:T(8,128)(2,1)} collective-permute-done((bf16[288,2304]{1,0:T(8,128)(2,1)}, bf16[288,2304]{1,0:T(8,128)(2,1)}, u32[]{:S(2)}, u32[]{:S(2)}) %collective-permute-start.12) | collective-permute-done | bytes 1327136 | tf_op jit(solution)/shard_map/ppermute | solution.py:54
  94.3 7.8 %attn_kernel.1 = (bf16[512,512]{1,0:T(8,128)(2,1)}, f32[512,256]{1,0:T(8,128)}, bf16[512,2304]{1,0:T(8,128)(2,1)}) custom-call(bf16[512,512]{1,0:T(8,128)(2,1)} %get-tuple-element.602.q_r, bf16[1024,512]{1,0:T(8,128)(2,1)} %copy-done.40, bf16[512,1024]{1,0:T(8,128)(2,1)} %and_convert_fusion.m_r, bf16[2304,512]{1,0:T(8,128)(2,1)} %get-tuple-element.601.w_r), custom_call_target="tpu_custom_call" | custom-call | flops 999999995904 | tf_op jit(solution)/shard_map/attn_kernel/pallas_call | solution.py:120
  105.2 13.6 %collective-permute-done.14.refs_4_ = bf16[144,2304]{1,0:T(8,128)(2,1)S(1)} collective-permute-done((bf16[144,2304]{1,0:T(8,128)(2,1)S(1)}, bf16[144,2304]{1,0:T(8,128)(2,1)S(1)}, u32[]{:S(2)}, u32[]{:S(2)}) %collective-permute-start.14) | collective-permute-done | bytes 663584 | tf_op jit(solution)/shard_map/ppermute | solution.py:50
  121.2 27.8 %collective-permute-done.16.refs_12_ = bf16[288,2304]{1,0:T(8,128)(2,1)S(1)} collective-permute-done((bf16[288,2304]{1,0:T(8,128)(2,1)}, bf16[288,2304]{1,0:T(8,128)(2,1)S(1)}, u32[]{:S(2)}, u32[]{:S(2)}) %collective-permute-start.16) | collective-permute-done | bytes 1327136 | tf_op jit(solution)/shard_map/ppermute | solution.py:54
  153.9 11.1 %collective-permute-done.23.refs_14_ = bf16[144,2304]{1,0:T(8,128)(2,1)} collective-permute-done((bf16[144,2304]{1,0:T(8,128)(2,1)}, bf16[144,2304]{1,0:T(8,128)(2,1)}, u32[]{:S(2)}, u32[]{:S(2)}) %collective-permute-start.23) | collective-permute-done | bytes 663584 | tf_op jit(solution)/shard_map/ppermute | solution.py:50
  177.2 28.3 %collective-permute-done.30.refs_2_ = bf16[288,2304]{1,0:T(8,128)(2,1)} collective-permute-done((bf16[288,2304]{1,0:T(8,128)(2,1)}, bf16[288,2304]{1,0:T(8,128)(2,1)}, u32[]{:S(2)}, u32[]{:S(2)}) %collective-permute-start.30) | collective-permute-done | bytes 1327136 | tf_op jit(solution)/shard_map/ppermute | solution.py:54
  215.2 21.1 %ffn_in_kernel.1 = (f32[512,2304]{1,0:T(8,128)}, bf16[512,2304]{1,0:T(8,128)(2,1)}, bf16[512,2304]{1,0:T(8,128)(2,1)}, bf16[512,2304]{1,0:T(8,128)(2,1)}, bf16[512,2304]{1,0:T(8,128)(2,1)}) custom-call(bf16[512,2304]{1,0:T(8,128)(2,1)} %all-gather.5.cloned.1.call-done.a_h.a_r, bf16[512,2304]{1,0:T(8,128)(2,1)} %get-tuple-element.459.x_r.x_h, ...), custom_call_target="tpu_custom_call" | custom-call | tf_op jit(solution)/shard_map/ffn_in_kernel/pallas_call | solution.py:318
  240.5 12.1 %project_kernel.2 = bf16[512,2304]{1,0:T(8,128)(2,1)} custom-call(bf16[512,2304]{1,0:T(8,128)(2,1)} %get-tuple-element.559.u_r.b_h, bf16[288,2304]{1,0:T(8,128)(2,1)} %refs_0_.2, bf16[288,2304]{1,0:T(8,128)(2,1)} %collective-permute-done.29.refs_1_, bf16[288,2304]{1,0:T(8,128)(2,1)} %collective-permute-done.30.refs_2_, ...), custom_call_target="tpu_custom_call" | custom-call | tf_op jit(solution)/shard_map/project_kernel/pallas_call | solution.py:318
  252.6 46.7 %reduce-scatter.7.cloned.1.call-done = bf16[128,2304]{1,0:T(8,128)(2,1)} async-done(((bf16[512,2304]{1,0:T(8,128)(2,1)}), bf16[128,2304]{1,0:T(8,128)(2,1)}) %reduce-scatter.7.cloned.1.call-update) | async-done | bytes 589840 | tf_op jit(solution)/shard_map/reduce_scatter | solution.py:756
  315.1 35.7 %all-gather.7.cloned.1.call-done.f_h = bf16[512,2304]{1,0:T(8,128)(2,1)} async-done(((bf16[128,2304]{1,0:T(8,128)(2,1)}), bf16[512,2304]{1,0:T(8,128)(2,1)}) %all-gather.7.cloned.1.call-update) | async-done | bytes 2359312 | tf_op jit(solution)/shard_map/all_gather | solution.py:763
  350.8 27.0 %ffn_back_kernel.1 = (bf16[512,2304]{1,0:T(8,128)(2,1)}, bf16[512,2304]{1,0:T(8,128)(2,1)}, bf16[512,2304]{1,0:T(8,128)(2,1)}, bf16[512,2304]{1,0:T(8,128)(2,1)}, f32[1,2304]{1,0:T(1,128)}) custom-call(bf16[512,2304]{1,0:T(8,128)(2,1)} %all-gather.7.cloned.1.call-done.f_h, f32[512,2304]{1,0:T(8,128)} %get-tuple-element.596.x2_h.x_r, ...), custom_call_target="tpu_custom_call" | custom-call | tf_op jit(solution)/shard_map/ffn_back_kernel/pallas_call | solution.py:318
  377.9 21.1 %ffn_inputs_kernel.1 = bf16[512,2304]{1,0:T(8,128)(2,1)} custom-call(bf16[512,2304]{1,0:T(8,128)(2,1)} %get-tuple-element.576.dg_r.b_h, bf16[512,2304]{1,0:T(8,128)(2,1)} %get-tuple-element.633.du_r.b_h, bf16[288,2304]{1,0:T(8,128)(2,1)} %refs_0_.3, bf16[288,2304]{1,0:T(8,128)(2,1)} %collective-permute-done.11.refs_1_, ...), custom_call_target="tpu_custom_call" | custom-call | tf_op jit(solution)/shard_map/ffn_inputs_kernel/pallas_call | solution.py:318
  416.4 9.1 %outer_kernel.12 = (bf16[288,2304]{1,0:T(8,128)(2,1)}, bf16[288,2304]{1,0:T(8,128)(2,1)}, bf16[288,2304]{1,0:T(8,128)(2,1)}, bf16[144,2304]{1,0:T(8,128)(2,1)}, bf16[144,2304]{1,0:T(8,128)(2,1)}) custom-call(bf16[512,2304]{1,0:T(8,128)(2,1)} %get-tuple-element.558.a_h, bf16[512,2304]{1,0:T(8,128)(2,1)} %get-tuple-element.559.u_r.b_h, ...), custom_call_target="tpu_custom_call" | custom-call | tf_op jit(solution)/shard_map/outer_kernel/pallas_call | solution.py:318
  432.5 13.5 %reduce-scatter.9.cloned.1.call-done = bf16[128,2304]{1,0:T(8,128)(2,1)} async-done(((bf16[512,2304]{1,0:T(8,128)(2,1)}), bf16[128,2304]{1,0:T(8,128)(2,1)}) %reduce-scatter.9.cloned.1.call-update) | async-done | bytes 589840 | tf_op jit(solution)/shard_map/reduce_scatter | solution.py:756
  460.5 9.1 %outer_kernel.14 = (bf16[288,2304]{1,0:T(8,128)(2,1)}, bf16[288,2304]{1,0:T(8,128)(2,1)}, bf16[288,2304]{1,0:T(8,128)(2,1)}, bf16[144,2304]{1,0:T(8,128)(2,1)}, bf16[144,2304]{1,0:T(8,128)(2,1)}) custom-call(bf16[512,2304]{1,0:T(8,128)(2,1)} %get-tuple-element.632.a_h, bf16[512,2304]{1,0:T(8,128)(2,1)} %get-tuple-element.576.dg_r.b_h, ...), custom_call_target="tpu_custom_call" | custom-call | tf_op jit(solution)/shard_map/outer_kernel/pallas_call | solution.py:318
  479.2 18.3 %all-gather.9.cloned.1.call-done.d_r = bf16[512,2304]{1,0:T(8,128)(2,1)} async-done(((bf16[128,2304]{1,0:T(8,128)(2,1)}), bf16[512,2304]{1,0:T(8,128)(2,1)}) %all-gather.9.cloned.1.call-update) | async-done | bytes 2359312 | tf_op jit(solution)/shard_map/all_gather | solution.py:763
  497.5 19.0 %attn_back_kernel.1 = (f32[512,2304]{1,0:T(8,128)}, bf16[512,2304]{1,0:T(8,128)(2,1)}, bf16[512,512]{1,0:T(8,128)(2,1)}, f32[1024,512]{1,0:T(8,128)}, f32[8,2304]{1,0:T(8,128)}) custom-call(bf16[512,2304]{1,0:T(8,128)(2,1)} %all-gather.9.cloned.1.call-done.d_r, f32[512,2304]{1,0:T(8,128)} %get-tuple-element.596.x2_h.x_r, ...), custom_call_target="tpu_custom_call" | custom-call | flops 999999995904 | tf_op jit(solution)/shard_map/attn_back_kernel/pallas_call | solution.py:120
  536.9 7.1 %project_kernel.3 = bf16[512,2304]{1,0:T(8,128)(2,1)} custom-call(bf16[512,1024]{1,0:T(8,128)(2,1)} %copy-done, bf16[2304,1024]{1,0:T(8,128)(2,1)} %slice_dynamic-update-slice_fusion.refs_0_), custom_call_target="tpu_custom_call" | custom-call | tf_op jit(solution)/shard_map/project_kernel/pallas_call | solution.py:318
  547.3 9.5 %outer_kernel.15 = (bf16[288,2304]{1,0:T(8,128)(2,1)}, bf16[288,2304]{1,0:T(8,128)(2,1)}, bf16[288,2304]{1,0:T(8,128)(2,1)}, bf16[144,2304]{1,0:T(8,128)(2,1)}, bf16[144,2304]{1,0:T(8,128)(2,1)}) custom-call(bf16[512,2304]{1,0:T(8,128)(2,1)} %get-tuple-element.632.a_h, bf16[512,2304]{1,0:T(8,128)(2,1)} %get-tuple-element.633.du_r.b_h, ...), custom_call_target="tpu_custom_call" | custom-call | tf_op jit(solution)/shard_map/outer_kernel/pallas_call | solution.py:318
  566.7 7.6 %shard_map.249.dx_r = f32[512,2304]{1,0:T(8,128)} custom-call(s32[3]{0:T(128)} %pad_add_fusion.2.b_r, f32[512,2304]{1,0:T(8,128)} %get-tuple-element.653.v_r), custom_call_target="tpu_custom_call" | custom-call | tf_op jit(solution)/shard_map/pallas_call | solution.py:682
  618.5 12.0 %collective-permute-done.64.gy_r = bf16[144,512]{1,0:T(8,128)(2,1)S(1)} collective-permute-done((bf16[144,512]{1,0:T(8,128)(2,1)}, bf16[144,512]{1,0:T(8,128)(2,1)S(1)}, u32[]{:S(2)}, u32[]{:S(2)}) %collective-permute-start.64) | collective-permute-done | bytes 147488 | tf_op jit(solution)/shard_map/ppermute | solution.py:54
  654.0 7.8 %last_kernel.1 = (f32[512,2304]{1,0:T(8,128)}, f32[1,2304]{1,0:T(1,128)}) custom-call(bf16[512,2304]{1,0:T(8,128)(2,1)} %bitcast.11, f32[1,2304]{1,0:T(1,128)} %slice.165.g_r, bf16[512,2304]{1,0:T(8,128)(2,1)} %all-gather.11.cloned.1.call-done.d_r, f32[512,2304]{1,0:T(8,128)} %shard_map.249.dx_r), custom_call_target="tpu_custom_call" | custom-call | tf_op jit(solution)/shard_map/last_kernel/pallas_call | solution.py:120
  (367 shorter events, 277.8 us)
Async XLA Ops:
  7.2 144.7 %reduce-scatter.5.cloned.1.call-start = ((), (), s32[]{:S(2)}) async-start(), calls=%async_computation.4 | async-start | bytes 2949120 | tf_op jit(solution)/shard_map/reduce_scatter | solution.py:756
  15.8 33.8 %collective-permute-start.5 = (bf16[304,1536]{1,0:T(8,128)(2,1)S(1)}, bf16[304,1536]{1,0:T(8,128)(2,1)}, u32[]{:S(2)}, u32[]{:S(2)}) collective-permute-start(bf16[304,1536]{1,0:T(8,128)(2,1)S(1)} %pad_maximum_fusion.refs_0_), channel_id=1, source_target_pairs={{0,8},{8,0},{1,9},{9,1},{2,10},{10,2},{3,11},{11,3},{4,12},{12,4},... | collective-permute-start | bytes 2801672 | tf_op jit(solution)/shard_map/ppermute | solution.py:58
  51.0 32.4 %collective-permute-start.11 = (bf16[288,2304]{1,0:T(8,128)(2,1)}, bf16[288,2304]{1,0:T(8,128)(2,1)}, u32[]{:S(2)}, u32[]{:S(2)}) collective-permute-start(bf16[288,2304]{1,0:T(8,128)(2,1)} %refs_0_.3), channel_id=1, source_target_pairs={{0,4},{4,0},{1,5},{5,1},{2,6},{6,2},{3,7},{7,3},{8,12},{12,8},{9,1... | collective-permute-start | bytes 3981320 | tf_op jit(solution)/shard_map/ppermute | solution.py:50
  102.1 113.1 %all-gather.5.cloned.1.call-start = ((), (), s32[]{:S(2)}) async-start(), calls=%async_computation.5 | async-start | bytes 2949120 | tf_op jit(solution)/shard_map/all_gather | solution.py:763
  121.2 52.4 %collective-permute-start.17 = (bf16[288,2304]{1,0:T(8,128)(2,1)}, bf16[288,2304]{1,0:T(8,128)(2,1)}, u32[]{:S(2)}, u32[]{:S(2)}) collective-permute-start(bf16[288,2304]{1,0:T(8,128)(2,1)} %refs_0_.3), channel_id=1, source_target_pairs={{0,8},{8,0},{1,9},{9,1},{2,10},{10,2},{3,11},{11,3},{4,12},{12,4},... | collective-permute-start | bytes 3981320 | tf_op jit(solution)/shard_map/ppermute | solution.py:58
  151.9 147.5 %reduce-scatter.7.cloned.1.call-start = ((), (), s32[]{:S(2)}) async-start(), calls=%async_computation.6 | async-start | bytes 2949120 | tf_op jit(solution)/shard_map/reduce_scatter | solution.py:756
  176.6 34.1 %collective-permute-start.24 = (bf16[288,2304]{1,0:T(8,128)(2,1)}, bf16[288,2304]{1,0:T(8,128)(2,1)S(1)}, u32[]{:S(2)}, u32[]{:S(2)}) collective-permute-start(bf16[288,2304]{1,0:T(8,128)(2,1)} %refs_10_.1), channel_id=1, source_target_pairs={{0,8},{8,0},{1,9},{9,1},{2,10},{10,2},{3,11},{11,3},{4,12},{12,4},... | collective-permute-start | bytes 3981320 | tf_op jit(solution)/shard_map/ppermute | solution.py:58
  176.6 35.5 %collective-permute-start.26 = (bf16[288,2304]{1,0:T(8,128)(2,1)S(1)}, bf16[288,2304]{1,0:T(8,128)(2,1)S(1)}, u32[]{:S(2)}, u32[]{:S(2)}) collective-permute-start(bf16[288,2304]{1,0:T(8,128)(2,1)S(1)} %collective-permute-done.16.refs_12_), channel_id=1, source_target_pairs={{0,8},{8,0},{1,9},{9,1},{2,10},{10,2},{3,11},{11,3},{4,12},{12,4},... | collective-permute-start | bytes 3981320 | tf_op jit(solution)/shard_map/ppermute | solution.py:58
  177.1 35.8 %collective-permute-start.25 = (bf16[288,2304]{1,0:T(8,128)(2,1)S(1)}, bf16[288,2304]{1,0:T(8,128)(2,1)S(1)}, u32[]{:S(2)}, u32[]{:S(2)}) collective-permute-start(bf16[288,2304]{1,0:T(8,128)(2,1)S(1)} %collective-permute-done.15.refs_11_), channel_id=1, source_target_pairs={{0,8},{8,0},{1,9},{9,1},{2,10},{10,2},{3,11},{11,3},{4,12},{12,4},... | collective-permute-start | bytes 3981320 | tf_op jit(solution)/shard_map/ppermute | solution.py:58
  252.6 98.2 %all-gather.7.cloned.1.call-start = ((), (), s32[]{:S(2)}) async-start(), calls=%async_computation.7 | async-start | bytes 2949120 | tf_op jit(solution)/shard_map/all_gather | solution.py:763
  299.4 146.6 %reduce-scatter.9.cloned.1.call-start = ((), (), s32[]{:S(2)}) async-start(), calls=%async_computation.8 | async-start | bytes 2949120 | tf_op jit(solution)/shard_map/reduce_scatter | solution.py:756
  399.0 98.4 %all-gather.9.cloned.1.call-start = ((), (), s32[]{:S(2)}) async-start(), calls=%async_computation.9 | async-start | bytes 2949120 | tf_op jit(solution)/shard_map/all_gather | solution.py:763
  446.1 148.4 %reduce-scatter.11.cloned.1.call-start = ((), (), s32[]{:S(2)}) async-start(), calls=%async_computation.10 | async-start | bytes 2949120 | tf_op jit(solution)/shard_map/reduce_scatter | solution.py:756
  446.8 32.4 %collective-permute-start.40 = (bf16[576,2304]{1,0:T(8,128)(2,1)}, bf16[576,2304]{1,0:T(8,128)(2,1)}, u32[]{:S(2)}, u32[]{:S(2)}) collective-permute-start(bf16[576,2304]{1,0:T(8,128)(2,1)} %get-tuple-element.572), channel_id=1, source_target_pairs={{0,8},{8,0},{1,9},{9,1},{2,10},{10,2},{3,11},{11,3},{4,12},{12,4},... | collective-permute-start | bytes 7962632 | tf_op jit(solution)/shard_map/ppermute | solution.py:58
  469.6 52.1 %collective-permute-start.49 = (bf16[144,2304]{1,0:T(8,128)(2,1)}, bf16[144,2304]{1,0:T(8,128)(2,1)}, u32[]{:S(2)}, u32[]{:S(2)}) collective-permute-start(bf16[144,2304]{1,0:T(8,128)(2,1)} %get-tuple-element.584), channel_id=1, source_target_pairs={{0,4},{4,0},{1,5},{5,1},{2,6},{6,2},{3,7},{7,3},{8,12},{12,8},{9,1... | collective-permute-start | bytes 1990664 | tf_op jit(solution)/shard_map/ppermute | solution.py:50
  471.1 50.6 %collective-permute-start.50 = (bf16[144,2304]{1,0:T(8,128)(2,1)}, bf16[144,2304]{1,0:T(8,128)(2,1)}, u32[]{:S(2)}, u32[]{:S(2)}) collective-permute-start(bf16[144,2304]{1,0:T(8,128)(2,1)} %get-tuple-element.585), channel_id=1, source_target_pairs={{0,16},{16,0},{1,17},{17,1},{2,18},{18,2},{3,19},{19,3},{4,20},{20... | collective-permute-start | bytes 1990664 | tf_op jit(solution)/shard_map/ppermute | solution.py:54
  477.8 48.2 %collective-permute-start.47 = (bf16[288,2304]{1,0:T(8,128)(2,1)}, bf16[288,2304]{1,0:T(8,128)(2,1)}, u32[]{:S(2)}, u32[]{:S(2)}) collective-permute-start(bf16[288,2304]{1,0:T(8,128)(2,1)} %get-tuple-element.591), channel_id=1, source_target_pairs={{0,4},{4,0},{1,5},{5,1},{2,6},{6,2},{3,7},{7,3},{8,12},{12,8},{9,1... | collective-permute-start | bytes 3981320 | tf_op jit(solution)/shard_map/ppermute | solution.py:50
  478.4 47.7 %collective-permute-start.48 = (bf16[288,2304]{1,0:T(8,128)(2,1)}, bf16[288,2304]{1,0:T(8,128)(2,1)}, u32[]{:S(2)}, u32[]{:S(2)}) collective-permute-start(bf16[288,2304]{1,0:T(8,128)(2,1)} %get-tuple-element.592), channel_id=1, source_target_pairs={{0,16},{16,0},{1,17},{17,1},{2,18},{18,2},{3,19},{19,3},{4,20},{20... | collective-permute-start | bytes 3981320 | tf_op jit(solution)/shard_map/ppermute | solution.py:54
  544.1 109.9 %all-gather.11.cloned.1.call-start = ((), (), s32[]{:S(2)}) async-start(), calls=%async_computation.11 | async-start | bytes 2949120 | tf_op jit(solution)/shard_map/all_gather | solution.py:763
  544.3 32.3 %collective-permute-start.54 = (bf16[288,2304]{1,0:T(8,128)(2,1)}, bf16[288,2304]{1,0:T(8,128)(2,1)S(1)}, u32[]{:S(2)}, u32[]{:S(2)}) collective-permute-start(bf16[288,2304]{1,0:T(8,128)(2,1)} %get-tuple-element.620), channel_id=1, source_target_pairs={{0,16},{16,0},{1,17},{17,1},{2,18},{18,2},{3,19},{19,3},{4,20},{20... | collective-permute-start | bytes 3981320 | tf_op jit(solution)/shard_map/ppermute | solution.py:54
  545.9 32.3 %collective-permute-start.53 = (bf16[288,2304]{1,0:T(8,128)(2,1)}, bf16[288,2304]{1,0:T(8,128)(2,1)S(1)}, u32[]{:S(2)}, u32[]{:S(2)}) collective-permute-start(bf16[288,2304]{1,0:T(8,128)(2,1)} %get-tuple-element.619), channel_id=1, source_target_pairs={{0,4},{4,0},{1,5},{5,1},{2,6},{6,2},{3,7},{7,3},{8,12},{12,8},{9,1... | collective-permute-start | bytes 3981320 | tf_op jit(solution)/shard_map/ppermute | solution.py:50
  557.4 32.7 %collective-permute-start.51 = (bf16[144,2304]{1,0:T(8,128)(2,1)}, bf16[144,2304]{1,0:T(8,128)(2,1)}, u32[]{:S(2)}, u32[]{:S(2)}) collective-permute-start(bf16[144,2304]{1,0:T(8,128)(2,1)} %get-tuple-element.641), channel_id=1, source_target_pairs={{0,4},{4,0},{1,5},{5,1},{2,6},{6,2},{3,7},{7,3},{8,12},{12,8},{9,1... | collective-permute-start | bytes 1990664 | tf_op jit(solution)/shard_map/ppermute | solution.py:50
  595.2 44.6 %collective-permute-start.62 = (bf16[288,2304]{1,0:T(8,128)(2,1)}, bf16[288,2304]{1,0:T(8,128)(2,1)S(1)}, u32[]{:S(2)}, u32[]{:S(2)}) collective-permute-start(bf16[288,2304]{1,0:T(8,128)(2,1)} %get-tuple-element.663), channel_id=1, source_target_pairs={{0,16},{16,0},{1,17},{17,1},{2,18},{18,2},{3,19},{19,3},{4,20},{20... | collective-permute-start | bytes 3981320 | tf_op jit(solution)/shard_map/ppermute | solution.py:54
  596.2 43.6 %collective-permute-start.61 = (bf16[288,2304]{1,0:T(8,128)(2,1)}, bf16[288,2304]{1,0:T(8,128)(2,1)S(1)}, u32[]{:S(2)}, u32[]{:S(2)}) collective-permute-start(bf16[288,2304]{1,0:T(8,128)(2,1)} %get-tuple-element.662), channel_id=1, source_target_pairs={{0,4},{4,0},{1,5},{5,1},{2,6},{6,2},{3,7},{7,3},{8,12},{12,8},{9,1... | collective-permute-start | bytes 3981320 | tf_op jit(solution)/shard_map/ppermute | solution.py:50
  (120 other events, 1502.6 us)
Sparse Core Ops, SparseCore 0:
  102.2 48.3 reduce-scatter.4
  152.2 51.3 all-gather.4
  252.7 46.6 reduce-scatter.6
  300.8 49.9 all-gather.6
  399.2 46.8 reduce-scatter.8
  447.5 49.9 all-gather.8
  544.2 46.9 reduce-scatter.10
  594.6 49.2 all-gather.10

commit v5 on v4

--- a/solution.py
+++ b/solution.py
@@ -235,18 +235,19 @@
 
 
 def attn_back_kernel(
-    dh3, x2, dy, a, g3, g2, w, q, kv, allowed, logs, cos, sin
+    dh3, x2, dy, a, g3, g2, w, q, kv, allowed, logs, cos, sin, toks
 ):
     rows, width = x2.shape
     qw = q.shape[1]
     length = kv.shape[0]
     qb = query_block(rows, length)
     heads = qw // HD
+    other = toks if length == 2 * toks else length
     scale = 1.0 / math.sqrt(HD)
 
     def body(
         d_r, x_r, dy_r, a_r, g3_r, g2_r, w_r, q_r, kv_r, m_r, t_r, c_r, s_r,
-        dx_r, da_r, dq_r, dkv_r, dg_r,
+        dx_r, da_r, dq_r, own_r, other_r, dg_r, dkv_r,
     ):
         @pl.when(pl.program_id(0) == 0)
         def _():
@@ -285,6 +286,11 @@
         dkv_r[:, :HD] += dk
         dkv_r[:, HD:] += dv
 
+        @pl.when(pl.program_id(0) == rows // qb - 1)
+        def _():
+            own_r[...] = dkv_r[:toks]
+            other_r[...] = dkv_r[length - other :].astype(LOW)
+
     row = lambda n: ((qb, n), lambda i: (i, 0))
     ins = [(v, *row(width)) for v in (dh3, x2, dy, a)]
     ins += [(v, *all_of(v.shape)) for v in (g3, g2, w)]
@@ -294,10 +300,12 @@
         ((rows, width), F32, *row(width)),
         ((rows, width), LOW, *row(width)),
         ((rows, qw), LOW, *row(qw)),
-        ((length, 2 * HD), F32, *all_of((length, 2 * HD))),
+        ((toks, 2 * HD), F32, *all_of((toks, 2 * HD))),
+        ((other, 2 * HD), LOW, *all_of((other, 2 * HD))),
         ((8, width), F32, *all_of((8, width))),
     ]
-    return kernel(body, (rows // qb,), ins, outs, cost=LONG)
+    scratch = [pltpu.VMEM((length, 2 * HD), F32)]
+    return kernel(body, (rows // qb,), ins, outs, scratch, LONG)
 
 
 class Copies:
@@ -383,8 +391,8 @@
 
     def body(a_h, x_h, g2_r, g3_r, *refs):
         w_h, refs = refs[: len(shapes)], refs[len(shapes) :]
-        x2_h, h_h, g_h, u_h, hid_h = refs[:5]
-        a_r, x_r, x2_r, h_r, wg_r, wu_r, g_r, u_r, hid_r, sems = refs[5:]
+        x2_h, h_h, gu_h, hid_h = refs[:4]
+        a_r, x_r, x2_r, h_r, wg_r, wu_r, gu_r, hid_r, sems = refs[4:]
         c = Copies(sems)
         for i, at in enumerate(parts):
             c.start(("a", i), a_h.at[at], a_r.at[at])
@@ -418,20 +426,22 @@
             at = pl.ds(lo, n)
             h = h_r[...]
             gate, up = nn(h, wg_r[:, at]), nn(h, wu_r[:, at])
-            g_r[:, at] = gate.astype(LOW)
-            u_r[:, at] = up.astype(LOW)
+            at2 = pl.ds(units + lo, n)
+            gu_r[:, at] = gate.astype(LOW)
+            gu_r[:, at2] = up.astype(LOW)
             hid_r[:, at] = (gelu_parts(gate)[0] * up).astype(LOW)
-            for src, dst in ((g_r, g_h), (u_r, u_h), (hid_r, hid_h)):
-                send(src, dst, (slice(None), at))
+            for src, dst, cut in ((gu_r, gu_h, at), (gu_r, gu_h, at2), (hid_r, hid_h, at)):
+                send(src, dst, (slice(None), cut))
         c.wait(*out)
 
     t, n = (rows, width), (rows, units)
     ins = [(a, "hbm"), (x, "hbm"), (g2, "vmem"), (g3, "vmem")]
     ins += [(w, "hbm") for w in weights]
-    outs = [(t, F32, "hbm"), (t, LOW, "hbm")] + [(n, LOW, "hbm")] * 3
+    gu = (rows, 2 * units)
+    outs = [(t, F32, "hbm"), (t, LOW, "hbm"), (gu, LOW, "hbm"), (n, LOW, "hbm")]
     w = (width, units)
     scratch = [(t, LOW), (t, LOW), (t, F32), (t, LOW), (w, LOW), (w, LOW)]
-    scratch += [(n, LOW)] * 3
+    scratch += [(gu, LOW), (n, LOW)]
     copies = 4 * len(parts) + (3 + len(weights)) * len(chunks)
     return streaming(body, ins, outs, scratch, copies)
 
@@ -459,14 +469,14 @@
     return streaming(body, ins, outs, scratch, len(weights) + len(groups))[0]
 
 
-def ffn_back_kernel(f, x2, dy, g4, gate, up, *weights, at):
+def ffn_back_kernel(f, x2, dy, g4, gate_up, *weights, at):
     rows, width = x2.shape
-    units = gate.shape[1]
+    units = gate_up.shape[1] // 2
     shapes = [w.shape for w in weights]
     parts = row_parts(rows)
-    chunks = col_chunks(at, units)
-
-    def body(f_h, x2_h, dy_h, g4_r, gate_h, up_h, *refs):
+    chunks = col_chunks(at, units, 1152)
+
+    def body(f_h, x2_h, dy_h, g4_r, gu_h, *refs):
         w_h, refs = refs[: len(shapes)], refs[len(shapes) :]
         y_h, df_h, dg_h, du_h, g_r = refs[:5]
         f_r, x2_r, dy_r, gate_r, up_r, w_r, y_r, df_r, dg_r, du_r, sems = refs[5:]
@@ -478,8 +488,9 @@
         for j, (lo, n) in enumerate(chunks):
             names = start_cols(c, "w", j, (lo, n), w_h, shapes, at, w_r)
             cut = pl.ds(lo, n)
-            c.start(("gate", j), gate_h.at[:, cut], gate_r.at[:, cut])
-            c.start(("up", j), up_h.at[:, cut], up_r.at[:, cut])
+            c.start(("gate", j), gu_h.at[:, cut], gate_r.at[:, cut])
+            up_at = pl.ds(units + lo, n)
+            c.start(("up", j), gu_h.at[:, up_at], up_r.at[:, cut])
             need.append(names + [("gate", j), ("up", j)])
         out = []
 
@@ -516,7 +527,7 @@
 
     t, n = (rows, width), (rows, units)
     ins = [(v, "hbm") for v in (f, x2, dy)] + [(g4, "vmem")]
-    ins += [(v, "hbm") for v in (gate, up, *weights)]
+    ins += [(v, "hbm") for v in (gate_up, *weights)]
     outs = [(t, LOW, "hbm"), (t, LOW, "hbm"), (n, LOW, "hbm"), (n, LOW, "hbm")]
     outs += [((1, width), F32, "vmem")]
     scratch = [(t, LOW), (t, F32), (t, LOW), (n, LOW), (n, LOW), ((width, units), LOW)]
@@ -692,14 +703,18 @@
     )(bits, v)
 
 
-def keys_back_kernel(own, got, cos, sin):
-    def body(a_r, b_r, c_r, s_r, o_r):
+def keys_back_kernel(own, got, cos, sin, dq):
+    qw = dq.shape[1]
+
+    def body(a_r, b_r, c_r, s_r, q_r, o_r):
         v = a_r[...] + wide(b_r[...])
-        o_r[:, :HD] = turn_back(v[:, :HD], c_r[...], s_r[...]).astype(LOW)
-        o_r[:, HD:] = v[:, HD:].astype(LOW)
-
-    ins = [(v, *all_of(v.shape)) for v in (own, got, cos, sin)]
-    return kernel(body, (1,), ins, [(own.shape, LOW, *all_of(own.shape))])[0]
+        o_r[:, :qw] = q_r[...]
+        o_r[:, qw : qw + HD] = turn_back(v[:, :HD], c_r[...], s_r[...]).astype(LOW)
+        o_r[:, qw + HD :] = v[:, HD:].astype(LOW)
+
+    ins = [(v, *all_of(v.shape)) for v in (own, got, cos, sin, dq)]
+    shape = (own.shape[0], qw + own.shape[1])
+    return kernel(body, (1,), ins, [(shape, LOW, *all_of(shape))])[0]
 
 
 def make_local(ny, nx, nz):
@@ -828,6 +843,10 @@
         own = [query_weight, key_weight, value_weight, output_weight]
         own = jnp.concatenate(own, axis=1)
         gains = jnp.pad(gains, ((0, 12), (0, own.shape[1] - blk)))
+        if square:
+            flags = jnp.concatenate([segment_ids, live_mask], axis=0).astype(LOW)
+            flags = jnp.pad(flags, ((0, 0), (0, own.shape[1] - toks)))
+            gains = jnp.concatenate([gains[:4], flags, gains[6:]], axis=0)
         packet = Weight(jnp.concatenate([own, gains], axis=0))
         index = lax.axis_index("ctx") * toks + jnp.arange(toks, dtype=jnp.int32)
         own_info = jnp.concatenate([segment_ids, live_mask, index[None]], axis=0)
@@ -852,12 +871,20 @@
         wg, wu, wd = Weight(gate_weight), Weight(up_weight), Weight(down_weight)
 
         packet.near()
-        if square:
-            info = jnp.concatenate([own_info, seq.send(to_ctx, own_info)], axis=1)
-        else:
+        if not square:
             info = lax.all_gather(own_info, "ctx", axis=1, tiled=True)
         x, factors = seq.run(order, x_raw, factors=True)
         packet.far()
+        if square:
+
+            def both_info(mine, wx):
+                flags = wx[blk + 4 : blk + 6, :toks].astype(jnp.int32)
+                there = mine[2:3] + (1 - 2 * lax.axis_index("ctx")) * toks
+                return jnp.concatenate(
+                    [mine, jnp.concatenate([flags, there], axis=0)], axis=1
+                )
+
+            info = seq.run(both_info, own_info, packet.mine[1])
         allowed, cos, sin = seq.run(positions, info)
         packet.core()
         wg.near()
@@ -882,7 +909,6 @@
         wg.core()
         wu.far()
         za.middle()
-        dy = seq.run(order, dy_raw)
         if square:
             wu.mine[3:] = settle(*wu.mine[3:])
         wd.near()
@@ -890,7 +916,7 @@
         wd.far()
         gate_p, gate_at = placed(wg)
         up_p, up_at = placed(wu)
-        x2, h3, gate, up, hid = seq.run(
+        x2, h3, gate_up, hid = seq.run(
             ffn_in_kernel, za.out, x, g2, g3, *gate_p, *up_p, gate_at=gate_at, up_at=up_at
         )
         wd.core()
@@ -898,11 +924,12 @@
         part = seq.run(project_kernel, hid, *down_p, at=down_at)
         zf = ZSum(part)
         zf.middle()
+        dy = seq.run(order, dy_raw)
         qkv_g = seq.run(row_order, w_qkv)
         g1_g = seq.run(order, jnp.broadcast_to(g1, (16, width)), back=True)[:1]
 
         y, df, dgate, dup, dg4 = seq.run(
-            ffn_back_kernel, zf.out, x2, dy, g4, gate, up, *down_p, at=down_at
+            ffn_back_kernel, zf.out, x2, dy, g4, gate_up, *down_p, at=down_at
         )
         part = seq.run(
             ffn_inputs_kernel, dgate, dup, *gate_p, *up_p, gate_at=gate_at, up_at=up_at
@@ -944,27 +971,24 @@
         sg.low()
         sd.first()
         su.low()
+        sg.first()
         zd.middle()
-        sg.first()
+        layer_output = seq.run(order, y, back=True)
         sd.second()
         su.got = settle(*su.got)
 
-        dx2, da, dq, dkv, dg23 = seq.run(
+        dx2, da, dq, own, other, dg23 = seq.run(
             attn_back_kernel, zd.out, x2, dy, za.out, g3, g2, w_out,
-            q, kv_all, allowed, logs, cos, sin,
+            q, kv_all, allowed, logs, cos, sin, toks=toks,
         )
         if square:
-            got = seq.send(to_ctx, dkv[toks:].astype(LOW))
-            own = dkv[:toks]
+            got = seq.send(to_ctx, other)
         else:
-            got = lax.psum_scatter(
-                dkv.astype(LOW), "ctx", scatter_dimension=0, tiled=True
-            )
-            own = jnp.zeros((toks, 2 * kw), F32)
+            got = lax.psum_scatter(other, "ctx", scatter_dimension=0, tiled=True)
+            own = jnp.zeros_like(own)
         sg.second()
         down_grad = sd.end()
-        dkv_low = seq.run(keys_back_kernel, own, got, cos, sin)
-        dqkv = seq.run(lambda a, b: jnp.concatenate([a, b], 1), dq, dkv_low)
+        dqkv = seq.run(keys_back_kernel, own, got, cos, sin, dq)
         part = seq.run(project_kernel, dqkv, qkv_g, at=[(0, 0)])
         z1 = ZSum(part)
         so, sq = Scatter(da, o), Scatter(h1, dqkv)
@@ -978,19 +1002,20 @@
         so.first()
         sq.first()
         so.second()
-        up_grad = su.end()
         sq.second()
         input_grad, dg1 = seq.run(last_kernel, x_raw, g1_g, z1.out, dx2)
-        layer_output = seq.run(order, y, back=True)
-        out_grad = so.end()
-        qkv_grad = sq.end()
-        dg1 = order(jnp.broadcast_to(dg1, (16, width)))[:1]
+        dg1 = seq.run(order, jnp.broadcast_to(dg1, (16, width)))[:1]
         dgain = jnp.concatenate([dg1, dg23[:2], dg4], axis=0)
-        dgain = dgain[:, :mid] + to_core(dgain[:, mid:])
+        got = seq.send(to_core, dgain[:, mid:])
+        up_grad = su.end()
+        dgain = seq.run(lambda a, b: a[:, :mid] + b, dgain, got)
         if square:
-            s = dgain[:, : mid // 2] + to_y(dgain[:, mid // 2 :])
-            dgain = s[:, :blk] + to_ctx(s[:, blk:])
+            got = seq.send(to_y, dgain[:, mid // 2 :])
+            out_grad, qkv_grad = so.end(), sq.end()
+            dgain = seq.run(lambda a, b: a[:, : mid // 2] + b, dgain, got)
+            dgain = dgain[:, :blk] + to_ctx(dgain[:, blk:])
         else:
+            out_grad, qkv_grad = so.end(), sq.end()
             dgain = lax.psum_scatter(
                 dgain, ("y", "ctx"), scatter_dimension=1, tiled=True
             )

time: 707 us -> 695 us (0.983)
  waiting for transfers between devices: 287 us -> 277 us
    ppermute x19, waiting for transfers between devices: 101 us -> 120 us  [to_y(): return lax.ppermute(a, 'y', SWAP)]
    reduce_scatter x4, waiting for transfers between devices: 60.3 us -> 48.9 us  [__init__(): self.own = lax.psum_scatter(part, 'tensor', scatter_dimension=0, tiled=True)]
    ppermute x31, waiting for transfers between devices: 16.6 us -> 7.39 us  [to_core(): return lax.ppermute(a, 'core', SWAP)]
    ppermute x22 -> x21, waiting for transfers between devices: 55.5 us -> 47 us  [to_ctx(): return lax.ppermute(a, 'ctx', SWAP)]
    ppermute x22 -> x21, starting transfers between devices: 25.5 us -> 25 us  [to_ctx(): return lax.ppermute(a, 'ctx', SWAP)]
    unnamed x130 -> x121, local copies, waits for them, and re-layouts: 22.1 us -> 21.9 us
  transfers between devices with their start and end apart: 80 -> 79, of which waited for: 33 -> 34; matrix products, arithmetic and copies ran while one was open for 6% -> 6% of each run, Pallas kernels for 28% -> 29%
where the time goes in v5:
time: 695 us; the launch traced here: 685 us
  waiting for transfers between devices  277 us (40%)
  Pallas kernels  274 us (39%)
  local copies, waits for them, and re-layouts  57.8 us (8%)
  starting transfers between devices  52.6 us (8%)
  between operations  15.4 us (2%)
  other arithmetic  8.17 us (1%)
    pallas_call x16, Pallas kernels, streaming(): pl.pallas_call(body, in_specs=[place[p] for _, p in ins], out_specs=[plac...  167 us
    ppermute x19, waiting for transfers between devices, to_y(): return lax.ppermute(a, 'y', SWAP)  120 us
    pallas_call x14, Pallas kernels, kernel(): pl.pallas_call(body, grid=grid, in_specs=[spec(*e[1:]) for e in ins], out...  76.8 us
    all_gather x4, waiting for transfers between devices, middle(): self.out = lax.all_gather(own, 'tensor', axis=0, tiled=True)  53.9 us
    reduce_scatter x4, waiting for transfers between devices, __init__(): self.own = lax.psum_scatter(part, 'tensor', scatter_dimension=0, tiled=True)  48.9 us
    ppermute x21, waiting for transfers between devices, to_ctx(): return lax.ppermute(a, 'ctx', SWAP)  47 us
    pallas_call x6, Pallas kernels, order_kernel(): pl.pallas_call(body, grid=(rows // br,), in_specs=[pl.BlockSpec(memory_sp...  29.7 us
    ppermute x21, starting transfers between devices, to_ctx(): return lax.ppermute(a, 'ctx', SWAP)  25 us
  transfers between devices with their start and end apart: 79, of which 34 were waited for; matrix products, arithmetic and copies ran while one was open for 6% of the time, Pallas kernels for 29%

profile of v5, /device:TPU:0, one launch (start us, length us, event | category | flops | bytes accessed | tf_op | source)
XLA Modules:
  0.0 685.0 jit_solution(16592906462662383239)
XLA Ops:
  24.6 12.1 %collective-permute-done.1.refs_2_ = bf16[304,1536]{1,0:T(8,128)(2,1)S(1)} collective-permute-done((bf16[304,1536]{1,0:T(8,128)(2,1)S(1)}, bf16[304,1536]{1,0:T(8,128)(2,1)S(1)}, u32[]{:S(2)}, u32[]{:S(2)}) %collective-permute-start.1) | collective-permute-done | bytes 933920 | tf_op jit(solution)/shard_map/ppermute | solution.py:54
  55.9 9.6 %first_kernel.1 = (bf16[512,2304]{1,0:T(8,128)(2,1)}, bf16[512,512]{1,0:T(8,128)(2,1)}, bf16[512,512]{1,0:T(8,128)(2,1)}, f32[8,2304]{1,0:T(8,128)}, bf16[2304,1...) custom-call(bf16[512,2304]{1,0:T(8,128)(2,1)} %get-tuple-element.463.x_r.x_h, f32[512,128]{1,0:T(8,128)} %get-tuple-element.396.r_r, ...), custom_call_target="tpu_custom_call" | custom-call | flops 999999995904 | tf_op jit(solution)/shard_map/first_kernel/pallas_call | solution.py:326
  66.0 16.4 %collective-permute-done.11.refs_2_ = bf16[288,2304]{1,0:T(8,128)(2,1)} collective-permute-done((bf16[288,2304]{1,0:T(8,128)(2,1)}, bf16[288,2304]{1,0:T(8,128)(2,1)}, u32[]{:S(2)}, u32[]{:S(2)}) %collective-permute-start.11) | collective-permute-done | bytes 1327136 | tf_op jit(solution)/shard_map/ppermute | solution.py:54
  95.7 7.8 %attn_kernel.1 = (bf16[512,512]{1,0:T(8,128)(2,1)}, f32[512,256]{1,0:T(8,128)}, bf16[512,2304]{1,0:T(8,128)(2,1)}) custom-call(bf16[512,512]{1,0:T(8,128)(2,1)} %get-tuple-element.606.q_r, bf16[1024,512]{1,0:T(8,128)(2,1)} %copy-done.42, bf16[512,1024]{1,0:T(8,128)(2,1)} %and_convert_fusion.m_r, bf16[2304,512]{1,0:T(8,128)(2,1)} %get-tuple-element.605.w_r), custom_call_target="tpu_custom_call" | custom-call | flops 999999995904 | tf_op jit(solution)/shard_map/attn_kernel/pallas_call | solution.py:120
  106.7 13.5 %collective-permute-done.13.refs_4_ = bf16[144,2304]{1,0:T(8,128)(2,1)S(1)} collective-permute-done((bf16[144,2304]{1,0:T(8,128)(2,1)S(1)}, bf16[144,2304]{1,0:T(8,128)(2,1)S(1)}, u32[]{:S(2)}, u32[]{:S(2)}) %collective-permute-start.13) | collective-permute-done | bytes 663584 | tf_op jit(solution)/shard_map/ppermute | solution.py:50
  122.7 27.8 %collective-permute-done.15.refs_12_ = bf16[288,2304]{1,0:T(8,128)(2,1)S(1)} collective-permute-done((bf16[288,2304]{1,0:T(8,128)(2,1)}, bf16[288,2304]{1,0:T(8,128)(2,1)S(1)}, u32[]{:S(2)}, u32[]{:S(2)}) %collective-permute-start.15) | collective-permute-done | bytes 1327136 | tf_op jit(solution)/shard_map/ppermute | solution.py:54
  155.3 11.0 %collective-permute-done.22.refs_14_ = bf16[144,2304]{1,0:T(8,128)(2,1)} collective-permute-done((bf16[144,2304]{1,0:T(8,128)(2,1)}, bf16[144,2304]{1,0:T(8,128)(2,1)}, u32[]{:S(2)}, u32[]{:S(2)}) %collective-permute-start.22) | collective-permute-done | bytes 663584 | tf_op jit(solution)/shard_map/ppermute | solution.py:50
  174.6 26.2 %collective-permute-done.29.refs_2_ = bf16[288,2304]{1,0:T(8,128)(2,1)} collective-permute-done((bf16[288,2304]{1,0:T(8,128)(2,1)}, bf16[288,2304]{1,0:T(8,128)(2,1)}, u32[]{:S(2)}, u32[]{:S(2)}) %collective-permute-start.29) | collective-permute-done | bytes 1327136 | tf_op jit(solution)/shard_map/ppermute | solution.py:54
  211.8 21.4 %ffn_in_kernel.1 = (f32[512,2304]{1,0:T(8,128)}, bf16[512,2304]{1,0:T(8,128)(2,1)}, bf16[512,4608]{1,0:T(8,128)(2,1)}, bf16[512,2304]{1,0:T(8,128)(2,1)}) custom-call(bf16[512,2304]{1,0:T(8,128)(2,1)} %all-gather.5.cloned.1.call-done.a_h.a_r, bf16[512,2304]{1,0:T(8,128)(2,1)} %get-tuple-element.463.x_r.x_h, f32[1,2304]{1,0:T(1,128)} %get-tuple-element.604.g2_r, ...), custom_call_target="tpu_custom_call" | custom-call | tf_op jit(solution)/shard_map/ffn_in_kernel/pallas_call | solution.py:326
  237.4 12.0 %project_kernel.2 = bf16[512,2304]{1,0:T(8,128)(2,1)} custom-call(bf16[512,2304]{1,0:T(8,128)(2,1)} %get-tuple-element.562.u_r.b_h, bf16[288,2304]{1,0:T(8,128)(2,1)} %refs_0_.2, bf16[288,2304]{1,0:T(8,128)(2,1)} %collective-permute-done.28.refs_1_, bf16[288,2304]{1,0:T(8,128)(2,1)} %collective-permute-done.29.refs_2_, ...), custom_call_target="tpu_custom_call" | custom-call | tf_op jit(solution)/shard_map/project_kernel/pallas_call | solution.py:326
  249.6 46.7 %reduce-scatter.7.cloned.1.call-done = bf16[128,2304]{1,0:T(8,128)(2,1)} async-done(((bf16[512,2304]{1,0:T(8,128)(2,1)}), bf16[128,2304]{1,0:T(8,128)(2,1)}) %reduce-scatter.7.cloned.1.call-update) | async-done | bytes 589840 | tf_op jit(solution)/shard_map/reduce_scatter | solution.py:771
  318.4 29.3 %all-gather.7.cloned.1.call-done.f_h = bf16[512,2304]{1,0:T(8,128)(2,1)} async-done(((bf16[128,2304]{1,0:T(8,128)(2,1)}), bf16[512,2304]{1,0:T(8,128)(2,1)}) %all-gather.7.cloned.1.call-update) | async-done | bytes 2359312 | tf_op jit(solution)/shard_map/all_gather | solution.py:778
  347.7 27.3 %ffn_back_kernel.1 = (bf16[512,2304]{1,0:T(8,128)(2,1)}, bf16[512,2304]{1,0:T(8,128)(2,1)}, bf16[512,2304]{1,0:T(8,128)(2,1)}, bf16[512,2304]{1,0:T(8,128)(2,1)}, f32[1,2304]{1,0:T(1,128)}) custom-call(bf16[512,2304]{1,0:T(8,128)(2,1)} %all-gather.7.cloned.1.call-done.f_h, f32[512,2304]{1,0:T(8,128)} %get-tuple-element.600.x2_h.x_r, ...), custom_call_target="tpu_custom_call" | custom-call | tf_op jit(solution)/shard_map/ffn_back_kernel/pallas_call | solution.py:326
  374.9 21.2 %ffn_inputs_kernel.1 = bf16[512,2304]{1,0:T(8,128)(2,1)} custom-call(bf16[512,2304]{1,0:T(8,128)(2,1)} %get-tuple-element.578.dg_r.b_h, bf16[512,2304]{1,0:T(8,128)(2,1)} %get-tuple-element.637.du_r.b_h, bf16[288,2304]{1,0:T(8,128)(2,1)} %refs_0_.3, bf16[288,2304]{1,0:T(8,128)(2,1)} %collective-permute-done.10.refs_1_, ...), custom_call_target="tpu_custom_call" | custom-call | tf_op jit(solution)/shard_map/ffn_inputs_kernel/pallas_call | solution.py:326
  412.7 9.1 %outer_kernel.12 = (bf16[288,2304]{1,0:T(8,128)(2,1)}, bf16[288,2304]{1,0:T(8,128)(2,1)}, bf16[288,2304]{1,0:T(8,128)(2,1)}, bf16[144,2304]{1,0:T(8,128)(2,1)}, bf16[144,2304]{1,0:T(8,128)(2,1)}) custom-call(bf16[512,2304]{1,0:T(8,128)(2,1)} %get-tuple-element.561.a_h, bf16[512,2304]{1,0:T(8,128)(2,1)} %get-tuple-element.562.u_r.b_h, ...), custom_call_target="tpu_custom_call" | custom-call | tf_op jit(solution)/shard_map/outer_kernel/pallas_call | solution.py:326
  431.8 9.1 %outer_kernel.14 = (bf16[288,2304]{1,0:T(8,128)(2,1)}, bf16[288,2304]{1,0:T(8,128)(2,1)}, bf16[288,2304]{1,0:T(8,128)(2,1)}, bf16[144,2304]{1,0:T(8,128)(2,1)}, bf16[144,2304]{1,0:T(8,128)(2,1)}) custom-call(bf16[512,2304]{1,0:T(8,128)(2,1)} %get-tuple-element.636.a_h, bf16[512,2304]{1,0:T(8,128)(2,1)} %get-tuple-element.578.dg_r.b_h, ...), custom_call_target="tpu_custom_call" | custom-call | tf_op jit(solution)/shard_map/outer_kernel/pallas_call | solution.py:326
  453.1 8.7 %collective-permute-done.44.gy_r = bf16[144,2304]{1,0:T(8,128)(2,1)S(1)} collective-permute-done((bf16[144,2304]{1,0:T(8,128)(2,1)}, bf16[144,2304]{1,0:T(8,128)(2,1)S(1)}, u32[]{:S(2)}, u32[]{:S(2)}) %collective-permute-start.44) | collective-permute-done | bytes 663584 | tf_op jit(solution)/shard_map/ppermute | solution.py:54
  469.9 24.7 %all-gather.9.cloned.1.call-done.d_r = bf16[512,2304]{1,0:T(8,128)(2,1)} async-done(((bf16[128,2304]{1,0:T(8,128)(2,1)}), bf16[512,2304]{1,0:T(8,128)(2,1)}) %all-gather.9.cloned.1.call-update) | async-done | bytes 2359312 | tf_op jit(solution)/shard_map/all_gather | solution.py:778
  494.6 20.3 %attn_back_kernel.1 = (f32[512,2304]{1,0:T(8,128)}, bf16[512,2304]{1,0:T(8,128)(2,1)}, bf16[512,512]{1,0:T(8,128)(2,1)}, f32[512,512]{1,0:T(8,128)}, bf16[512,512]{1,0:T(8,128)(2,1)}, /*index=5*/f32[8,2304]{1,0:T(8,128)}) custom-call(bf16[512,2304]{1,0:T(8,128)(2,1)} %all-gather.9.cloned.1.call-done.d_r, f32[512,2304]{1,0:T(8,128)} %get-tuple-element.600.x2_h.x_r, ...), custom_call_target="tpu_custom_call" | custom-call | flops 999999995904 | tf_op jit(solution)/shard_map/attn_back_kernel/pallas_call | solution.py:120
  532.4 7.2 %project_kernel.3 = bf16[512,2304]{1,0:T(8,128)(2,1)} custom-call(bf16[512,1024]{1,0:T(8,128)(2,1)} %keys_back_kernel.1.u_r.b_h, bf16[2304,1024]{1,0:T(8,128)(2,1)} %slice_dynamic-update-slice_fusion.refs_0_), custom_call_target="tpu_custom_call" | custom-call | tf_op jit(solution)/shard_map/project_kernel/pallas_call | solution.py:326
  543.0 9.6 %outer_kernel.15 = (bf16[288,2304]{1,0:T(8,128)(2,1)}, bf16[288,2304]{1,0:T(8,128)(2,1)}, bf16[288,2304]{1,0:T(8,128)(2,1)}, bf16[144,2304]{1,0:T(8,128)(2,1)}, bf16[144,2304]{1,0:T(8,128)(2,1)}) custom-call(bf16[512,2304]{1,0:T(8,128)(2,1)} %get-tuple-element.636.a_h, bf16[512,2304]{1,0:T(8,128)(2,1)} %get-tuple-element.637.du_r.b_h, ...), custom_call_target="tpu_custom_call" | custom-call | tf_op jit(solution)/shard_map/outer_kernel/pallas_call | solution.py:326
  562.5 7.6 %shard_map.250.dx_r = f32[512,2304]{1,0:T(8,128)} custom-call(s32[3]{0:T(128)} %pad_add_fusion.1.b_r, f32[512,2304]{1,0:T(8,128)} %get-tuple-element.657.v_r), custom_call_target="tpu_custom_call" | custom-call | tf_op jit(solution)/shard_map/pallas_call | solution.py:693
  614.2 11.9 %collective-permute-done.61.gy_r = bf16[144,512]{1,0:T(8,128)(2,1)S(1)} collective-permute-done((bf16[144,512]{1,0:T(8,128)(2,1)}, bf16[144,512]{1,0:T(8,128)(2,1)S(1)}, u32[]{:S(2)}, u32[]{:S(2)}) %collective-permute-start.61) | collective-permute-done | bytes 147488 | tf_op jit(solution)/shard_map/ppermute | solution.py:54
  643.0 7.8 %last_kernel.1 = (f32[512,2304]{1,0:T(8,128)}, f32[1,2304]{1,0:T(1,128)}) custom-call(bf16[512,2304]{1,0:T(8,128)(2,1)} %bitcast.11, f32[1,2304]{1,0:T(1,128)} %slice.175.g_r, bf16[512,2304]{1,0:T(8,128)(2,1)} %all-gather.11.cloned.1.call-done.d_r, f32[512,2304]{1,0:T(8,128)} %shard_map.250.dx_r), custom_call_target="tpu_custom_call" | custom-call | tf_op jit(solution)/shard_map/last_kernel/pallas_call | solution.py:120
  (360 shorter events, 271.6 us)
Async XLA Ops:
  7.2 146.1 %reduce-scatter.5.cloned.1.call-start = ((), (), s32[]{:S(2)}) async-start(), calls=%async_computation.4 | async-start | bytes 2949120 | tf_op jit(solution)/shard_map/reduce_scatter | solution.py:771
  17.4 33.6 %collective-permute-start.4 = (bf16[304,1536]{1,0:T(8,128)(2,1)S(1)}, bf16[304,1536]{1,0:T(8,128)(2,1)}, u32[]{:S(2)}, u32[]{:S(2)}) collective-permute-start(bf16[304,1536]{1,0:T(8,128)(2,1)S(1)} %maximum_maximum_fusion.refs_0_), channel_id=1, source_target_pairs={{0,8},{8,0},{1,9},{9,1},{2,10},{10,2},{3,11},{11,3},{4,12},{12,4},... | collective-permute-start | bytes 2801672 | tf_op jit(solution)/shard_map/ppermute | solution.py:58
  52.4 32.4 %collective-permute-start.10 = (bf16[288,2304]{1,0:T(8,128)(2,1)}, bf16[288,2304]{1,0:T(8,128)(2,1)}, u32[]{:S(2)}, u32[]{:S(2)}) collective-permute-start(bf16[288,2304]{1,0:T(8,128)(2,1)} %refs_0_.3), channel_id=1, source_target_pairs={{0,4},{4,0},{1,5},{5,1},{2,6},{6,2},{3,7},{7,3},{8,12},{12,8},{9,1... | collective-permute-start | bytes 3981320 | tf_op jit(solution)/shard_map/ppermute | solution.py:50
  103.5 108.2 %all-gather.5.cloned.1.call-start = ((), (), s32[]{:S(2)}) async-start(), calls=%async_computation.5 | async-start | bytes 2949120 | tf_op jit(solution)/shard_map/all_gather | solution.py:778
  122.7 46.2 %collective-permute-start.16 = (bf16[288,2304]{1,0:T(8,128)(2,1)}, bf16[288,2304]{1,0:T(8,128)(2,1)}, u32[]{:S(2)}, u32[]{:S(2)}) collective-permute-start(bf16[288,2304]{1,0:T(8,128)(2,1)} %refs_0_.3), channel_id=1, source_target_pairs={{0,8},{8,0},{1,9},{9,1},{2,10},{10,2},{3,11},{11,3},{4,12},{12,4},... | collective-permute-start | bytes 3981320 | tf_op jit(solution)/shard_map/ppermute | solution.py:58
  153.4 142.9 %reduce-scatter.7.cloned.1.call-start = ((), (), s32[]{:S(2)}) async-start(), calls=%async_computation.6 | async-start | bytes 2949120 | tf_op jit(solution)/shard_map/reduce_scatter | solution.py:771
  168.9 31.9 %collective-permute-start.29 = (bf16[288,2304]{1,0:T(8,128)(2,1)}, bf16[288,2304]{1,0:T(8,128)(2,1)}, u32[]{:S(2)}, u32[]{:S(2)}) collective-permute-start(bf16[288,2304]{1,0:T(8,128)(2,1)} %refs_0_.2), channel_id=1, source_target_pairs={{0,16},{16,0},{1,17},{17,1},{2,18},{18,2},{3,19},{19,3},{4,20},{20... | collective-permute-start | bytes 3981320 | tf_op jit(solution)/shard_map/ppermute | solution.py:54
  171.9 34.0 %collective-permute-start.23 = (bf16[288,2304]{1,0:T(8,128)(2,1)}, bf16[288,2304]{1,0:T(8,128)(2,1)S(1)}, u32[]{:S(2)}, u32[]{:S(2)}) collective-permute-start(bf16[288,2304]{1,0:T(8,128)(2,1)} %refs_10_.1), channel_id=1, source_target_pairs={{0,8},{8,0},{1,9},{9,1},{2,10},{10,2},{3,11},{11,3},{4,12},{12,4},... | collective-permute-start | bytes 3981320 | tf_op jit(solution)/shard_map/ppermute | solution.py:58
  171.9 35.5 %collective-permute-start.25 = (bf16[288,2304]{1,0:T(8,128)(2,1)S(1)}, bf16[288,2304]{1,0:T(8,128)(2,1)S(1)}, u32[]{:S(2)}, u32[]{:S(2)}) collective-permute-start(bf16[288,2304]{1,0:T(8,128)(2,1)S(1)} %collective-permute-done.15.refs_12_), channel_id=1, source_target_pairs={{0,8},{8,0},{1,9},{9,1},{2,10},{10,2},{3,11},{11,3},{4,12},{12,4},... | collective-permute-start | bytes 3981320 | tf_op jit(solution)/shard_map/ppermute | solution.py:58
  174.3 34.1 %collective-permute-start.24 = (bf16[288,2304]{1,0:T(8,128)(2,1)S(1)}, bf16[288,2304]{1,0:T(8,128)(2,1)S(1)}, u32[]{:S(2)}, u32[]{:S(2)}) collective-permute-start(bf16[288,2304]{1,0:T(8,128)(2,1)S(1)} %collective-permute-done.14.refs_11_), channel_id=1, source_target_pairs={{0,8},{8,0},{1,9},{9,1},{2,10},{10,2},{3,11},{11,3},{4,12},{12,4},... | collective-permute-start | bytes 3981320 | tf_op jit(solution)/shard_map/ppermute | solution.py:58
  249.5 98.2 %all-gather.7.cloned.1.call-start = ((), (), s32[]{:S(2)}) async-start(), calls=%async_computation.7 | async-start | bytes 2949120 | tf_op jit(solution)/shard_map/all_gather | solution.py:778
  296.3 146.9 %reduce-scatter.9.cloned.1.call-start = ((), (), s32[]{:S(2)}) async-start(), calls=%async_computation.8 | async-start | bytes 2949120 | tf_op jit(solution)/shard_map/reduce_scatter | solution.py:771
  396.1 98.4 %all-gather.9.cloned.1.call-start = ((), (), s32[]{:S(2)}) async-start(), calls=%async_computation.9 | async-start | bytes 2949120 | tf_op jit(solution)/shard_map/all_gather | solution.py:778
  443.2 146.9 %reduce-scatter.11.cloned.1.call-start = ((), (), s32[]{:S(2)}) async-start(), calls=%async_computation.10 | async-start | bytes 2949120 | tf_op jit(solution)/shard_map/reduce_scatter | solution.py:771
  446.7 69.6 %collective-permute-start.49 = (bf16[144,2304]{1,0:T(8,128)(2,1)}, bf16[144,2304]{1,0:T(8,128)(2,1)}, u32[]{:S(2)}, u32[]{:S(2)}) collective-permute-start(bf16[144,2304]{1,0:T(8,128)(2,1)} %get-tuple-element.587), channel_id=1, source_target_pairs={{0,16},{16,0},{1,17},{17,1},{2,18},{18,2},{3,19},{19,3},{4,20},{20... | collective-permute-start | bytes 1990664 | tf_op jit(solution)/shard_map/ppermute | solution.py:54
  461.8 54.6 %collective-permute-start.48 = (bf16[144,2304]{1,0:T(8,128)(2,1)}, bf16[144,2304]{1,0:T(8,128)(2,1)}, u32[]{:S(2)}, u32[]{:S(2)}) collective-permute-start(bf16[144,2304]{1,0:T(8,128)(2,1)} %get-tuple-element.586), channel_id=1, source_target_pairs={{0,4},{4,0},{1,5},{5,1},{2,6},{6,2},{3,7},{7,3},{8,12},{12,8},{9,1... | collective-permute-start | bytes 1990664 | tf_op jit(solution)/shard_map/ppermute | solution.py:50
  467.6 53.2 %collective-permute-start.46 = (bf16[288,2304]{1,0:T(8,128)(2,1)}, bf16[288,2304]{1,0:T(8,128)(2,1)}, u32[]{:S(2)}, u32[]{:S(2)}) collective-permute-start(bf16[288,2304]{1,0:T(8,128)(2,1)} %get-tuple-element.595), channel_id=1, source_target_pairs={{0,4},{4,0},{1,5},{5,1},{2,6},{6,2},{3,7},{7,3},{8,12},{12,8},{9,1... | collective-permute-start | bytes 3981320 | tf_op jit(solution)/shard_map/ppermute | solution.py:50
  468.4 52.4 %collective-permute-start.47 = (bf16[288,2304]{1,0:T(8,128)(2,1)}, bf16[288,2304]{1,0:T(8,128)(2,1)}, u32[]{:S(2)}, u32[]{:S(2)}) collective-permute-start(bf16[288,2304]{1,0:T(8,128)(2,1)} %get-tuple-element.596), channel_id=1, source_target_pairs={{0,16},{16,0},{1,17},{17,1},{2,18},{18,2},{3,19},{19,3},{4,20},{20... | collective-permute-start | bytes 3981320 | tf_op jit(solution)/shard_map/ppermute | solution.py:54
  539.7 103.3 %all-gather.11.cloned.1.call-start = ((), (), s32[]{:S(2)}) async-start(), calls=%async_computation.11 | async-start | bytes 2949120 | tf_op jit(solution)/shard_map/all_gather | solution.py:778
  539.9 32.3 %collective-permute-start.53 = (bf16[288,2304]{1,0:T(8,128)(2,1)}, bf16[288,2304]{1,0:T(8,128)(2,1)S(1)}, u32[]{:S(2)}, u32[]{:S(2)}) collective-permute-start(bf16[288,2304]{1,0:T(8,128)(2,1)} %get-tuple-element.625), channel_id=1, source_target_pairs={{0,16},{16,0},{1,17},{17,1},{2,18},{18,2},{3,19},{19,3},{4,20},{20... | collective-permute-start | bytes 3981320 | tf_op jit(solution)/shard_map/ppermute | solution.py:54
  541.5 32.3 %collective-permute-start.52 = (bf16[288,2304]{1,0:T(8,128)(2,1)}, bf16[288,2304]{1,0:T(8,128)(2,1)S(1)}, u32[]{:S(2)}, u32[]{:S(2)}) collective-permute-start(bf16[288,2304]{1,0:T(8,128)(2,1)} %get-tuple-element.624), channel_id=1, source_target_pairs={{0,4},{4,0},{1,5},{5,1},{2,6},{6,2},{3,7},{7,3},{8,12},{12,8},{9,1... | collective-permute-start | bytes 3981320 | tf_op jit(solution)/shard_map/ppermute | solution.py:50
  553.1 32.6 %collective-permute-start.50 = (bf16[144,2304]{1,0:T(8,128)(2,1)}, bf16[144,2304]{1,0:T(8,128)(2,1)}, u32[]{:S(2)}, u32[]{:S(2)}) collective-permute-start(bf16[144,2304]{1,0:T(8,128)(2,1)} %get-tuple-element.645), channel_id=1, source_target_pairs={{0,4},{4,0},{1,5},{5,1},{2,6},{6,2},{3,7},{7,3},{8,12},{12,8},{9,1... | collective-permute-start | bytes 1990664 | tf_op jit(solution)/shard_map/ppermute | solution.py:50
  590.7 64.3 %collective-permute-start.68 = (bf16[288,2304]{1,0:T(8,128)(2,1)}, bf16[288,2304]{1,0:T(8,128)(2,1)S(1)}, u32[]{:S(2)}, u32[]{:S(2)}) collective-permute-start(bf16[288,2304]{1,0:T(8,128)(2,1)} %get-tuple-element.667), channel_id=1, source_target_pairs={{0,16},{16,0},{1,17},{17,1},{2,18},{18,2},{3,19},{19,3},{4,20},{20... | collective-permute-start | bytes 3981320 | tf_op jit(solution)/shard_map/ppermute | solution.py:54
  591.7 64.4 %collective-permute-start.67 = (bf16[288,2304]{1,0:T(8,128)(2,1)}, bf16[288,2304]{1,0:T(8,128)(2,1)S(1)}, u32[]{:S(2)}, u32[]{:S(2)}) collective-permute-start(bf16[288,2304]{1,0:T(8,128)(2,1)} %get-tuple-element.666), channel_id=1, source_target_pairs={{0,4},{4,0},{1,5},{5,1},{2,6},{6,2},{3,7},{7,3},{8,12},{12,8},{9,1... | collective-permute-start | bytes 3981320 | tf_op jit(solution)/shard_map/ppermute | solution.py:50
  (115 other events, 1582.6 us)
Sparse Core Ops, SparseCore 0:
  103.7 48.3 reduce-scatter.4
  153.6 51.3 all-gather.4
  249.6 46.5 reduce-scatter.6
  297.7 49.9 all-gather.6
  396.3 46.8 reduce-scatter.8
  444.6 49.9 all-gather.8
  539.8 46.9 reduce-scatter.10
  590.2 49.2 all-gather.10

commit v6 on v5

--- a/solution.py
+++ b/solution.py
@@ -234,8 +234,31 @@
     return kernel(body, (rows // qb,), ins, outs, cost=LONG)
 
 
+def probs_kernel(q, kv, allowed, logs):
+    rows, qw = q.shape
+    length = kv.shape[0]
+    qb = query_block(rows, length)
+    heads = qw // HD
+
+    def body(q_r, kv_r, m_r, t_r, p_r, s_r):
+        ok = m_r[...] > 0
+        for j in range(heads):
+            b = jnp.tanh(nt(q_r[:, j * HD : (j + 1) * HD], kv_r[:, :HD]) * (1.0 / SOFT_CAP))
+            logit = jnp.where(ok, SOFT_CAP * b, MASKED_SCORE)
+            p = jnp.exp(logit - t_r[:, j * 128 : j * 128 + 1])
+            keys = slice(j * length, (j + 1) * length)
+            p_r[:, keys] = p.astype(LOW)
+            s_r[:, keys] = (p * (1.0 - b * b)).astype(LOW)
+
+    row = lambda n: ((qb, n), lambda i: (i, 0))
+    ins = [(q, *row(qw)), (kv, *all_of(kv.shape)), (allowed, *row(length))]
+    ins += [(logs, *row(128 * heads))]
+    outs = [((rows, heads * length), LOW, *row(heads * length))] * 2
+    return kernel(body, (rows // qb,), ins, outs)
+
+
 def attn_back_kernel(
-    dh3, x2, dy, a, g3, g2, w, q, kv, allowed, logs, cos, sin, toks
+    dh3, x2, dy, a, g3, g2, w, q, kv, p, slope, cos, sin, toks
 ):
     rows, width = x2.shape
     qw = q.shape[1]
@@ -246,7 +269,7 @@
     scale = 1.0 / math.sqrt(HD)
 
     def body(
-        d_r, x_r, dy_r, a_r, g3_r, g2_r, w_r, q_r, kv_r, m_r, t_r, c_r, s_r,
+        d_r, x_r, dy_r, a_r, g3_r, g2_r, w_r, q_r, kv_r, p_r, t_r, c_r, s_r,
         dx_r, da_r, dq_r, own_r, other_r, dg_r, dkv_r,
     ):
         @pl.when(pl.program_id(0) == 0)
@@ -267,22 +290,20 @@
         dg_r[0:1] += jnp.sum(dg2, axis=0, keepdims=True)
         dg_r[1:2] += jnp.sum(dg3, axis=0, keepdims=True)
         do = nn(da_r[...], w_r[...]).astype(LOW)
-        ok = m_r[...] > 0
         k, v = kv_r[:, :HD], kv_r[:, HD:]
         c, s = c_r[...], s_r[...]
         dk = dv = 0.0
         for j in range(heads):
             cut = slice(j * HD, (j + 1) * HD)
             qj, doj = q_r[:, cut], do[:, cut]
-            b = jnp.tanh(nt(qj, k) * (1.0 / SOFT_CAP))
-            logit = jnp.where(ok, SOFT_CAP * b, MASKED_SCORE)
-            p = jnp.exp(logit - t_r[:, j * 128 : j * 128 + 1])
+            keys = slice(j * length, (j + 1) * length)
+            p = p_r[:, keys]
             dp = nt(doj, v)
-            dc = p * (dp - jnp.sum(p * dp, axis=-1, keepdims=True))
-            ds = (dc * (1.0 - b * b)).astype(LOW)
+            dp = dp - jnp.sum(wide(p) * dp, axis=-1, keepdims=True)
+            ds = (wide(t_r[:, keys]) * dp).astype(LOW)
             dq_r[:, cut] = (turn_back(nn(ds, k), c, s) * scale).astype(LOW)
             dk = dk + tn(ds, qj)
-            dv = dv + tn(p.astype(LOW), doj)
+            dv = dv + tn(p, doj)
         dkv_r[:, :HD] += dk
         dkv_r[:, HD:] += dv
 
@@ -294,8 +315,8 @@
     row = lambda n: ((qb, n), lambda i: (i, 0))
     ins = [(v, *row(width)) for v in (dh3, x2, dy, a)]
     ins += [(v, *all_of(v.shape)) for v in (g3, g2, w)]
-    ins += [(q, *row(qw)), (kv, *all_of(kv.shape)), (allowed, *row(length))]
-    ins += [(logs, *row(128 * heads)), (cos, *row(HD // 2)), (sin, *row(HD // 2))]
+    ins += [(q, *row(qw)), (kv, *all_of(kv.shape)), (p, *row(p.shape[1]))]
+    ins += [(slope, *row(p.shape[1])), (cos, *row(HD // 2)), (sin, *row(HD // 2))]
     outs = [
         ((rows, width), F32, *row(width)),
         ((rows, width), LOW, *row(width)),
@@ -924,6 +945,7 @@
         part = seq.run(project_kernel, hid, *down_p, at=down_at)
         zf = ZSum(part)
         zf.middle()
+        probs, slopes = seq.run(probs_kernel, q, kv_all, allowed, logs)
         dy = seq.run(order, dy_raw)
         qkv_g = seq.run(row_order, w_qkv)
         g1_g = seq.run(order, jnp.broadcast_to(g1, (16, width)), back=True)[:1]
@@ -979,7 +1001,7 @@
 
         dx2, da, dq, own, other, dg23 = seq.run(
             attn_back_kernel, zd.out, x2, dy, za.out, g3, g2, w_out,
-            q, kv_all, allowed, logs, cos, sin, toks=toks,
+            q, kv_all, probs, slopes, cos, sin, toks=toks,
         )
         if square:
             got = seq.send(to_ctx, other)
@@ -1001,13 +1023,13 @@
         z1.middle()
         so.first()
         sq.first()
+        up_grad = su.end()
         so.second()
         sq.second()
         input_grad, dg1 = seq.run(last_kernel, x_raw, g1_g, z1.out, dx2)
         dg1 = seq.run(order, jnp.broadcast_to(dg1, (16, width)))[:1]
         dgain = jnp.concatenate([dg1, dg23[:2], dg4], axis=0)
         got = seq.send(to_core, dgain[:, mid:])
-        up_grad = su.end()
         dgain = seq.run(lambda a, b: a[:, :mid] + b, dgain, got)
         if square:
             got = seq.send(to_y, dgain[:, mid // 2 :])

time: 695 us -> 695 us (level)
    pallas_call x14 -> x15, Pallas kernels: 76.8 us -> 81 us  [kernel(): pl.pallas_call(body, grid=grid, in_specs=[spec(*e[1:]) for e in ins], out...]
    unnamed x121 -> x133, local copies, waits for them, and re-layouts: 21.9 us -> 23.6 us
  transfers between devices with their start and end apart: 79 -> 79, of which waited for: 34 -> 34; matrix products, arithmetic and copies ran while one was open for 6% -> 5% of each run, Pallas kernels for 29% -> 29%
where the time goes in v6:
time: 695 us; the launch traced here: 685 us
  Pallas kernels  278 us (40%)
  waiting for transfers between devices  271 us (39%)
  local copies, waits for them, and re-layouts  59.3 us (9%)
  starting transfers between devices  52.8 us (8%)
  between operations  15.4 us (2%)
  other arithmetic  8.16 us (1%)
    pallas_call x16, Pallas kernels, streaming(): pl.pallas_call(body, in_specs=[place[p] for _, p in ins], out_specs=[plac...  167 us
    ppermute x19, waiting for transfers between devices, to_y(): return lax.ppermute(a, 'y', SWAP)  121 us
    pallas_call x15, Pallas kernels, kernel(): pl.pallas_call(body, grid=grid, in_specs=[spec(*e[1:]) for e in ins], out...  81 us
    reduce_scatter x4, waiting for transfers between devices, __init__(): self.own = lax.psum_scatter(part, 'tensor', scatter_dimension=0, tiled=True)  48.8 us
    all_gather x4, waiting for transfers between devices, middle(): self.out = lax.all_gather(own, 'tensor', axis=0, tiled=True)  48.7 us
    ppermute x21, waiting for transfers between devices, to_ctx(): return lax.ppermute(a, 'ctx', SWAP)  44.8 us
    pallas_call x6, Pallas kernels, order_kernel(): pl.pallas_call(body, grid=(rows // br,), in_specs=[pl.BlockSpec(memory_sp...  29.8 us
    ppermute x21, starting transfers between devices, to_ctx(): return lax.ppermute(a, 'ctx', SWAP)  25.2 us
  transfers between devices with their start and end apart: 79, of which 34 were waited for; matrix products, arithmetic and copies ran while one was open for 5% of the time, Pallas kernels for 29%

profile of v6, /device:TPU:0, one launch (start us, length us, event | category | flops | bytes accessed | tf_op | source)
XLA Modules:
  0.0 684.8 jit_solution(1276116772859541538)
XLA Ops:
  24.6 12.1 %collective-permute-done.1.refs_2_ = bf16[304,1536]{1,0:T(8,128)(2,1)S(1)} collective-permute-done((bf16[304,1536]{1,0:T(8,128)(2,1)S(1)}, bf16[304,1536]{1,0:T(8,128)(2,1)S(1)}, u32[]{:S(2)}, u32[]{:S(2)}) %collective-permute-start.1) | collective-permute-done | bytes 933920 | tf_op jit(solution)/shard_map/ppermute | solution.py:54
  55.9 9.6 %first_kernel.1 = (bf16[512,2304]{1,0:T(8,128)(2,1)}, bf16[512,512]{1,0:T(8,128)(2,1)}, bf16[512,512]{1,0:T(8,128)(2,1)}, f32[8,2304]{1,0:T(8,128)}, bf16[2304,1...) custom-call(bf16[512,2304]{1,0:T(8,128)(2,1)} %get-tuple-element.469.x_r.x_h, f32[512,128]{1,0:T(8,128)} %get-tuple-element.402.r_r, ...), custom_call_target="tpu_custom_call" | custom-call | flops 999999995904 | tf_op jit(solution)/shard_map/first_kernel/pallas_call | solution.py:347
  66.0 16.4 %collective-permute-done.11.refs_2_ = bf16[288,2304]{1,0:T(8,128)(2,1)} collective-permute-done((bf16[288,2304]{1,0:T(8,128)(2,1)}, bf16[288,2304]{1,0:T(8,128)(2,1)}, u32[]{:S(2)}, u32[]{:S(2)}) %collective-permute-start.11) | collective-permute-done | bytes 1327136 | tf_op jit(solution)/shard_map/ppermute | solution.py:54
  95.7 7.8 %attn_kernel.1 = (bf16[512,512]{1,0:T(8,128)(2,1)}, f32[512,256]{1,0:T(8,128)}, bf16[512,2304]{1,0:T(8,128)(2,1)}) custom-call(bf16[512,512]{1,0:T(8,128)(2,1)} %get-tuple-element.618.q_r, bf16[1024,512]{1,0:T(8,128)(2,1)} %copy-done.22, bf16[512,1024]{1,0:T(8,128)(2,1)} %and_convert_fusion.m_r, bf16[2304,512]{1,0:T(8,128)(2,1)} %get-tuple-element.617.w_r), custom_call_target="tpu_custom_call" | custom-call | flops 999999995904 | tf_op jit(solution)/shard_map/attn_kernel/pallas_call | solution.py:120
  106.7 13.5 %collective-permute-done.13.refs_4_ = bf16[144,2304]{1,0:T(8,128)(2,1)S(1)} collective-permute-done((bf16[144,2304]{1,0:T(8,128)(2,1)S(1)}, bf16[144,2304]{1,0:T(8,128)(2,1)S(1)}, u32[]{:S(2)}, u32[]{:S(2)}) %collective-permute-start.13) | collective-permute-done | bytes 663584 | tf_op jit(solution)/shard_map/ppermute | solution.py:50
  122.7 27.8 %collective-permute-done.15.refs_12_ = bf16[288,2304]{1,0:T(8,128)(2,1)S(1)} collective-permute-done((bf16[288,2304]{1,0:T(8,128)(2,1)}, bf16[288,2304]{1,0:T(8,128)(2,1)S(1)}, u32[]{:S(2)}, u32[]{:S(2)}) %collective-permute-start.15) | collective-permute-done | bytes 1327136 | tf_op jit(solution)/shard_map/ppermute | solution.py:54
  155.4 11.1 %collective-permute-done.22.refs_14_ = bf16[144,2304]{1,0:T(8,128)(2,1)} collective-permute-done((bf16[144,2304]{1,0:T(8,128)(2,1)}, bf16[144,2304]{1,0:T(8,128)(2,1)}, u32[]{:S(2)}, u32[]{:S(2)}) %collective-permute-start.22) | collective-permute-done | bytes 663584 | tf_op jit(solution)/shard_map/ppermute | solution.py:50
  174.6 26.2 %collective-permute-done.29.refs_2_ = bf16[288,2304]{1,0:T(8,128)(2,1)} collective-permute-done((bf16[288,2304]{1,0:T(8,128)(2,1)}, bf16[288,2304]{1,0:T(8,128)(2,1)}, u32[]{:S(2)}, u32[]{:S(2)}) %collective-permute-start.29) | collective-permute-done | bytes 1327136 | tf_op jit(solution)/shard_map/ppermute | solution.py:54
  211.9 21.4 %ffn_in_kernel.1 = (f32[512,2304]{1,0:T(8,128)}, bf16[512,2304]{1,0:T(8,128)(2,1)}, bf16[512,4608]{1,0:T(8,128)(2,1)}, bf16[512,2304]{1,0:T(8,128)(2,1)}) custom-call(bf16[512,2304]{1,0:T(8,128)(2,1)} %all-gather.5.cloned.1.call-done.a_h.a_r, bf16[512,2304]{1,0:T(8,128)(2,1)} %get-tuple-element.469.x_r.x_h, f32[1,2304]{1,0:T(1,128)} %get-tuple-element.616.g2_r, ...), custom_call_target="tpu_custom_call" | custom-call | tf_op jit(solution)/shard_map/ffn_in_kernel/pallas_call | solution.py:347
  237.5 12.0 %project_kernel.2 = bf16[512,2304]{1,0:T(8,128)(2,1)} custom-call(bf16[512,2304]{1,0:T(8,128)(2,1)} %get-tuple-element.574.u_r.b_h, bf16[288,2304]{1,0:T(8,128)(2,1)} %refs_0_.2, bf16[288,2304]{1,0:T(8,128)(2,1)} %collective-permute-done.28.refs_1_, bf16[288,2304]{1,0:T(8,128)(2,1)} %collective-permute-done.29.refs_2_, ...), custom_call_target="tpu_custom_call" | custom-call | tf_op jit(solution)/shard_map/project_kernel/pallas_call | solution.py:347
  249.7 46.7 %reduce-scatter.7.cloned.1.call-done = bf16[128,2304]{1,0:T(8,128)(2,1)} async-done(((bf16[512,2304]{1,0:T(8,128)(2,1)}), bf16[128,2304]{1,0:T(8,128)(2,1)}) %reduce-scatter.7.cloned.1.call-update) | async-done | bytes 589840 | tf_op jit(solution)/shard_map/reduce_scatter | solution.py:792
  323.7 24.0 %all-gather.7.cloned.1.call-done.f_h = bf16[512,2304]{1,0:T(8,128)(2,1)} async-done(((bf16[128,2304]{1,0:T(8,128)(2,1)}), bf16[512,2304]{1,0:T(8,128)(2,1)}) %all-gather.7.cloned.1.call-update) | async-done | bytes 2359312 | tf_op jit(solution)/shard_map/all_gather | solution.py:799
  347.8 27.3 %ffn_back_kernel.1 = (bf16[512,2304]{1,0:T(8,128)(2,1)}, bf16[512,2304]{1,0:T(8,128)(2,1)}, bf16[512,2304]{1,0:T(8,128)(2,1)}, bf16[512,2304]{1,0:T(8,128)(2,1)}, f32[1,2304]{1,0:T(1,128)}) custom-call(bf16[512,2304]{1,0:T(8,128)(2,1)} %all-gather.7.cloned.1.call-done.f_h, f32[512,2304]{1,0:T(8,128)} %get-tuple-element.612.x2_h.x_r, ...), custom_call_target="tpu_custom_call" | custom-call | tf_op jit(solution)/shard_map/ffn_back_kernel/pallas_call | solution.py:347
  375.0 21.2 %ffn_inputs_kernel.1 = bf16[512,2304]{1,0:T(8,128)(2,1)} custom-call(bf16[512,2304]{1,0:T(8,128)(2,1)} %get-tuple-element.590.dg_r.b_h, bf16[512,2304]{1,0:T(8,128)(2,1)} %get-tuple-element.649.du_r.b_h, bf16[288,2304]{1,0:T(8,128)(2,1)} %refs_0_.3, bf16[288,2304]{1,0:T(8,128)(2,1)} %collective-permute-done.10.refs_1_, ...), custom_call_target="tpu_custom_call" | custom-call | tf_op jit(solution)/shard_map/ffn_inputs_kernel/pallas_call | solution.py:347
  412.8 9.2 %outer_kernel.12 = (bf16[288,2304]{1,0:T(8,128)(2,1)}, bf16[288,2304]{1,0:T(8,128)(2,1)}, bf16[288,2304]{1,0:T(8,128)(2,1)}, bf16[144,2304]{1,0:T(8,128)(2,1)}, bf16[144,2304]{1,0:T(8,128)(2,1)}) custom-call(bf16[512,2304]{1,0:T(8,128)(2,1)} %get-tuple-element.573.a_h, bf16[512,2304]{1,0:T(8,128)(2,1)} %get-tuple-element.574.u_r.b_h, ...), custom_call_target="tpu_custom_call" | custom-call | tf_op jit(solution)/shard_map/outer_kernel/pallas_call | solution.py:347
  432.0 9.1 %outer_kernel.14 = (bf16[288,2304]{1,0:T(8,128)(2,1)}, bf16[288,2304]{1,0:T(8,128)(2,1)}, bf16[288,2304]{1,0:T(8,128)(2,1)}, bf16[144,2304]{1,0:T(8,128)(2,1)}, bf16[144,2304]{1,0:T(8,128)(2,1)}) custom-call(bf16[512,2304]{1,0:T(8,128)(2,1)} %get-tuple-element.648.a_h, bf16[512,2304]{1,0:T(8,128)(2,1)} %get-tuple-element.590.dg_r.b_h, ...), custom_call_target="tpu_custom_call" | custom-call | tf_op jit(solution)/shard_map/outer_kernel/pallas_call | solution.py:347
  453.3 8.7 %collective-permute-done.44.gy_r = bf16[144,2304]{1,0:T(8,128)(2,1)S(1)} collective-permute-done((bf16[144,2304]{1,0:T(8,128)(2,1)}, bf16[144,2304]{1,0:T(8,128)(2,1)S(1)}, u32[]{:S(2)}, u32[]{:S(2)}) %collective-permute-start.44) | collective-permute-done | bytes 663584 | tf_op jit(solution)/shard_map/ppermute | solution.py:54
  470.1 24.6 %all-gather.9.cloned.1.call-done.d_r = bf16[512,2304]{1,0:T(8,128)(2,1)} async-done(((bf16[128,2304]{1,0:T(8,128)(2,1)}), bf16[512,2304]{1,0:T(8,128)(2,1)}) %all-gather.9.cloned.1.call-update) | async-done | bytes 2359312 | tf_op jit(solution)/shard_map/all_gather | solution.py:799
  494.7 19.0 %attn_back_kernel.1 = (f32[512,2304]{1,0:T(8,128)}, bf16[512,2304]{1,0:T(8,128)(2,1)}, bf16[512,512]{1,0:T(8,128)(2,1)}, f32[512,512]{1,0:T(8,128)}, bf16[512,512]{1,0:T(8,128)(2,1)}, /*index=5*/f32[8,2304]{1,0:T(8,128)}) custom-call(bf16[512,2304]{1,0:T(8,128)(2,1)} %all-gather.9.cloned.1.call-done.d_r, f32[512,2304]{1,0:T(8,128)} %get-tuple-element.612.x2_h.x_r, ...), custom_call_target="tpu_custom_call" | custom-call | flops 999999995904 | tf_op jit(solution)/shard_map/attn_back_kernel/pallas_call | solution.py:120
  531.3 7.2 %project_kernel.3 = bf16[512,2304]{1,0:T(8,128)(2,1)} custom-call(bf16[512,1024]{1,0:T(8,128)(2,1)} %keys_back_kernel.1.u_r.b_h, bf16[2304,1024]{1,0:T(8,128)(2,1)} %slice_dynamic-update-slice_fusion.refs_0_), custom_call_target="tpu_custom_call" | custom-call | tf_op jit(solution)/shard_map/project_kernel/pallas_call | solution.py:347
  541.8 9.7 %outer_kernel.15 = (bf16[288,2304]{1,0:T(8,128)(2,1)}, bf16[288,2304]{1,0:T(8,128)(2,1)}, bf16[288,2304]{1,0:T(8,128)(2,1)}, bf16[144,2304]{1,0:T(8,128)(2,1)}, bf16[144,2304]{1,0:T(8,128)(2,1)}) custom-call(bf16[512,2304]{1,0:T(8,128)(2,1)} %get-tuple-element.648.a_h, bf16[512,2304]{1,0:T(8,128)(2,1)} %get-tuple-element.649.du_r.b_h, ...), custom_call_target="tpu_custom_call" | custom-call | tf_op jit(solution)/shard_map/outer_kernel/pallas_call | solution.py:347
  561.4 7.6 %shard_map.250.dx_r = f32[512,2304]{1,0:T(8,128)} custom-call(s32[3]{0:T(128)} %pad_add_fusion.1.b_r, f32[512,2304]{1,0:T(8,128)} %get-tuple-element.669.v_r), custom_call_target="tpu_custom_call" | custom-call | tf_op jit(solution)/shard_map/pallas_call | solution.py:714
  612.9 8.8 %collective-permute-done.63.y_r = bf16[288,2304]{1,0:T(8,128)(2,1)S(1)} collective-permute-done((bf16[288,2304]{1,0:T(8,128)(2,1)}, bf16[288,2304]{1,0:T(8,128)(2,1)S(1)}, u32[]{:S(2)}, u32[]{:S(2)}) %collective-permute-start.63) | collective-permute-done | bytes 1327136 | tf_op jit(solution)/shard_map/ppermute | solution.py:54
  641.8 7.8 %last_kernel.1 = (f32[512,2304]{1,0:T(8,128)}, f32[1,2304]{1,0:T(1,128)}) custom-call(bf16[512,2304]{1,0:T(8,128)(2,1)} %bitcast.11, f32[1,2304]{1,0:T(1,128)} %slice.175.g_r, bf16[512,2304]{1,0:T(8,128)(2,1)} %all-gather.11.cloned.1.call-done.d_r, f32[512,2304]{1,0:T(8,128)} %shard_map.250.dx_r), custom_call_target="tpu_custom_call" | custom-call | tf_op jit(solution)/shard_map/last_kernel/pallas_call | solution.py:120
  (373 shorter events, 280.6 us)
Async XLA Ops:
  7.2 146.2 %reduce-scatter.5.cloned.1.call-start = ((), (), s32[]{:S(2)}) async-start(), calls=%async_computation.4 | async-start | bytes 2949120 | tf_op jit(solution)/shard_map/reduce_scatter | solution.py:792
  17.4 33.6 %collective-permute-start.4 = (bf16[304,1536]{1,0:T(8,128)(2,1)S(1)}, bf16[304,1536]{1,0:T(8,128)(2,1)}, u32[]{:S(2)}, u32[]{:S(2)}) collective-permute-start(bf16[304,1536]{1,0:T(8,128)(2,1)S(1)} %maximum_maximum_fusion.refs_0_), channel_id=1, source_target_pairs={{0,8},{8,0},{1,9},{9,1},{2,10},{10,2},{3,11},{11,3},{4,12},{12,4},... | collective-permute-start | bytes 2801672 | tf_op jit(solution)/shard_map/ppermute | solution.py:58
  52.4 32.4 %collective-permute-start.10 = (bf16[288,2304]{1,0:T(8,128)(2,1)}, bf16[288,2304]{1,0:T(8,128)(2,1)}, u32[]{:S(2)}, u32[]{:S(2)}) collective-permute-start(bf16[288,2304]{1,0:T(8,128)(2,1)} %refs_0_.3), channel_id=1, source_target_pairs={{0,4},{4,0},{1,5},{5,1},{2,6},{6,2},{3,7},{7,3},{8,12},{12,8},{9,1... | collective-permute-start | bytes 3981320 | tf_op jit(solution)/shard_map/ppermute | solution.py:50
  103.6 108.3 %all-gather.5.cloned.1.call-start = ((), (), s32[]{:S(2)}) async-start(), calls=%async_computation.5 | async-start | bytes 2949120 | tf_op jit(solution)/shard_map/all_gather | solution.py:799
  122.7 46.2 %collective-permute-start.16 = (bf16[288,2304]{1,0:T(8,128)(2,1)}, bf16[288,2304]{1,0:T(8,128)(2,1)}, u32[]{:S(2)}, u32[]{:S(2)}) collective-permute-start(bf16[288,2304]{1,0:T(8,128)(2,1)} %refs_0_.3), channel_id=1, source_target_pairs={{0,8},{8,0},{1,9},{9,1},{2,10},{10,2},{3,11},{11,3},{4,12},{12,4},... | collective-permute-start | bytes 3981320 | tf_op jit(solution)/shard_map/ppermute | solution.py:58
  153.4 142.9 %reduce-scatter.7.cloned.1.call-start = ((), (), s32[]{:S(2)}) async-start(), calls=%async_computation.6 | async-start | bytes 2949120 | tf_op jit(solution)/shard_map/reduce_scatter | solution.py:792
  168.9 31.9 %collective-permute-start.29 = (bf16[288,2304]{1,0:T(8,128)(2,1)}, bf16[288,2304]{1,0:T(8,128)(2,1)}, u32[]{:S(2)}, u32[]{:S(2)}) collective-permute-start(bf16[288,2304]{1,0:T(8,128)(2,1)} %refs_0_.2), channel_id=1, source_target_pairs={{0,16},{16,0},{1,17},{17,1},{2,18},{18,2},{3,19},{19,3},{4,20},{20... | collective-permute-start | bytes 3981320 | tf_op jit(solution)/shard_map/ppermute | solution.py:54
  171.9 34.1 %collective-permute-start.23 = (bf16[288,2304]{1,0:T(8,128)(2,1)}, bf16[288,2304]{1,0:T(8,128)(2,1)S(1)}, u32[]{:S(2)}, u32[]{:S(2)}) collective-permute-start(bf16[288,2304]{1,0:T(8,128)(2,1)} %refs_10_.1), channel_id=1, source_target_pairs={{0,8},{8,0},{1,9},{9,1},{2,10},{10,2},{3,11},{11,3},{4,12},{12,4},... | collective-permute-start | bytes 3981320 | tf_op jit(solution)/shard_map/ppermute | solution.py:58
  172.0 35.6 %collective-permute-start.25 = (bf16[288,2304]{1,0:T(8,128)(2,1)S(1)}, bf16[288,2304]{1,0:T(8,128)(2,1)S(1)}, u32[]{:S(2)}, u32[]{:S(2)}) collective-permute-start(bf16[288,2304]{1,0:T(8,128)(2,1)S(1)} %collective-permute-done.15.refs_12_), channel_id=1, source_target_pairs={{0,8},{8,0},{1,9},{9,1},{2,10},{10,2},{3,11},{11,3},{4,12},{12,4},... | collective-permute-start | bytes 3981320 | tf_op jit(solution)/shard_map/ppermute | solution.py:58
  174.3 34.1 %collective-permute-start.24 = (bf16[288,2304]{1,0:T(8,128)(2,1)S(1)}, bf16[288,2304]{1,0:T(8,128)(2,1)S(1)}, u32[]{:S(2)}, u32[]{:S(2)}) collective-permute-start(bf16[288,2304]{1,0:T(8,128)(2,1)S(1)} %collective-permute-done.14.refs_11_), channel_id=1, source_target_pairs={{0,8},{8,0},{1,9},{9,1},{2,10},{10,2},{3,11},{11,3},{4,12},{12,4},... | collective-permute-start | bytes 3981320 | tf_op jit(solution)/shard_map/ppermute | solution.py:58
  249.6 98.2 %all-gather.7.cloned.1.call-start = ((), (), s32[]{:S(2)}) async-start(), calls=%async_computation.7 | async-start | bytes 2949120 | tf_op jit(solution)/shard_map/all_gather | solution.py:799
  296.3 146.9 %reduce-scatter.9.cloned.1.call-start = ((), (), s32[]{:S(2)}) async-start(), calls=%async_computation.8 | async-start | bytes 2949120 | tf_op jit(solution)/shard_map/reduce_scatter | solution.py:792
  396.3 98.4 %all-gather.9.cloned.1.call-start = ((), (), s32[]{:S(2)}) async-start(), calls=%async_computation.9 | async-start | bytes 2949120 | tf_op jit(solution)/shard_map/all_gather | solution.py:799
  443.3 145.6 %reduce-scatter.11.cloned.1.call-start = ((), (), s32[]{:S(2)}) async-start(), calls=%async_computation.10 | async-start | bytes 2949120 | tf_op jit(solution)/shard_map/reduce_scatter | solution.py:792
  446.9 68.4 %collective-permute-start.49 = (bf16[144,2304]{1,0:T(8,128)(2,1)}, bf16[144,2304]{1,0:T(8,128)(2,1)}, u32[]{:S(2)}, u32[]{:S(2)}) collective-permute-start(bf16[144,2304]{1,0:T(8,128)(2,1)} %get-tuple-element.599), channel_id=1, source_target_pairs={{0,16},{16,0},{1,17},{17,1},{2,18},{18,2},{3,19},{19,3},{4,20},{20... | collective-permute-start | bytes 1990664 | tf_op jit(solution)/shard_map/ppermute | solution.py:54
  461.9 53.4 %collective-permute-start.48 = (bf16[144,2304]{1,0:T(8,128)(2,1)}, bf16[144,2304]{1,0:T(8,128)(2,1)}, u32[]{:S(2)}, u32[]{:S(2)}) collective-permute-start(bf16[144,2304]{1,0:T(8,128)(2,1)} %get-tuple-element.598), channel_id=1, source_target_pairs={{0,4},{4,0},{1,5},{5,1},{2,6},{6,2},{3,7},{7,3},{8,12},{12,8},{9,1... | collective-permute-start | bytes 1990664 | tf_op jit(solution)/shard_map/ppermute | solution.py:50
  467.8 51.9 %collective-permute-start.46 = (bf16[288,2304]{1,0:T(8,128)(2,1)}, bf16[288,2304]{1,0:T(8,128)(2,1)}, u32[]{:S(2)}, u32[]{:S(2)}) collective-permute-start(bf16[288,2304]{1,0:T(8,128)(2,1)} %get-tuple-element.607), channel_id=1, source_target_pairs={{0,4},{4,0},{1,5},{5,1},{2,6},{6,2},{3,7},{7,3},{8,12},{12,8},{9,1... | collective-permute-start | bytes 3981320 | tf_op jit(solution)/shard_map/ppermute | solution.py:50
  468.6 51.1 %collective-permute-start.47 = (bf16[288,2304]{1,0:T(8,128)(2,1)}, bf16[288,2304]{1,0:T(8,128)(2,1)}, u32[]{:S(2)}, u32[]{:S(2)}) collective-permute-start(bf16[288,2304]{1,0:T(8,128)(2,1)} %get-tuple-element.608), channel_id=1, source_target_pairs={{0,16},{16,0},{1,17},{17,1},{2,18},{18,2},{3,19},{19,3},{4,20},{20... | collective-permute-start | bytes 3981320 | tf_op jit(solution)/shard_map/ppermute | solution.py:54
  538.6 103.2 %all-gather.11.cloned.1.call-start = ((), (), s32[]{:S(2)}) async-start(), calls=%async_computation.11 | async-start | bytes 2949120 | tf_op jit(solution)/shard_map/all_gather | solution.py:799
  538.8 32.3 %collective-permute-start.53 = (bf16[288,2304]{1,0:T(8,128)(2,1)}, bf16[288,2304]{1,0:T(8,128)(2,1)S(1)}, u32[]{:S(2)}, u32[]{:S(2)}) collective-permute-start(bf16[288,2304]{1,0:T(8,128)(2,1)} %get-tuple-element.637), channel_id=1, source_target_pairs={{0,16},{16,0},{1,17},{17,1},{2,18},{18,2},{3,19},{19,3},{4,20},{20... | collective-permute-start | bytes 3981320 | tf_op jit(solution)/shard_map/ppermute | solution.py:54
  540.4 32.3 %collective-permute-start.52 = (bf16[288,2304]{1,0:T(8,128)(2,1)}, bf16[288,2304]{1,0:T(8,128)(2,1)S(1)}, u32[]{:S(2)}, u32[]{:S(2)}) collective-permute-start(bf16[288,2304]{1,0:T(8,128)(2,1)} %get-tuple-element.636), channel_id=1, source_target_pairs={{0,4},{4,0},{1,5},{5,1},{2,6},{6,2},{3,7},{7,3},{8,12},{12,8},{9,1... | collective-permute-start | bytes 3981320 | tf_op jit(solution)/shard_map/ppermute | solution.py:50
  552.1 32.5 %collective-permute-start.50 = (bf16[144,2304]{1,0:T(8,128)(2,1)}, bf16[144,2304]{1,0:T(8,128)(2,1)}, u32[]{:S(2)}, u32[]{:S(2)}) collective-permute-start(bf16[144,2304]{1,0:T(8,128)(2,1)} %get-tuple-element.657), channel_id=1, source_target_pairs={{0,4},{4,0},{1,5},{5,1},{2,6},{6,2},{3,7},{7,3},{8,12},{12,8},{9,1... | collective-permute-start | bytes 1990664 | tf_op jit(solution)/shard_map/ppermute | solution.py:50
  589.6 32.1 %collective-permute-start.63 = (bf16[288,2304]{1,0:T(8,128)(2,1)}, bf16[288,2304]{1,0:T(8,128)(2,1)S(1)}, u32[]{:S(2)}, u32[]{:S(2)}) collective-permute-start(bf16[288,2304]{1,0:T(8,128)(2,1)} %get-tuple-element.679), channel_id=1, source_target_pairs={{0,16},{16,0},{1,17},{17,1},{2,18},{18,2},{3,19},{19,3},{4,20},{20... | collective-permute-start | bytes 3981320 | tf_op jit(solution)/shard_map/ppermute | solution.py:54
  590.6 35.0 %collective-permute-start.62 = (bf16[288,2304]{1,0:T(8,128)(2,1)}, bf16[288,2304]{1,0:T(8,128)(2,1)S(1)}, u32[]{:S(2)}, u32[]{:S(2)}) collective-permute-start(bf16[288,2304]{1,0:T(8,128)(2,1)} %get-tuple-element.678), channel_id=1, source_target_pairs={{0,4},{4,0},{1,5},{5,1},{2,6},{6,2},{3,7},{7,3},{8,12},{12,8},{9,1... | collective-permute-start | bytes 3981320 | tf_op jit(solution)/shard_map/ppermute | solution.py:50
  (121 other events, 1634.8 us)
Sparse Core Ops, SparseCore 0:
  103.7 48.3 reduce-scatter.4
  153.7 51.3 all-gather.4
  249.7 46.5 reduce-scatter.6
  297.7 49.9 all-gather.6
  396.4 46.8 reduce-scatter.8
  444.7 49.9 all-gather.8
  538.7 46.9 reduce-scatter.10
  589.1 49.2 all-gather.10

commit v7 on v5

--- a/solution.py
+++ b/solution.py
@@ -642,7 +642,7 @@
 
 def last_kernel(x, gain, dh1, dx2):
     rows, width = x.shape
-    br = min(rows, 128)
+    br = min(rows, 256)
 
     def body(x_r, g_r, d_r, dx_r, o_r, dg_r):
         def step(at, total):
@@ -1001,13 +1001,13 @@
         z1.middle()
         so.first()
         sq.first()
+        up_grad = su.end()
         so.second()
         sq.second()
         input_grad, dg1 = seq.run(last_kernel, x_raw, g1_g, z1.out, dx2)
         dg1 = seq.run(order, jnp.broadcast_to(dg1, (16, width)))[:1]
         dgain = jnp.concatenate([dg1, dg23[:2], dg4], axis=0)
         got = seq.send(to_core, dgain[:, mid:])
-        up_grad = su.end()
         dgain = seq.run(lambda a, b: a[:, :mid] + b, dgain, got)
         if square:
             got = seq.send(to_y, dgain[:, mid // 2 :])

time: 695 us -> 696 us (level)
    unnamed x121 -> x133, local copies, waits for them, and re-layouts: 21.9 us -> 23.3 us
  transfers between devices with their start and end apart: 79 -> 79, of which waited for: 34 -> 34; matrix products, arithmetic and copies ran while one was open for 6% -> 6% of each run, Pallas kernels for 29% -> 28%
where the time goes in v7:
time: 696 us; the launch traced here: 686 us
  waiting for transfers between devices  277 us (40%)
  Pallas kernels  273 us (39%)
  local copies, waits for them, and re-layouts  59.4 us (9%)
  starting transfers between devices  52.9 us (8%)
  between operations  15.4 us (2%)
  other arithmetic  8.18 us (1%)
    pallas_call x16, Pallas kernels, streaming(): pl.pallas_call(body, in_specs=[place[p] for _, p in ins], out_specs=[plac...  167 us
    ppermute x19, waiting for transfers between devices, to_y(): return lax.ppermute(a, 'y', SWAP)  122 us
    pallas_call x14, Pallas kernels, kernel(): pl.pallas_call(body, grid=grid, in_specs=[spec(*e[1:]) for e in ins], out...  76.7 us
    all_gather x4, waiting for transfers between devices, middle(): self.out = lax.all_gather(own, 'tensor', axis=0, tiled=True)  53.9 us
    reduce_scatter x4, waiting for transfers between devices, __init__(): self.own = lax.psum_scatter(part, 'tensor', scatter_dimension=0, tiled=True)  48.9 us
    ppermute x21, waiting for transfers between devices, to_ctx(): return lax.ppermute(a, 'ctx', SWAP)  44.8 us
    pallas_call x6, Pallas kernels, order_kernel(): pl.pallas_call(body, grid=(rows // br,), in_specs=[pl.BlockSpec(memory_sp...  29.7 us
    ppermute x21, starting transfers between devices, to_ctx(): return lax.ppermute(a, 'ctx', SWAP)  25.2 us
  transfers between devices with their start and end apart: 79, of which 34 were waited for; matrix products, arithmetic and copies ran while one was open for 6% of the time, Pallas kernels for 28%

profile of v7, /device:TPU:0, one launch (start us, length us, event | category | flops | bytes accessed | tf_op | source)
XLA Modules:
  0.0 685.9 jit_solution(13509832798639349232)
XLA Ops:
  24.6 12.1 %collective-permute-done.1.refs_2_ = bf16[304,1536]{1,0:T(8,128)(2,1)S(1)} collective-permute-done((bf16[304,1536]{1,0:T(8,128)(2,1)S(1)}, bf16[304,1536]{1,0:T(8,128)(2,1)S(1)}, u32[]{:S(2)}, u32[]{:S(2)}) %collective-permute-start.1) | collective-permute-done | bytes 933920 | tf_op jit(solution)/shard_map/ppermute | solution.py:54
  55.8 9.6 %first_kernel.1 = (bf16[512,2304]{1,0:T(8,128)(2,1)}, bf16[512,512]{1,0:T(8,128)(2,1)}, bf16[512,512]{1,0:T(8,128)(2,1)}, f32[8,2304]{1,0:T(8,128)}, bf16[2304,1...) custom-call(bf16[512,2304]{1,0:T(8,128)(2,1)} %get-tuple-element.463.x_r.x_h, f32[512,128]{1,0:T(8,128)} %get-tuple-element.396.r_r, ...), custom_call_target="tpu_custom_call" | custom-call | flops 999999995904 | tf_op jit(solution)/shard_map/first_kernel/pallas_call | solution.py:326
  66.0 16.4 %collective-permute-done.11.refs_2_ = bf16[288,2304]{1,0:T(8,128)(2,1)} collective-permute-done((bf16[288,2304]{1,0:T(8,128)(2,1)}, bf16[288,2304]{1,0:T(8,128)(2,1)}, u32[]{:S(2)}, u32[]{:S(2)}) %collective-permute-start.11) | collective-permute-done | bytes 1327136 | tf_op jit(solution)/shard_map/ppermute | solution.py:54
  95.7 7.8 %attn_kernel.1 = (bf16[512,512]{1,0:T(8,128)(2,1)}, f32[512,256]{1,0:T(8,128)}, bf16[512,2304]{1,0:T(8,128)(2,1)}) custom-call(bf16[512,512]{1,0:T(8,128)(2,1)} %get-tuple-element.606.q_r, bf16[1024,512]{1,0:T(8,128)(2,1)} %copy-done.43, bf16[512,1024]{1,0:T(8,128)(2,1)} %and_convert_fusion.m_r, bf16[2304,512]{1,0:T(8,128)(2,1)} %get-tuple-element.605.w_r), custom_call_target="tpu_custom_call" | custom-call | flops 999999995904 | tf_op jit(solution)/shard_map/attn_kernel/pallas_call | solution.py:120
  106.7 13.5 %collective-permute-done.13.refs_4_ = bf16[144,2304]{1,0:T(8,128)(2,1)S(1)} collective-permute-done((bf16[144,2304]{1,0:T(8,128)(2,1)S(1)}, bf16[144,2304]{1,0:T(8,128)(2,1)S(1)}, u32[]{:S(2)}, u32[]{:S(2)}) %collective-permute-start.13) | collective-permute-done | bytes 663584 | tf_op jit(solution)/shard_map/ppermute | solution.py:50
  122.7 27.8 %collective-permute-done.15.refs_12_ = bf16[288,2304]{1,0:T(8,128)(2,1)S(1)} collective-permute-done((bf16[288,2304]{1,0:T(8,128)(2,1)}, bf16[288,2304]{1,0:T(8,128)(2,1)S(1)}, u32[]{:S(2)}, u32[]{:S(2)}) %collective-permute-start.15) | collective-permute-done | bytes 1327136 | tf_op jit(solution)/shard_map/ppermute | solution.py:54
  155.3 11.0 %collective-permute-done.22.refs_14_ = bf16[144,2304]{1,0:T(8,128)(2,1)} collective-permute-done((bf16[144,2304]{1,0:T(8,128)(2,1)}, bf16[144,2304]{1,0:T(8,128)(2,1)}, u32[]{:S(2)}, u32[]{:S(2)}) %collective-permute-start.22) | collective-permute-done | bytes 663584 | tf_op jit(solution)/shard_map/ppermute | solution.py:50
  174.6 26.2 %collective-permute-done.29.refs_2_ = bf16[288,2304]{1,0:T(8,128)(2,1)} collective-permute-done((bf16[288,2304]{1,0:T(8,128)(2,1)}, bf16[288,2304]{1,0:T(8,128)(2,1)}, u32[]{:S(2)}, u32[]{:S(2)}) %collective-permute-start.29) | collective-permute-done | bytes 1327136 | tf_op jit(solution)/shard_map/ppermute | solution.py:54
  211.8 21.3 %ffn_in_kernel.1 = (f32[512,2304]{1,0:T(8,128)}, bf16[512,2304]{1,0:T(8,128)(2,1)}, bf16[512,4608]{1,0:T(8,128)(2,1)}, bf16[512,2304]{1,0:T(8,128)(2,1)}) custom-call(bf16[512,2304]{1,0:T(8,128)(2,1)} %all-gather.5.cloned.1.call-done.a_h.a_r, bf16[512,2304]{1,0:T(8,128)(2,1)} %get-tuple-element.463.x_r.x_h, f32[1,2304]{1,0:T(1,128)} %get-tuple-element.604.g2_r, ...), custom_call_target="tpu_custom_call" | custom-call | tf_op jit(solution)/shard_map/ffn_in_kernel/pallas_call | solution.py:326
  237.3 12.0 %project_kernel.2 = bf16[512,2304]{1,0:T(8,128)(2,1)} custom-call(bf16[512,2304]{1,0:T(8,128)(2,1)} %get-tuple-element.562.u_r.b_h, bf16[288,2304]{1,0:T(8,128)(2,1)} %refs_0_.2, bf16[288,2304]{1,0:T(8,128)(2,1)} %collective-permute-done.28.refs_1_, bf16[288,2304]{1,0:T(8,128)(2,1)} %collective-permute-done.29.refs_2_, ...), custom_call_target="tpu_custom_call" | custom-call | tf_op jit(solution)/shard_map/project_kernel/pallas_call | solution.py:326
  249.4 46.7 %reduce-scatter.7.cloned.1.call-done = bf16[128,2304]{1,0:T(8,128)(2,1)} async-done(((bf16[512,2304]{1,0:T(8,128)(2,1)}), bf16[128,2304]{1,0:T(8,128)(2,1)}) %reduce-scatter.7.cloned.1.call-update) | async-done | bytes 589840 | tf_op jit(solution)/shard_map/reduce_scatter | solution.py:771
  318.3 29.2 %all-gather.7.cloned.1.call-done.f_h = bf16[512,2304]{1,0:T(8,128)(2,1)} async-done(((bf16[128,2304]{1,0:T(8,128)(2,1)}), bf16[512,2304]{1,0:T(8,128)(2,1)}) %all-gather.7.cloned.1.call-update) | async-done | bytes 2359312 | tf_op jit(solution)/shard_map/all_gather | solution.py:778
  347.5 27.2 %ffn_back_kernel.1 = (bf16[512,2304]{1,0:T(8,128)(2,1)}, bf16[512,2304]{1,0:T(8,128)(2,1)}, bf16[512,2304]{1,0:T(8,128)(2,1)}, bf16[512,2304]{1,0:T(8,128)(2,1)}, f32[1,2304]{1,0:T(1,128)}) custom-call(bf16[512,2304]{1,0:T(8,128)(2,1)} %all-gather.7.cloned.1.call-done.f_h, f32[512,2304]{1,0:T(8,128)} %get-tuple-element.600.x2_h.x_r, ...), custom_call_target="tpu_custom_call" | custom-call | tf_op jit(solution)/shard_map/ffn_back_kernel/pallas_call | solution.py:326
  374.8 21.2 %ffn_inputs_kernel.1 = bf16[512,2304]{1,0:T(8,128)(2,1)} custom-call(bf16[512,2304]{1,0:T(8,128)(2,1)} %get-tuple-element.578.dg_r.b_h, bf16[512,2304]{1,0:T(8,128)(2,1)} %get-tuple-element.637.du_r.b_h, bf16[288,2304]{1,0:T(8,128)(2,1)} %refs_0_.3, bf16[288,2304]{1,0:T(8,128)(2,1)} %collective-permute-done.10.refs_1_, ...), custom_call_target="tpu_custom_call" | custom-call | tf_op jit(solution)/shard_map/ffn_inputs_kernel/pallas_call | solution.py:326
  412.6 9.1 %outer_kernel.12 = (bf16[288,2304]{1,0:T(8,128)(2,1)}, bf16[288,2304]{1,0:T(8,128)(2,1)}, bf16[288,2304]{1,0:T(8,128)(2,1)}, bf16[144,2304]{1,0:T(8,128)(2,1)}, bf16[144,2304]{1,0:T(8,128)(2,1)}) custom-call(bf16[512,2304]{1,0:T(8,128)(2,1)} %get-tuple-element.561.a_h, bf16[512,2304]{1,0:T(8,128)(2,1)} %get-tuple-element.562.u_r.b_h, ...), custom_call_target="tpu_custom_call" | custom-call | tf_op jit(solution)/shard_map/outer_kernel/pallas_call | solution.py:326
  431.7 9.1 %outer_kernel.14 = (bf16[288,2304]{1,0:T(8,128)(2,1)}, bf16[288,2304]{1,0:T(8,128)(2,1)}, bf16[288,2304]{1,0:T(8,128)(2,1)}, bf16[144,2304]{1,0:T(8,128)(2,1)}, bf16[144,2304]{1,0:T(8,128)(2,1)}) custom-call(bf16[512,2304]{1,0:T(8,128)(2,1)} %get-tuple-element.636.a_h, bf16[512,2304]{1,0:T(8,128)(2,1)} %get-tuple-element.578.dg_r.b_h, ...), custom_call_target="tpu_custom_call" | custom-call | tf_op jit(solution)/shard_map/outer_kernel/pallas_call | solution.py:326
  453.0 8.6 %collective-permute-done.44.gy_r = bf16[144,2304]{1,0:T(8,128)(2,1)S(1)} collective-permute-done((bf16[144,2304]{1,0:T(8,128)(2,1)}, bf16[144,2304]{1,0:T(8,128)(2,1)S(1)}, u32[]{:S(2)}, u32[]{:S(2)}) %collective-permute-start.44) | collective-permute-done | bytes 663584 | tf_op jit(solution)/shard_map/ppermute | solution.py:54
  469.8 24.6 %all-gather.9.cloned.1.call-done.d_r = bf16[512,2304]{1,0:T(8,128)(2,1)} async-done(((bf16[128,2304]{1,0:T(8,128)(2,1)}), bf16[512,2304]{1,0:T(8,128)(2,1)}) %all-gather.9.cloned.1.call-update) | async-done | bytes 2359312 | tf_op jit(solution)/shard_map/all_gather | solution.py:778
  494.4 20.3 %attn_back_kernel.1 = (f32[512,2304]{1,0:T(8,128)}, bf16[512,2304]{1,0:T(8,128)(2,1)}, bf16[512,512]{1,0:T(8,128)(2,1)}, f32[512,512]{1,0:T(8,128)}, bf16[512,512]{1,0:T(8,128)(2,1)}, /*index=5*/f32[8,2304]{1,0:T(8,128)}) custom-call(bf16[512,2304]{1,0:T(8,128)(2,1)} %all-gather.9.cloned.1.call-done.d_r, f32[512,2304]{1,0:T(8,128)} %get-tuple-element.600.x2_h.x_r, ...), custom_call_target="tpu_custom_call" | custom-call | flops 999999995904 | tf_op jit(solution)/shard_map/attn_back_kernel/pallas_call | solution.py:120
  532.3 7.2 %project_kernel.3 = bf16[512,2304]{1,0:T(8,128)(2,1)} custom-call(bf16[512,1024]{1,0:T(8,128)(2,1)} %keys_back_kernel.1.u_r.b_h, bf16[2304,1024]{1,0:T(8,128)(2,1)} %slice_dynamic-update-slice_fusion.refs_0_), custom_call_target="tpu_custom_call" | custom-call | tf_op jit(solution)/shard_map/project_kernel/pallas_call | solution.py:326
  542.8 9.5 %outer_kernel.15 = (bf16[288,2304]{1,0:T(8,128)(2,1)}, bf16[288,2304]{1,0:T(8,128)(2,1)}, bf16[288,2304]{1,0:T(8,128)(2,1)}, bf16[144,2304]{1,0:T(8,128)(2,1)}, bf16[144,2304]{1,0:T(8,128)(2,1)}) custom-call(bf16[512,2304]{1,0:T(8,128)(2,1)} %get-tuple-element.636.a_h, bf16[512,2304]{1,0:T(8,128)(2,1)} %get-tuple-element.637.du_r.b_h, ...), custom_call_target="tpu_custom_call" | custom-call | tf_op jit(solution)/shard_map/outer_kernel/pallas_call | solution.py:326
  562.2 7.6 %shard_map.250.dx_r = f32[512,2304]{1,0:T(8,128)} custom-call(s32[3]{0:T(128)} %pad_add_fusion.1.b_r, f32[512,2304]{1,0:T(8,128)} %get-tuple-element.657.v_r), custom_call_target="tpu_custom_call" | custom-call | tf_op jit(solution)/shard_map/pallas_call | solution.py:693
  613.9 8.8 %collective-permute-done.63.y_r = bf16[288,2304]{1,0:T(8,128)(2,1)S(1)} collective-permute-done((bf16[288,2304]{1,0:T(8,128)(2,1)}, bf16[288,2304]{1,0:T(8,128)(2,1)S(1)}, u32[]{:S(2)}, u32[]{:S(2)}) %collective-permute-start.63) | collective-permute-done | bytes 1327136 | tf_op jit(solution)/shard_map/ppermute | solution.py:54
  642.8 7.8 %last_kernel.1 = (f32[512,2304]{1,0:T(8,128)}, f32[1,2304]{1,0:T(1,128)}) custom-call(bf16[512,2304]{1,0:T(8,128)(2,1)} %bitcast.11, f32[1,2304]{1,0:T(1,128)} %slice.175.g_r, bf16[512,2304]{1,0:T(8,128)(2,1)} %all-gather.11.cloned.1.call-done.d_r, f32[512,2304]{1,0:T(8,128)} %shard_map.250.dx_r), custom_call_target="tpu_custom_call" | custom-call | tf_op jit(solution)/shard_map/last_kernel/pallas_call | solution.py:120
  (372 shorter events, 275.6 us)
Async XLA Ops:
  7.2 146.1 %reduce-scatter.5.cloned.1.call-start = ((), (), s32[]{:S(2)}) async-start(), calls=%async_computation.4 | async-start | bytes 2949120 | tf_op jit(solution)/shard_map/reduce_scatter | solution.py:771
  17.4 33.6 %collective-permute-start.4 = (bf16[304,1536]{1,0:T(8,128)(2,1)S(1)}, bf16[304,1536]{1,0:T(8,128)(2,1)}, u32[]{:S(2)}, u32[]{:S(2)}) collective-permute-start(bf16[304,1536]{1,0:T(8,128)(2,1)S(1)} %maximum_maximum_fusion.refs_0_), channel_id=1, source_target_pairs={{0,8},{8,0},{1,9},{9,1},{2,10},{10,2},{3,11},{11,3},{4,12},{12,4},... | collective-permute-start | bytes 2801672 | tf_op jit(solution)/shard_map/ppermute | solution.py:58
  52.4 32.4 %collective-permute-start.10 = (bf16[288,2304]{1,0:T(8,128)(2,1)}, bf16[288,2304]{1,0:T(8,128)(2,1)}, u32[]{:S(2)}, u32[]{:S(2)}) collective-permute-start(bf16[288,2304]{1,0:T(8,128)(2,1)} %refs_0_.3), channel_id=1, source_target_pairs={{0,4},{4,0},{1,5},{5,1},{2,6},{6,2},{3,7},{7,3},{8,12},{12,8},{9,1... | collective-permute-start | bytes 3981320 | tf_op jit(solution)/shard_map/ppermute | solution.py:50
  103.5 108.2 %all-gather.5.cloned.1.call-start = ((), (), s32[]{:S(2)}) async-start(), calls=%async_computation.5 | async-start | bytes 2949120 | tf_op jit(solution)/shard_map/all_gather | solution.py:778
  122.7 46.2 %collective-permute-start.16 = (bf16[288,2304]{1,0:T(8,128)(2,1)}, bf16[288,2304]{1,0:T(8,128)(2,1)}, u32[]{:S(2)}, u32[]{:S(2)}) collective-permute-start(bf16[288,2304]{1,0:T(8,128)(2,1)} %refs_0_.3), channel_id=1, source_target_pairs={{0,8},{8,0},{1,9},{9,1},{2,10},{10,2},{3,11},{11,3},{4,12},{12,4},... | collective-permute-start | bytes 3981320 | tf_op jit(solution)/shard_map/ppermute | solution.py:58
  153.4 142.7 %reduce-scatter.7.cloned.1.call-start = ((), (), s32[]{:S(2)}) async-start(), calls=%async_computation.6 | async-start | bytes 2949120 | tf_op jit(solution)/shard_map/reduce_scatter | solution.py:771
  171.9 34.1 %collective-permute-start.23 = (bf16[288,2304]{1,0:T(8,128)(2,1)}, bf16[288,2304]{1,0:T(8,128)(2,1)S(1)}, u32[]{:S(2)}, u32[]{:S(2)}) collective-permute-start(bf16[288,2304]{1,0:T(8,128)(2,1)} %refs_10_.1), channel_id=1, source_target_pairs={{0,8},{8,0},{1,9},{9,1},{2,10},{10,2},{3,11},{11,3},{4,12},{12,4},... | collective-permute-start | bytes 3981320 | tf_op jit(solution)/shard_map/ppermute | solution.py:58
  171.9 35.6 %collective-permute-start.25 = (bf16[288,2304]{1,0:T(8,128)(2,1)S(1)}, bf16[288,2304]{1,0:T(8,128)(2,1)S(1)}, u32[]{:S(2)}, u32[]{:S(2)}) collective-permute-start(bf16[288,2304]{1,0:T(8,128)(2,1)S(1)} %collective-permute-done.15.refs_12_), channel_id=1, source_target_pairs={{0,8},{8,0},{1,9},{9,1},{2,10},{10,2},{3,11},{11,3},{4,12},{12,4},... | collective-permute-start | bytes 3981320 | tf_op jit(solution)/shard_map/ppermute | solution.py:58
  174.3 34.1 %collective-permute-start.24 = (bf16[288,2304]{1,0:T(8,128)(2,1)S(1)}, bf16[288,2304]{1,0:T(8,128)(2,1)S(1)}, u32[]{:S(2)}, u32[]{:S(2)}) collective-permute-start(bf16[288,2304]{1,0:T(8,128)(2,1)S(1)} %collective-permute-done.14.refs_11_), channel_id=1, source_target_pairs={{0,8},{8,0},{1,9},{9,1},{2,10},{10,2},{3,11},{11,3},{4,12},{12,4},... | collective-permute-start | bytes 3981320 | tf_op jit(solution)/shard_map/ppermute | solution.py:58
  249.4 98.1 %all-gather.7.cloned.1.call-start = ((), (), s32[]{:S(2)}) async-start(), calls=%async_computation.7 | async-start | bytes 2949120 | tf_op jit(solution)/shard_map/all_gather | solution.py:778
  296.1 146.9 %reduce-scatter.9.cloned.1.call-start = ((), (), s32[]{:S(2)}) async-start(), calls=%async_computation.8 | async-start | bytes 2949120 | tf_op jit(solution)/shard_map/reduce_scatter | solution.py:771
  396.0 98.4 %all-gather.9.cloned.1.call-start = ((), (), s32[]{:S(2)}) async-start(), calls=%async_computation.9 | async-start | bytes 2949120 | tf_op jit(solution)/shard_map/all_gather | solution.py:778
  443.0 146.9 %reduce-scatter.11.cloned.1.call-start = ((), (), s32[]{:S(2)}) async-start(), calls=%async_computation.10 | async-start | bytes 2949120 | tf_op jit(solution)/shard_map/reduce_scatter | solution.py:771
  446.6 69.7 %collective-permute-start.49 = (bf16[144,2304]{1,0:T(8,128)(2,1)}, bf16[144,2304]{1,0:T(8,128)(2,1)}, u32[]{:S(2)}, u32[]{:S(2)}) collective-permute-start(bf16[144,2304]{1,0:T(8,128)(2,1)} %get-tuple-element.587), channel_id=1, source_target_pairs={{0,16},{16,0},{1,17},{17,1},{2,18},{18,2},{3,19},{19,3},{4,20},{20... | collective-permute-start | bytes 1990664 | tf_op jit(solution)/shard_map/ppermute | solution.py:54
  461.6 54.6 %collective-permute-start.48 = (bf16[144,2304]{1,0:T(8,128)(2,1)}, bf16[144,2304]{1,0:T(8,128)(2,1)}, u32[]{:S(2)}, u32[]{:S(2)}) collective-permute-start(bf16[144,2304]{1,0:T(8,128)(2,1)} %get-tuple-element.586), channel_id=1, source_target_pairs={{0,4},{4,0},{1,5},{5,1},{2,6},{6,2},{3,7},{7,3},{8,12},{12,8},{9,1... | collective-permute-start | bytes 1990664 | tf_op jit(solution)/shard_map/ppermute | solution.py:50
  467.5 53.2 %collective-permute-start.46 = (bf16[288,2304]{1,0:T(8,128)(2,1)}, bf16[288,2304]{1,0:T(8,128)(2,1)}, u32[]{:S(2)}, u32[]{:S(2)}) collective-permute-start(bf16[288,2304]{1,0:T(8,128)(2,1)} %get-tuple-element.595), channel_id=1, source_target_pairs={{0,4},{4,0},{1,5},{5,1},{2,6},{6,2},{3,7},{7,3},{8,12},{12,8},{9,1... | collective-permute-start | bytes 3981320 | tf_op jit(solution)/shard_map/ppermute | solution.py:50
  468.3 52.3 %collective-permute-start.47 = (bf16[288,2304]{1,0:T(8,128)(2,1)}, bf16[288,2304]{1,0:T(8,128)(2,1)}, u32[]{:S(2)}, u32[]{:S(2)}) collective-permute-start(bf16[288,2304]{1,0:T(8,128)(2,1)} %get-tuple-element.596), channel_id=1, source_target_pairs={{0,16},{16,0},{1,17},{17,1},{2,18},{18,2},{3,19},{19,3},{4,20},{20... | collective-permute-start | bytes 3981320 | tf_op jit(solution)/shard_map/ppermute | solution.py:54
  539.5 103.2 %all-gather.11.cloned.1.call-start = ((), (), s32[]{:S(2)}) async-start(), calls=%async_computation.11 | async-start | bytes 2949120 | tf_op jit(solution)/shard_map/all_gather | solution.py:778
  539.8 32.3 %collective-permute-start.53 = (bf16[288,2304]{1,0:T(8,128)(2,1)}, bf16[288,2304]{1,0:T(8,128)(2,1)S(1)}, u32[]{:S(2)}, u32[]{:S(2)}) collective-permute-start(bf16[288,2304]{1,0:T(8,128)(2,1)} %get-tuple-element.625), channel_id=1, source_target_pairs={{0,16},{16,0},{1,17},{17,1},{2,18},{18,2},{3,19},{19,3},{4,20},{20... | collective-permute-start | bytes 3981320 | tf_op jit(solution)/shard_map/ppermute | solution.py:54
  541.3 32.3 %collective-permute-start.52 = (bf16[288,2304]{1,0:T(8,128)(2,1)}, bf16[288,2304]{1,0:T(8,128)(2,1)S(1)}, u32[]{:S(2)}, u32[]{:S(2)}) collective-permute-start(bf16[288,2304]{1,0:T(8,128)(2,1)} %get-tuple-element.624), channel_id=1, source_target_pairs={{0,4},{4,0},{1,5},{5,1},{2,6},{6,2},{3,7},{7,3},{8,12},{12,8},{9,1... | collective-permute-start | bytes 3981320 | tf_op jit(solution)/shard_map/ppermute | solution.py:50
  552.4 31.9 %collective-permute-start.51 = (bf16[144,2304]{1,0:T(8,128)(2,1)}, bf16[144,2304]{1,0:T(8,128)(2,1)S(1)}, u32[]{:S(2)}, u32[]{:S(2)}) collective-permute-start(bf16[144,2304]{1,0:T(8,128)(2,1)} %get-tuple-element.646), channel_id=1, source_target_pairs={{0,16},{16,0},{1,17},{17,1},{2,18},{18,2},{3,19},{19,3},{4,20},{20... | collective-permute-start | bytes 1990664 | tf_op jit(solution)/shard_map/ppermute | solution.py:54
  552.9 32.7 %collective-permute-start.50 = (bf16[144,2304]{1,0:T(8,128)(2,1)}, bf16[144,2304]{1,0:T(8,128)(2,1)}, u32[]{:S(2)}, u32[]{:S(2)}) collective-permute-start(bf16[144,2304]{1,0:T(8,128)(2,1)} %get-tuple-element.645), channel_id=1, source_target_pairs={{0,4},{4,0},{1,5},{5,1},{2,6},{6,2},{3,7},{7,3},{8,12},{12,8},{9,1... | collective-permute-start | bytes 1990664 | tf_op jit(solution)/shard_map/ppermute | solution.py:50
  590.6 32.1 %collective-permute-start.63 = (bf16[288,2304]{1,0:T(8,128)(2,1)}, bf16[288,2304]{1,0:T(8,128)(2,1)S(1)}, u32[]{:S(2)}, u32[]{:S(2)}) collective-permute-start(bf16[288,2304]{1,0:T(8,128)(2,1)} %get-tuple-element.667), channel_id=1, source_target_pairs={{0,16},{16,0},{1,17},{17,1},{2,18},{18,2},{3,19},{19,3},{4,20},{20... | collective-permute-start | bytes 3981320 | tf_op jit(solution)/shard_map/ppermute | solution.py:54
  591.7 34.9 %collective-permute-start.62 = (bf16[288,2304]{1,0:T(8,128)(2,1)}, bf16[288,2304]{1,0:T(8,128)(2,1)S(1)}, u32[]{:S(2)}, u32[]{:S(2)}) collective-permute-start(bf16[288,2304]{1,0:T(8,128)(2,1)} %get-tuple-element.666), channel_id=1, source_target_pairs={{0,4},{4,0},{1,5},{5,1},{2,6},{6,2},{3,7},{7,3},{8,12},{12,8},{9,1... | collective-permute-start | bytes 3981320 | tf_op jit(solution)/shard_map/ppermute | solution.py:50
  (121 other events, 1635.4 us)
Sparse Core Ops, SparseCore 0:
  103.6 48.3 reduce-scatter.4
  153.6 51.3 all-gather.4
  249.5 46.5 reduce-scatter.6
  297.5 49.9 all-gather.6
  396.1 46.8 reduce-scatter.8
  444.4 49.9 all-gather.8
  539.7 46.9 reduce-scatter.10
  590.1 49.2 all-gather.10
